TPU v7x, 128 devices: a whole 4x4x4 slice. The times are simulated.
128 devices in a mesh: fsdp: 4 (over z), ctx: 32 (over x, y, core).
Axes of the slice: x: 4, y: 4, z: 4, core: 2. Of those that a mesh axis runs over, the one named last changes fastest.
Arguments:
- query_vectors: bfloat16 [4, 4096, 1024], P('fsdp', 'ctx'), may hold values from -6 to 6
- key_vectors: bfloat16 [4, 4096, 1024], P('fsdp', 'ctx'), may hold values from -6 to 6
- value_vectors: bfloat16 [4, 4096, 2048], P('fsdp', 'ctx'), may hold values from -24 to 24
- output_gate: bfloat16 [4, 4096, 2048], P('fsdp', 'ctx'), may hold values from -6 to 6
- log_decay: float32 [4, 4096, 16], P('fsdp', 'ctx'), may hold values from -1 to 0
- write_rate: float32 [4, 4096, 16], P('fsdp', 'ctx'), may hold values from 0 to 1
- out_weight: bfloat16 [2048, 2048], P('fsdp'), may hold values from -0.125 to 0.125
- cotangent: bfloat16 [4, 4096, 2048], P('fsdp', 'ctx'), may hold values from -6 to 6
- lengths: int32 [4], replicated, may hold values from 2048 to 4096, as said below
- pairing: int32 [4], replicated, may hold values from 0 to 3, each once
- log_ratio: float32 [4], replicated, may hold values from -1 to 1
Outputs:
- mixed_out: bfloat16 [4, 4096, 2048], P('fsdp', 'ctx')
- query_grad: bfloat16 [4, 4096, 1024], P('fsdp', 'ctx')
- key_grad: bfloat16 [4, 4096, 1024], P('fsdp', 'ctx')
- value_grad: bfloat16 [4, 4096, 2048], P('fsdp', 'ctx')
- gate_grad: bfloat16 [4, 4096, 2048], P('fsdp', 'ctx')
- weight_grad: float32 [2048, 2048], P(('fsdp', 'ctx'))
Inputs may be any that keep to these rules, and one draw needn't show every extreme that they name: `lengths`: some sequence has exactly 4096 live tokens.
All inputs are finite; a program needn't handle non-finite values.
Results may differ from a plain program's by a relative error of at most 0.019.
Values may be sent and summed in bfloat16 or wider, within the bound.
No kernel may reach another device: no remote copies, remote signals or barrier semaphores. Data moves between devices by JAX's collectives and lax.ppermute only.
A program may use at most 448 MiB of HBM per device.

v0:
```python
from functools import partial

import jax
import jax.numpy as jnp
from jax import lax
from jax.sharding import PartitionSpec as P

VALUE_HEADS = 16
HK = 8
DK = 128
DV = 128
BLOCK = 64


PRECISE = lax.Precision.HIGHEST
BLOCKWISE = lax.Precision.HIGH
CHI_BETA = 0.5
NORM_EPS = 1e-06


def prefix_2(value, axis, join, neutral):
    count, mine = (lax.axis_size(axis), lax.axis_index(axis))
    pieces = jax.tree.map(lambda part: lax.all_gather(part, axis), value)
    so_far = jax.tree.map(
        lambda part, zero: jnp.full_like(part, 0) + jnp.asarray(zero, part.dtype), value, neutral
    )

    def step(position, so_far):
        longer = join(so_far, jax.tree.map(lambda part: part[position], pieces))
        return jax.tree.map(lambda new, old: jnp.where(position < mine, new, old), longer, so_far)

    return lax.fori_loop(0, count - 1, step, so_far)


def carried_in(x, axis, join, neutral):
    count = lax.axis_size(axis)
    place = lax.axis_index(axis)
    ahead = count - 1 - place
    gathered = jax.tree.map(
        lambda a, kind: lax.all_gather(a.astype(kind), axis),
        x,
        jax.tree.map(lambda a: jnp.bfloat16 if a.dtype == jnp.float32 else a.dtype, x),
    )
    state = jax.tree.map(lambda a, e: jnp.zeros_like(a) + jnp.asarray(e, a.dtype), x, neutral)

    def one(step, state):
        source = count - 1 - step
        return join(
            state,
            jax.tree.map(
                lambda a, own: lax.dynamic_index_in_dim(a, source, 0, False).astype(own.dtype),
                gathered,
                x,
            ),
        )

    return lax.fori_loop(0, ahead, one, state)


def unit_rows(matrix):
    return matrix * lax.rsqrt(jnp.sum(matrix * matrix, axis=-1, keepdims=True) + NORM_EPS)


def head_major(matrix, head_count):
    return jnp.swapaxes(matrix.reshape(matrix.shape[0], head_count, -1), 0, 1)


def prepare(query_vectors, key_vectors, value_vectors):
    group_size = VALUE_HEADS // HK
    queries = unit_rows(head_major(query_vectors, HK)) * DK ** (-0.5)
    unit_keys = unit_rows(head_major(key_vectors, HK))
    return (
        jnp.repeat(queries, group_size, axis=0),
        jnp.repeat(unit_keys, group_size, axis=0),
        head_major(value_vectors, VALUE_HEADS),
    )


def block_parts(queries, unit_keys, values, decays, write_rates):
    block_len = queries.shape[-2]
    cumulative = jnp.cumsum(decays, axis=-1)
    row_index = lax.broadcasted_iota(jnp.int32, (block_len, block_len), 0)
    col_index = lax.broadcasted_iota(jnp.int32, (block_len, block_len), 1)
    causal = row_index >= col_index
    strict = row_index > col_index
    spread = cumulative[..., :, None] - cumulative[..., None, :]
    within = jnp.where(causal, jnp.exp(jnp.where(causal, spread, 0.0)), 0.0)
    intersection = jnp.einsum("bhtd,bhjd->bhtj", unit_keys, unit_keys, precision=BLOCKWISE)
    coupling = jnp.where(strict, intersection * within, 0.0) * write_rates[..., :, None]
    identity_c = jnp.eye(block_len, dtype=decays.dtype)
    negated = -coupling
    inverse = identity_c + negated
    powered = negated
    for repeat in range(block_len.bit_length() - 2):
        powered = jnp.einsum("bhij,bhjk->bhik", powered, powered, precision=PRECISE)
        inverse = jnp.einsum("bhij,bhjk->bhik", inverse, identity_c + powered, precision=PRECISE)
    growth = jnp.exp(cumulative)
    new_values = jnp.einsum(
        "bhtj,bhjv->bhtv", inverse, write_rates[..., None] * values, precision=BLOCKWISE
    )
    new_keys = jnp.einsum(
        "bhtj,bhjk->bhtk",
        inverse,
        (write_rates * growth)[..., None] * unit_keys,
        precision=BLOCKWISE,
    )
    scores = jnp.einsum("bhtd,bhjd->bhtj", queries, unit_keys, precision=BLOCKWISE) * within
    inner_out = jnp.einsum("bhtj,bhjv->bhtv", scores, new_values, precision=BLOCKWISE)
    reach_rows = growth[..., None] * queries - jnp.einsum(
        "bhtj,bhjk->bhtk", scores, new_keys, precision=BLOCKWISE
    )
    block_total = cumulative[..., -1:]
    carried = jnp.exp(block_total - cumulative)[..., None] * unit_keys
    identity_k = jnp.eye(unit_keys.shape[-1], dtype=decays.dtype)
    transit = jnp.exp(block_total)[..., None] * identity_k - jnp.einsum(
        "bhcx,bhcy->bhxy", new_keys, carried, precision=BLOCKWISE
    )
    written = jnp.einsum("bhcv,bhck->bhvk", new_values, carried, precision=BLOCKWISE)
    return (inner_out, reach_rows, transit, written)


def norm_gate(outputs, gates):
    shaped = outputs.reshape(outputs.shape[:-1] + (VALUE_HEADS, DV))
    scaled = shaped * lax.rsqrt(jnp.mean(shaped * shaped, axis=-1, keepdims=True) + NORM_EPS)
    return scaled.reshape(outputs.shape) * jax.nn.silu(gates)


def pair_weights(log_ratio, pairing):
    seq_count = log_ratio.shape[0]
    couples = pairing.reshape(seq_count // 2, 2)
    seq_index = lax.broadcasted_iota(jnp.int32, (seq_count // 2, seq_count), 1)
    chosen = (couples[:, :1] == seq_index).astype(log_ratio.dtype)
    rejected = (couples[:, 1:] == seq_index).astype(log_ratio.dtype)
    ratio_c = jnp.sum(chosen * log_ratio[None, :], axis=1)
    ratio_r = jnp.sum(rejected * log_ratio[None, :], axis=1)
    margin = CHI_BETA * (jnp.exp(ratio_c) + ratio_c - jnp.exp(ratio_r) - ratio_r)
    pull_scale = CHI_BETA * jax.nn.sigmoid(-margin)
    weight_c = -pull_scale * (jnp.exp(ratio_c) + 1.0)
    weight_r = pull_scale * (jnp.exp(ratio_r) + 1.0)
    return jnp.sum(chosen * weight_c[:, None] + rejected * weight_r[:, None], axis=0)


def device_core(decays, write_rates, query_vectors, key_vectors, value_vectors):
    queries, unit_keys, values = prepare(query_vectors, key_vectors, value_vectors)
    block_count = values.shape[1] // BLOCK

    def to_blocks(tensor):
        shaped = tensor.reshape((tensor.shape[0], block_count, BLOCK) + tensor.shape[2:])
        return jnp.swapaxes(shaped, 0, 1)

    inner_out, reach_rows, transit, written = block_parts(
        to_blocks(queries),
        to_blocks(unit_keys),
        to_blocks(values),
        to_blocks(decays.T),
        to_blocks(write_rates.T),
    )
    head_count = values.shape[0]
    identity_k = jnp.eye(unit_keys.shape[-1], dtype=jnp.float32)
    initial = (
        jnp.broadcast_to(identity_k, (head_count,) + identity_k.shape),
        jnp.zeros((head_count, values.shape[-1], unit_keys.shape[-1]), jnp.float32),
    )

    def advance(prefixes, pieces):
        prefix_a, prefix_b = prefixes
        block_transit, block_written, block_reach = pieces
        device_reach = jnp.einsum("hck,hxk->hcx", block_reach, prefix_a, precision=BLOCKWISE)
        offset = jnp.einsum("hck,hvk->hcv", block_reach, prefix_b, precision=BLOCKWISE)
        next_a = jnp.einsum("hxk,hky->hxy", prefix_a, block_transit, precision=PRECISE)
        next_b = (
            jnp.einsum("hvk,hky->hvy", prefix_b, block_transit, precision=PRECISE) + block_written
        )
        return ((next_a, next_b), (device_reach, offset))

    totals, per_block = lax.scan(advance, initial, (transit, written, reach_rows))
    return (inner_out + per_block[1], per_block[0], totals[0], totals[1])


def carry_forward(earlier, later):
    return (
        jnp.einsum("hxk,hky->hxy", earlier[0], later[0], precision=PRECISE),
        jnp.einsum("hvk,hky->hvy", earlier[1], later[0], precision=PRECISE) + later[1],
    )


def carry_backward(earlier, later):
    return (
        jnp.einsum("hxk,hky->hxy", later[0], earlier[0], precision=PRECISE),
        later[1] + jnp.einsum("hvx,hyx->hvy", earlier[1], later[0], precision=PRECISE),
    )


def body(
    query_vectors,
    key_vectors,
    value_vectors,
    output_gate,
    log_decay,
    write_rate,
    out_weight,
    cotangent,
    lengths,
    pairing,
    log_ratio,
):
    tokens = query_vectors.shape[1]
    block_count = tokens // BLOCK
    floats = (
        query_vectors[0].astype(jnp.float32),
        key_vectors[0].astype(jnp.float32),
        value_vectors[0].astype(jnp.float32),
    )
    core_parts, core_pullback = jax.vjp(partial(device_core, log_decay[0], write_rate[0]), *floats)
    local_out, device_reach, total_a, total_b = core_parts
    identity_k = jnp.broadcast_to(jnp.eye(total_a.shape[-1], dtype=jnp.float32), total_a.shape)
    prefix = prefix_2(
        (total_a, total_b), "ctx", carry_forward, (identity_k, jnp.zeros_like(total_b))
    )
    entering = prefix[1]
    blocked_out = local_out + jnp.einsum(
        "nhck,hvk->nhcv", device_reach, entering, precision=BLOCKWISE
    )
    flat_out = jnp.swapaxes(blocked_out, 1, 2).reshape(tokens, -1)
    gated_out, norm_pullback = jax.vjp(norm_gate, flat_out, output_gate[0].astype(jnp.float32))
    normed = gated_out.astype(jnp.bfloat16)
    full_weight = lax.all_gather(out_weight, "fsdp", axis=0, tiled=True)
    mixed_out = jnp.dot(normed, full_weight, preferred_element_type=jnp.float32).astype(
        jnp.bfloat16
    )
    weights = pair_weights(log_ratio, pairing)
    own_seq = lax.axis_index("fsdp")
    seq_ids = lax.broadcasted_iota(jnp.int32, weights.shape, 0)
    own_weight = jnp.sum(jnp.where(seq_ids == own_seq, weights, 0.0))
    own_length = jnp.sum(jnp.where(seq_ids == own_seq, lengths, 0))
    token_positions = lax.axis_index("ctx") * tokens + lax.broadcasted_iota(
        jnp.int32, (tokens, 1), 0
    )
    live_mask = (token_positions < own_length).astype(jnp.float32)
    scaled = (cotangent[0].astype(jnp.float32) * (own_weight * live_mask)).astype(jnp.bfloat16)
    back_grad = lax.dot_general(
        scaled, full_weight, (((1,), (1,)), ((), ())), preferred_element_type=jnp.float32
    ).astype(jnp.bfloat16)
    back_grad = lax.optimization_barrier(back_grad).astype(jnp.float32)
    out_grad, gate_grad = norm_pullback(back_grad)
    blocked_grad = jnp.swapaxes(out_grad.reshape(block_count, BLOCK, VALUE_HEADS, -1), 1, 2)
    reach_grad = jnp.einsum("nhcv,hvk->nhck", blocked_grad, entering, precision=BLOCKWISE)
    state_grad = jnp.einsum("nhcv,nhck->hvk", blocked_grad, device_reach, precision=BLOCKWISE)
    suffix = carried_in(
        (total_a, state_grad), "ctx", carry_backward, (identity_k, jnp.zeros_like(state_grad))
    )
    leaving = suffix[1]
    transit_grad = jnp.einsum("hvx,hvy->hxy", entering, leaving, precision=PRECISE)
    input_grads = core_pullback((blocked_grad, reach_grad, transit_grad, leaving))
    feature_rows = lax.all_to_all(normed, "fsdp", split_axis=1, concat_axis=0, tiled=True)
    every_scaled = lax.all_gather(scaled, "fsdp", axis=0, tiled=True)
    weight_grad = lax.psum_scatter(
        lax.dot_general(
            feature_rows, every_scaled, (((0,), (0,)), ((), ())), preferred_element_type=jnp.float32
        ).astype(jnp.bfloat16),
        "ctx",
        scatter_dimension=0,
        tiled=True,
    ).astype(jnp.float32)
    return (
        mixed_out[None],
        input_grads[0].astype(jnp.bfloat16)[None],
        input_grads[1].astype(jnp.bfloat16)[None],
        input_grads[2].astype(jnp.bfloat16)[None],
        gate_grad.astype(jnp.bfloat16)[None],
        weight_grad,
    )


def solution(mesh):
    return jax.shard_map(
        body,
        mesh=mesh,
        in_specs=(
            P("fsdp", "ctx", None),
            P("fsdp", "ctx", None),
            P("fsdp", "ctx", None),
            P("fsdp", "ctx", None),
            P("fsdp", "ctx", None),
            P("fsdp", "ctx", None),
            P("fsdp", None),
            P("fsdp", "ctx", None),
            P(),
            P(),
            P(),
        ),
        out_specs=(
            P("fsdp", "ctx", None),
            P("fsdp", "ctx", None),
            P("fsdp", "ctx", None),
            P("fsdp", "ctx", None),
            P("fsdp", "ctx", None),
            P(("fsdp", "ctx"), None),
        ),
        check_vma=False,
    )
```

profile of v0, /device:TPU:0, one launch (start us, length us, event | category | flops | bytes accessed | tf_op | source)
XLA Modules:
  0.0 1176.4 jit_solution(8200393298307586715)
XLA Ops:
  30.6 3.1 fusion.160
  43.2 27.6 %while.73 = (s32[]{:T(128)}, f32[16,128,128]{1,2,0:T(8,128)}, f32[16,128,128]{1,2,0:T(8,128)}, f32[2,16,64,128]{3,2,1,0:T(8,128)}, f32[2,16,64,128]{3,2,1,0:T(8,...) while((s32[]{:T(128)}, f32[16,128,128]{1,2,0:T(8,128)}, ...), condition=%wide.region_4.5_spmd.clone, body=%wide.region_3.4_spmd.clone.sunk | while | flops 1007681536 | bytes 70258000 | solution.py:176
  49.9 2.9 fusion.377
  54.2 2.9 convolution_bitcast_fusion.21
  63.7 2.9 fusion.377
  68.0 2.9 convolution_bitcast_fusion.21
  70.8 2.9 copy.370
  73.8 2.6 copy.371
  81.7 3.1 convolution_add_fusion.18
  84.8 2.9 reshape.240
  87.7 7.9 all-gather.11.cloned.1.call-done
  95.6 6.5 convolution_convert_fusion.1
  103.5 108.8 %all-gather.15.cloned.1.call-done = f32[512,128,128]{2,1,0:T(8,128)} async-done(((f32[16,128,128]{2,1,0:T(8,128)}), f32[512,128,128]{2,1,0:T(8,128)}) %all-gather.15.cloned.1.call-update) | async-done | bytes 33554448 | tf_op jit(solution)/shard_map/all_gather | solution.py:23
  212.3 115.3 %all-gather.17.cloned.1.call-done = f32[512,128,128]{2,1,0:T(8,128)} async-done(((f32[16,128,128]{2,1,0:T(8,128)}), f32[512,128,128]{2,1,0:T(8,128)}) %all-gather.17.cloned.1.call-update) | async-done | bytes 33554448 | tf_op jit(solution)/shard_map/all_gather | solution.py:23
  327.7 256.1 %while.74 = (s32[]{:T(128)}, f32[16,128,128]{1,2,0:T(8,128)}, s32[]{:T(128)}, f32[32,16,128,128]{3,2,1,0:T(8,128)}, f32[32,16,128,128]{3,2,1,0:T(8,128)}, /*index=5*/s32[]{:T(128)}, s32[]{:T(128)}) while((s32[]{:T(128)}, f32[16,128,128]{1,2,0:T(8,128)}, s32[]{:T(128)}, f32[32,16,128,128]{3,2,1,0:T(8,128)}, ...), condition=%wide.region_6.7_spmd.clone, body=%wide.region_5.6_spmd.clone.sunk | while | flops 403701760 | bytes 15730815 | solution.py:32
  332.2 4.1 fusion.382
  340.6 4.1 fusion.382
  348.9 4.1 fusion.382
  357.1 4.1 fusion.382
  365.4 4.1 fusion.382
  373.6 4.1 fusion.382
  381.8 4.1 fusion.382
  390.1 4.1 fusion.382
  398.3 4.1 fusion.382
  406.6 4.1 fusion.382
  414.8 4.1 fusion.382
  423.1 4.1 fusion.382
  431.3 4.1 fusion.382
  439.6 4.1 fusion.382
  447.8 4.1 fusion.382
  456.0 4.1 fusion.382
  464.3 4.1 fusion.382
  472.5 4.1 fusion.382
  480.8 4.1 fusion.382
  489.0 4.1 fusion.382
  497.3 4.1 fusion.382
  505.5 4.1 fusion.382
  513.7 4.1 fusion.382
  522.0 4.1 fusion.382
  530.2 4.1 fusion.382
  538.5 4.1 fusion.382
  546.7 4.1 fusion.382
  555.0 4.1 fusion.382
  563.2 4.1 fusion.382
  571.4 4.1 fusion.382
  579.7 4.1 fusion.382
  583.8 3.3 multiply_reduce_fusion
  598.5 4.4 all-to-all-start
  602.9 10.0 all-to-all-done
  612.9 4.2 convolution_convert_fusion
  621.4 3.4 fusion.108
  624.9 3.6 convolution_bitcast_fusion.13
  630.4 6.3 fusion.74
  636.6 56.7 %reduce-scatter.2.cloned.1.call-done = bf16[16,2048]{1,0:T(8,128)(2,1)} async-done(((bf16[512,2048]{1,0:T(8,128)(2,1)}), bf16[16,2048]{1,0:T(8,128)(2,1)}) %reduce-scatter.2.cloned.1.call-update) | async-done | bytes 65552 | tf_op jit(solution)/shard_map/reduce_scatter | solution.py:257
  694.8 72.4 %all-gather.21.cloned.1.call-done = bf16[512,128,128]{2,1,0:T(8,128)(2,1)} async-done(((bf16[16,128,128]{2,1,0:T(8,128)(2,1)}), bf16[512,128,128]{2,1,0:T(8,128)(2,1)}) %all-gather.21.cloned.1.call-update) | async-done | bytes 16777232 | tf_op jit(solution)/shard_map/all_gather | solution.py:40
  767.2 74.8 %all-gather.19.cloned.1.call-done = bf16[512,128,128]{2,1,0:T(8,128)(2,1)} async-done(((bf16[16,128,128]{2,1,0:T(8,128)(2,1)}), bf16[512,128,128]{2,1,0:T(8,128)(2,1)}) %all-gather.19.cloned.1.call-update) | async-done | bytes 16777232 | tf_op jit(solution)/shard_map/all_gather | solution.py:40
  842.1 208.6 %while.71 = (s32[]{:T(128)}, f32[16,128,128]{1,2,0:T(8,128)S(1)}, s32[]{:T(128)}, bf16[32,16,128,128]{3,2,1,0:T(8,128)(2,1)}, bf16[32,16,128,128]{3,2,1,0:T(8,12...) while((s32[]{:T(128)}, f32[16,128,128]{1,2,0:T(8,128)S(1)}, s32[]{:T(128)}, ...), condition=%wide.region_15.16_spmd, body=%wide.region_14.15_spmd.sunk | while | flops 403177472 | bytes 9437359 | solution.py:57
  1050.7 4.5 fusion.206
  1059.5 31.4 %while.72 = (s32[]{:T(128)}, f32[16,128,128]{1,2,0:T(8,128)}, f32[16,128,128]{1,2,0:T(8,128)S(1)}, f32[2,16,128,128]{3,2,1,0:T(8,128)}, f32[2,16,128,128]{2,3,1,...) while((s32[]{:T(128)}, f32[16,128,128]{1,2,0:T(8,128)}, ...), condition=%wide.region_17.18_spmd, body=%wide.region_16.17_spmd.sunk | while | flops 2014183424 | bytes 102242296 | solution.py:176
  1090.9 3.0 fusion.157
  1102.0 3.0 fusion.209
  1105.0 2.8 fusion.208
  1107.8 3.2 fusion.207
  1119.3 3.2 fusion.210
  (775 shorter events, 508.0 us)
Async XLA Ops:
  7.2 88.4 %all-gather.11.cloned.1.call-start = ((), (), s32[]{:S(2)}) async-start(), calls=%async_computation.2 | async-start | bytes 10485760 | tf_op jit(solution)/shard_map/all_gather | solution.py:227
  8.0 204.4 %all-gather.15.cloned.1.call-start = ((), (), s32[]{:S(2)}) async-start(), calls=%async_computation.5 | async-start | bytes 34603008 | tf_op jit(solution)/shard_map/all_gather | solution.py:23
  8.3 3.7 copy-start.56
  8.8 20.7 %copy-start.89 = (f32[2,16,64]{2,1,0:T(8,128)}, f32[2,16,64]{2,1,0:T(8,128)S(1)}, u32[]{:S(2)}) copy-start(f32[2,16,64]{2,1,0:T(8,128)S(1)} %reduce_window_sum.13) | copy-start | bytes 24580
  9.1 24.7 %copy-start.94 = (f32[2,16,64]{2,1,0:T(8,128)}, f32[2,16,64]{2,1,0:T(8,128)S(1)}, u32[]{:S(2)}) copy-start(f32[2,16,64]{2,1,0:T(8,128)S(1)} %get-tuple-element.788) | copy-start | bytes 24580
  9.3 3.0 copy-start.54
  10.8 17.5 %copy-start.77 = (f32[16,128,128]{2,1,0:T(8,128)}, f32[16,128,128]{2,1,0:T(8,128)S(1)}, u32[]{:S(2)}) copy-start(f32[16,128,128]{2,1,0:T(8,128)S(1)} %copy.360) | copy-start | bytes 3145732
  11.0 18.6 %copy-start.98 = (pred[64,64]{1,0:T(8,128)(4,1)}, pred[64,64]{1,0:T(8,128)(4,1)S(1)}, u32[]{:S(2)}) copy-start(pred[64,64]{1,0:T(8,128)(4,1)S(1)} %get-tuple-element.797) | copy-start | bytes 12292
  12.6 17.0 %copy-start.22 = (f32[8,2,128,128]{3,2,1,0:T(8,128)}, f32[8,2,128,128]{3,2,1,0:T(8,128)S(1)}, u32[]{:S(2)}) copy-start(f32[8,2,128,128]{3,2,1,0:T(8,128)S(1)} %broadcast_in_dim.122) | copy-start | bytes 3145732
  13.7 4.8 copy-start.24
  14.9 3.6 copy-start.14
  16.1 3.7 copy-start.16
  17.2 3.7 copy-start.18
  18.5 5.1 copy-start.20
  23.6 3.4 copy-start.58
  27.6 6.8 copy-start.32
  28.3 6.2 copy-start.27
  29.5 4.2 copy-start.52
  30.6 3.2 copy-start.34
  43.4 2.8 copy-start.7
  43.4 2.8 copy-start.10
  46.5 6.3 copy-start.8
  46.5 6.3 copy-start.11
  46.5 3.4 copy-start.40
  48.2 4.6 copy-start.88
  57.1 2.9 copy-start.7
  57.1 2.9 copy-start.10
  60.3 6.3 copy-start.8
  60.3 6.3 copy-start.11
  60.3 3.4 copy-start.40
  61.9 4.6 copy-start.88
  70.8 5.6 copy-start.1
  73.8 3.0 copy-start.111
  73.8 4.0 copy-start.113
  73.8 253.9 %all-gather.17.cloned.1.call-start = ((), (), s32[]{:S(2)}) async-start(), calls=%async_computation.6 | async-start | bytes 34603008 | tf_op jit(solution)/shard_map/all_gather | solution.py:23
  76.4 5.3 copy-start.35
  76.5 526.5 %all-gather.13.cloned.1.call-start = ((), (), s32[]{:S(2)}) async-start(), calls=%async_computation.3 | async-start | bytes 2621440 | tf_op jit(solution)/shard_map/all_gather | solution.py:256
  87.7 14.3 %copy-start.80 = (bf16[1,128,2048]{2,1,0:T(8,128)(2,1)S(1)}, bf16[1,128,2048]{2,1,0:T(8,128)(2,1)}, u32[]{:S(2)}) copy-start(bf16[1,128,2048]{2,1,0:T(8,128)(2,1)} %param.22) | copy-start | bytes 1572868
  587.1 5.6 copy-start.64
  598.5 14.4 %all-to-all-start = ((bf16[128,4,512]{2,0,1:T(8,128)(2,1)}), bf16[128,4,512]{2,0,1:T(8,128)(2,1)S(1)}, u32[]{:S(2)}, u32[]{:S(2)}) async-start(bf16[128,4,512]{2,0,1:T(8,128)(2,1)} %copy.425), calls=%async_computation | async-start | bytes 1048576 | tf_op jit(solution)/shard_map/all_to_all | solution.py:255
  602.9 90.4 %reduce-scatter.2.cloned.1.call-start = ((), (), s32[]{:S(2)}) async-start(), calls=%async_computation.4 | async-start | bytes 2162688 | tf_op jit(solution)/shard_map/reduce_scatter | solution.py:257
  617.1 150.1 %all-gather.21.cloned.1.call-start = ((), (), s32[]{:S(2)}) async-start(), calls=%async_computation.8 | async-start | bytes 17301504 | tf_op jit(solution)/shard_map/all_gather | solution.py:40
  619.2 222.7 %all-gather.19.cloned.1.call-start = ((), (), s32[]{:S(2)}) async-start(), calls=%async_computation.7 | async-start | bytes 17301504 | tf_op jit(solution)/shard_map/all_gather | solution.py:40
  621.4 7.1 copy-start.3
  624.8 3.7 copy-start.73
  624.8 3.6 copy-start.74
  624.8 3.6 copy-start.81
  624.8 3.6 copy-start.83
  1061.2 3.8 copy-start.2
  1061.2 3.8 copy-start.4
  1066.1 3.4 copy-start
  1066.1 3.3 copy-start.44
  1076.6 3.8 copy-start.2
  1076.7 3.8 copy-start.4
  1081.5 3.4 copy-start
  1081.5 3.3 copy-start.44
  1090.8 3.0 copy-start.5
  1090.9 3.0 copy-start.36
  1102.0 3.0 copy-start.59
  1105.0 2.8 copy-start.38
  1105.0 2.8 copy-start.43
  1107.8 3.2 copy-start.28
  1114.3 4.9 copy-start.21
  1119.3 3.2 copy-start.76
  (137 other events, 206.8 us)
Sparse Core Ops, SparseCore 0:
  9.7 85.8 all-gather.10
  97.8 114.4 all-gather.14
  214.6 113.0 all-gather.16
  329.8 30.4 all-gather.12
  617.2 76.0 reduce-scatter.1
  695.4 71.7 all-gather.20
  770.0 71.8 all-gather.18
where the time goes:
time: 1200 us; the launch traced here: 1180 us
  waiting for transfers between devices  447 us (37%)
  local copies, waits for them, and re-layouts  346 us (29%)
  matrix products  341 us (28%)
  other arithmetic  18.8 us (2%)
  between operations  15.9 us (1%)
    all_gather x2, waiting for transfers between devices, prefix_2(): pieces = jax.tree.map(lambda part: lax.all_gather(part, axis), value)  224 us
    all_gather x2, waiting for transfers between devices, carried_in(): lax.all_gather(a.astype(kind), axis)  147 us
    dot_general x31, matrix products, carry_forward(): jnp.einsum('hvk,hky->hvy', earlier[1], later[0], precision=PRECISE)  126 us
    dynamic_slice x62, local copies, waits for them, and re-layouts, one(): lax.dynamic_index_in_dim(a, source, 0, False).astype(own.dtype)  122 us
    while x266, local copies, waits for them, and re-layouts  97 us
    dynamic_slice x62, local copies, waits for them, and re-layouts, step(): longer = join(so_far, jax.tree.map(lambda part: part[position], pieces))  81.6 us
    reduce_scatter x1, waiting for transfers between devices, body(): lax.psum_scatter(lax.dot_general(feature_rows, every_scaled, (((0,), (0,)...  56.7 us
    dot_general x31, matrix products, carry_backward(): jnp.einsum('hvx,hyx->hvy', earlier[1], later[0], precision=PRECISE)  53.4 us
  transfers between devices with their start and end apart: 8, of which 7 were waited for; matrix products, arithmetic and copies ran while one was open for 31% of the time, Pallas kernels for 0%

commit v1 on v0

v1 whole, which is shorter than its diff:
```python
import functools

import jax
import jax.numpy as jnp
from jax import lax
from jax.experimental import pallas as pl
from jax.experimental.pallas import tpu as pltpu
from jax.sharding import PartitionSpec as P

VALUE_HEADS = 16
HK = 8
DK = 128
DV = 128
T = 128
HALF = 64
TAIL = 16
CHI_BETA = 0.5
NORM_EPS = 1e-06
F32 = jnp.float32
BF16 = jnp.bfloat16

NN = (((1,), (0,)), ((), ()))
NT = (((1,), (1,)), ((), ()))
TN = (((0,), (0,)), ((), ()))


def dot1(a, b, dims=NN):
    return lax.dot_general(a.astype(BF16), b.astype(BF16), dims, preferred_element_type=F32)


def split(a):
    high = a.astype(BF16)
    return high, (a - high.astype(F32)).astype(BF16)


def dot3(a, b, dims=NN):
    a_high, a_low = split(a)
    b_high, b_low = split(b)
    return dot1(a_high, b_high, dims) + (dot1(a_low, b_high, dims) + dot1(a_high, b_low, dims))


def grid_index():
    row = lax.broadcasted_iota(jnp.int32, (T, T), 0)
    col = lax.broadcasted_iota(jnp.int32, (T, T), 1)
    return row, col


def unit(x):
    return lax.rsqrt(jnp.sum(x * x, axis=-1, keepdims=True) + NORM_EPS)


def cumulative_decay(decay, row, col):
    lower = (row >= col).astype(BF16)
    first, rest = decay.astype(BF16), decay
    rest = rest - first.astype(F32)
    second = rest.astype(BF16)
    third = (rest - second.astype(F32)).astype(BF16)
    return dot1(lower, first) + (dot1(lower, second) + dot1(lower, third))


def column(table, head):
    lane = lax.broadcasted_iota(jnp.int32, table.shape, 1)
    return jnp.sum(jnp.where(lane == head, table, 0.0), axis=1, keepdims=True)


def as_row(table_t, head):
    sub = lax.broadcasted_iota(jnp.int32, table_t.shape, 0)
    return jnp.sum(jnp.where(sub == head, table_t, 0.0), axis=0, keepdims=True)


def decay_within(cum_col, cum_row, causal):
    return jnp.where(causal, jnp.exp(jnp.where(causal, cum_col - cum_row, 0.0)), 0.0)


def invert(coupling, row, col):
    eye = (row == col).astype(F32)
    inverse = eye - jnp.where((row >> 1) == (col >> 1), coupling, 0.0)
    for level in range(1, 7):
        mask = ((row >> (level + 1)) == (col >> (level + 1))) & ((row >> level) != (col >> level))
        off = jnp.where(mask, coupling, 0.0)
        inverse = inverse - dot1(inverse, dot1(off, inverse))
    residual = eye - inverse - dot3(coupling, inverse)
    return inverse + dot1(inverse, residual)


def forward_kernel(heads, q_ref, k_ref, v_ref, ld_ref, be_ref,
                   ab_ref, t_ref, p_ref, u0_ref, kg_ref, r_ref, io_ref):
    group = pl.program_id(0)
    row, col = grid_index()
    causal, strict = row >= col, row > col
    cum = cumulative_decay(ld_ref[...], row, col)
    cum_t = cum.T
    beta = be_ref[...]
    for key_head in range(heads):
        lanes = slice(key_head * DK, (key_head + 1) * DK)
        q = q_ref[:, lanes].astype(F32)
        k = k_ref[:, lanes].astype(F32)
        qn = q * unit(q) * DK ** (-0.5)
        kn = k * unit(k)
        kk = dot3(kn, kn, NT)
        qk = dot3(qn, kn, NT)
        for sub in range(2):
            local = 2 * key_head + sub
            head = 2 * heads * group + local
            cum_col = column(cum, head)
            cum_row = as_row(cum_t, head)
            rate = column(beta, head)
            within = decay_within(cum_col, cum_row, causal)
            coupling = jnp.where(strict, kk * within, 0.0) * rate
            inverse = invert(coupling, row, col)
            growth = jnp.exp(cum_col)
            total = cum_col[T - 1:, :]
            v = v_ref[:, local * DV:(local + 1) * DV].astype(F32)
            u0 = dot1(inverse, rate * v)
            kg = dot1(inverse, (rate * growth) * kn)
            scores = qk * within
            io_ref[local] = dot1(scores, u0)
            r_ref[local] = (growth * qn - dot1(scores, kg)).astype(BF16)
            carried = jnp.exp(total - cum_col) * kn
            transit = dot1(kg, carried, TN).astype(BF16)
            written = dot1(u0, carried, TN).astype(BF16)
            t_ref[local] = inverse.astype(BF16)
            p_ref[local] = scores.astype(BF16)
            u0_ref[local] = u0
            kg_ref[local] = kg.astype(BF16)
            wide = jnp.broadcast_to(total, (TAIL, DK))
            high, low = split(wide)
            low2 = (wide - high.astype(F32) - low.astype(F32)).astype(BF16)
            sub_row = lax.broadcasted_iota(jnp.int32, (TAIL, DK), 0)
            tail = jnp.where(sub_row == 0, high.astype(F32),
                             jnp.where(sub_row == 1, low.astype(F32),
                                       jnp.where(sub_row == 2, low2.astype(F32), 0.0)))
            for half in range(2):
                slot = 2 * local + half
                ab_ref[slot, 0:DK, :] = transit
                ab_ref[slot, DK:DK + HALF, :] = written[half * HALF:(half + 1) * HALF]
                ab_ref[slot, DK + HALF:, :] = tail.astype(BF16)


def forward_local(q, k, v, ld, be, heads=2):
    steps = HK // heads
    nv = 2 * heads
    per_head = lambda dtype: jax.ShapeDtypeStruct((VALUE_HEADS, T, DK), dtype)
    head_block = pl.BlockSpec((nv, T, DK), lambda i: (i, 0, 0))
    whole = pl.BlockSpec((T, VALUE_HEADS), lambda i: (0, 0))
    rows = DK + HALF + TAIL
    return pl.pallas_call(
        functools.partial(forward_kernel, heads),
        grid=(steps,),
        in_specs=[
            pl.BlockSpec((T, heads * DK), lambda i: (0, i)),
            pl.BlockSpec((T, heads * DK), lambda i: (0, i)),
            pl.BlockSpec((T, nv * DV), lambda i: (0, i)),
            whole,
            whole,
        ],
        out_specs=[pl.BlockSpec((2 * nv, rows, DK), lambda i: (i, 0, 0))] + [head_block] * 6,
        out_shape=[
            jax.ShapeDtypeStruct((2 * VALUE_HEADS, rows, DK), BF16),
            per_head(BF16), per_head(BF16), per_head(F32), per_head(BF16), per_head(BF16),
            per_head(F32),
        ],
        compiler_params=pltpu.CompilerParams(vmem_limit_bytes=48 << 20),
        name="forward_local",
    )(q, k, v, ld, be)


def chain_up_kernel(count, ab_ref, s_ref):
    def step(i, state):
        s_ref[i] = state.astype(BF16)
        tail = ab_ref[i, DK + HALF:, :].astype(F32)
        decay = jnp.exp(jnp.sum(tail, axis=0, keepdims=True))
        high, low = split(state)
        moved = dot1(jnp.concatenate([high, low], axis=0), ab_ref[i, 0:DK, :])
        written = ab_ref[i, DK:DK + HALF, :].astype(F32)
        return decay * state - (moved[:HALF] + moved[HALF:]) + written

    lax.fori_loop(0, count, step, jnp.zeros((HALF, DK), F32), unroll=True)


def chain_down_kernel(count, ab_ref, g_ref, l_ref):
    def step(j, state):
        i = count - 1 - j
        l_ref[i] = state.astype(BF16)
        tail = ab_ref[i, DK + HALF:, :].astype(F32)
        decay = jnp.exp(jnp.sum(tail, axis=0, keepdims=True))
        high, low = split(state)
        moved = dot1(jnp.concatenate([high, low], axis=0), ab_ref[i, 0:DK, :], NT)
        return decay * state - (moved[:HALF] + moved[HALF:]) + g_ref[i].astype(F32)

    lax.fori_loop(0, count, step, jnp.zeros((HALF, DK), F32), unroll=True)


def chain(kernel, count, *args):
    return pl.pallas_call(
        functools.partial(kernel, count),
        out_shape=jax.ShapeDtypeStruct((count, HALF, DK), BF16),
        compiler_params=pltpu.CompilerParams(vmem_limit_bytes=48 << 20),
        name="chain",
    )(*args)


def gate_kernel(heads, s_ref, gate_ref, bg_ref, io_ref, u0_ref, kg_ref, r_ref,
                normed_ref, gg_ref, do_ref, u_ref, g_ref):
    for local in range(heads):
        lanes = slice(local * DV, (local + 1) * DV)
        state = s_ref[local]
        reach = r_ref[local]
        out = io_ref[local] + dot1(reach, state, NT)
        u_ref[local] = (u0_ref[local] - dot1(kg_ref[local], state, NT)).astype(BF16)
        scale = lax.rsqrt(jnp.mean(out * out, axis=-1, keepdims=True) + NORM_EPS)
        z = out * scale
        gate = gate_ref[:, lanes].astype(F32)
        sig = 1.0 / (1.0 + jnp.exp(-gate))
        sil = gate * sig
        normed_ref[:, lanes] = (z * sil).astype(BF16)
        bg = bg_ref[:, lanes].astype(F32)
        gg_ref[:, lanes] = (bg * z * (sig + sil * (1.0 - sig))).astype(BF16)
        dz = bg * sil
        d_out = scale * (dz - z * jnp.mean(dz * z, axis=-1, keepdims=True))
        d_out = d_out.astype(BF16)
        do_ref[local] = d_out
        g_ref[local] = dot1(d_out, reach, TN).astype(BF16)


def gate_local(s, gate, bg, io, u0, kg, r, heads=4):
    steps = VALUE_HEADS // heads
    head_block = pl.BlockSpec((heads, T, DK), lambda i: (i, 0, 0))
    flat = pl.BlockSpec((T, heads * DV), lambda i: (0, i))
    per_head = jax.ShapeDtypeStruct((VALUE_HEADS, T, DK), BF16)
    tokens = jax.ShapeDtypeStruct((T, VALUE_HEADS * DV), BF16)
    return pl.pallas_call(
        functools.partial(gate_kernel, heads),
        grid=(steps,),
        in_specs=[head_block, flat, flat] + [head_block] * 4,
        out_specs=[flat, flat] + [head_block] * 3,
        out_shape=[tokens, tokens, per_head, per_head, per_head],
        compiler_params=pltpu.CompilerParams(vmem_limit_bytes=48 << 20),
        name="gate_local",
    )(s, gate, bg, io, u0, kg, r)


def backward_kernel(heads, q_ref, k_ref, ld_ref, be_ref, t_ref, p_ref, u_ref, do_ref, s_ref, l_ref,
                    dq_ref, dk_ref, dv_ref):
    group = pl.program_id(0)
    row, col = grid_index()
    causal, strict = row >= col, row > col
    cum = cumulative_decay(ld_ref[...], row, col)
    cum_t = cum.T
    beta = be_ref[...]
    for key_head in range(heads):
        lanes = slice(key_head * DK, (key_head + 1) * DK)
        q = q_ref[:, lanes].astype(F32)
        k = k_ref[:, lanes].astype(F32)
        q_scale, k_scale = unit(q), unit(k)
        qn = q * q_scale * DK ** (-0.5)
        kn = k * k_scale
        qn_b, kn_b = qn.astype(BF16), kn.astype(BF16)
        dqn = jnp.zeros((T, DK), F32)
        dkn = jnp.zeros((T, DK), F32)
        for sub in range(2):
            local = 2 * key_head + sub
            head = 2 * heads * group + local
            cum_col = column(cum, head)
            cum_row = as_row(cum_t, head)
            rate = column(beta, head)
            within = decay_within(cum_col, cum_row, causal)
            growth = jnp.exp(cum_col)
            fade = jnp.exp(cum_col[T - 1:, :] - cum_col)
            state, leaving = s_ref[local], l_ref[local]
            u, d_out = u_ref[local], do_ref[local]
            du = dot1(p_ref[local], d_out, TN) + fade * dot1(kn_b, leaving, NT)
            dx = dot1(t_ref[local], du, TN)
            dv_ref[:, local * DV:(local + 1) * DV] = (rate * dx).astype(BF16)
            dx_b = dx.astype(BF16)
            d_scores = dot1(d_out, u, NT) * within
            d_inter = jnp.where(strict, dot1(dx_b, u, NT) * within, 0.0) * (-rate)
            both = d_inter + d_inter.T
            d_scores_b = d_scores.astype(BF16)
            dqn += growth * dot1(d_out, state) + dot1(d_scores_b, kn_b)
            dkn += (dot1(d_scores_b, qn_b, TN) + dot1(both, kn_b)
                    - (rate * growth) * dot1(dx_b, state) + fade * dot1(u, leaving))
        dq = q_scale * DK ** (-0.5) * (
            dqn - q * (q_scale * q_scale) * jnp.sum(q * dqn, axis=-1, keepdims=True))
        dk = k_scale * (dkn - k * (k_scale * k_scale) * jnp.sum(k * dkn, axis=-1, keepdims=True))
        dq_ref[:, lanes] = dq.astype(BF16)
        dk_ref[:, lanes] = dk.astype(BF16)


def backward_local(q, k, ld, be, t, p, u, d_out, s, l, heads=2):
    steps = HK // heads
    nv = 2 * heads
    head_block = pl.BlockSpec((nv, T, DK), lambda i: (i, 0, 0))
    keys = pl.BlockSpec((T, heads * DK), lambda i: (0, i))
    values = pl.BlockSpec((T, nv * DV), lambda i: (0, i))
    whole = pl.BlockSpec((T, VALUE_HEADS), lambda i: (0, 0))
    return pl.pallas_call(
        functools.partial(backward_kernel, heads),
        grid=(steps,),
        in_specs=[keys, keys, whole, whole] + [head_block] * 6,
        out_specs=[keys, keys, values],
        out_shape=[
            jax.ShapeDtypeStruct((T, HK * DK), BF16),
            jax.ShapeDtypeStruct((T, HK * DK), BF16),
            jax.ShapeDtypeStruct((T, VALUE_HEADS * DV), BF16),
        ],
        compiler_params=pltpu.CompilerParams(vmem_limit_bytes=48 << 20),
        name="backward_local",
    )(q, k, ld, be, t, p, u, d_out, s, l)


def pair_weights(log_ratio, pairing):
    seq_count = log_ratio.shape[0]
    couples = pairing.reshape(seq_count // 2, 2)
    seq_index = lax.broadcasted_iota(jnp.int32, (seq_count // 2, seq_count), 1)
    chosen = (couples[:, :1] == seq_index).astype(log_ratio.dtype)
    rejected = (couples[:, 1:] == seq_index).astype(log_ratio.dtype)
    ratio_c = jnp.sum(chosen * log_ratio[None, :], axis=1)
    ratio_r = jnp.sum(rejected * log_ratio[None, :], axis=1)
    margin = CHI_BETA * (jnp.exp(ratio_c) + ratio_c - jnp.exp(ratio_r) - ratio_r)
    pull_scale = CHI_BETA * jax.nn.sigmoid(-margin)
    weight_c = -pull_scale * (jnp.exp(ratio_c) + 1.0)
    weight_r = pull_scale * (jnp.exp(ratio_r) + 1.0)
    return jnp.sum(chosen * weight_c[:, None] + rejected * weight_r[:, None], axis=0)


def exchange(x, axis):
    return lax.all_to_all(x, axis, split_axis=0, concat_axis=0, tiled=True)


def body(query_vectors, key_vectors, value_vectors, output_gate, log_decay, write_rate,
         out_weight, cotangent, lengths, pairing, log_ratio):
    q, k, v, gate = query_vectors[0], key_vectors[0], value_vectors[0], output_gate[0]
    ld, be = log_decay[0], write_rate[0]
    tokens = q.shape[0]
    count = lax.axis_size("ctx")
    seqs = lax.axis_size("fsdp")
    own_seq = lax.axis_index("fsdp")
    features = out_weight.shape[0]

    with jax.named_scope("scaled_cotangent"):
        weights = pair_weights(log_ratio, pairing)
        seq_ids = lax.broadcasted_iota(jnp.int32, weights.shape, 0)
        own_weight = jnp.sum(jnp.where(seq_ids == own_seq, weights, 0.0))
        own_length = jnp.sum(jnp.where(seq_ids == own_seq, lengths, 0))
        positions = lax.axis_index("ctx") * tokens + lax.broadcasted_iota(
            jnp.int32, (tokens, 1), 0)
        live = (positions < own_length).astype(F32)
        scaled = (cotangent[0].astype(F32) * (own_weight * live)).astype(BF16)
        every_scaled = lax.all_gather(scaled, "fsdp", axis=0, tiled=True)
    with jax.named_scope("back_grad"):
        bg_slice = lax.dot_general(every_scaled, out_weight, NT,
                                   preferred_element_type=F32).astype(BF16)
        bg_all = lax.all_gather(bg_slice, "fsdp", axis=0)
        bg = lax.dynamic_slice_in_dim(bg_all, own_seq * tokens, tokens, axis=1)
        bg = jnp.swapaxes(bg, 0, 1).reshape(tokens, seqs * features)

    ab, t, p, u0, kg, r, io = forward_local(q, k, v, ld, be)
    ab = exchange(ab, "ctx")
    entering = exchange(chain(chain_up_kernel, count, ab), "ctx").reshape(VALUE_HEADS, DV, DK)
    normed, gate_grad, d_out, u, g = gate_local(entering, gate, bg, io, u0, kg, r)
    with jax.named_scope("every_normed"):
        every_normed = lax.all_gather(normed, "fsdp", axis=0, tiled=True)
        rows = lax.dynamic_slice_in_dim(every_normed, own_seq * features, features, axis=1)
    with jax.named_scope("mixed_out"):
        mixed = lax.dot_general(rows, out_weight, NN, preferred_element_type=F32).astype(BF16)
        mixed = lax.psum_scatter(mixed, "fsdp", scatter_dimension=0, tiled=True)
    with jax.named_scope("weight_grad"):
        partial = lax.dot_general(rows, every_scaled, TN, preferred_element_type=F32).astype(BF16)
        weight_grad = lax.psum_scatter(
            partial, "ctx", scatter_dimension=0, tiled=True).astype(F32)
    g = exchange(g.reshape(count, HALF, DK), "ctx")
    leaving = exchange(chain(chain_down_kernel, count, ab, g), "ctx").reshape(VALUE_HEADS, DV, DK)
    dq, dk, dv = backward_local(q, k, ld, be, t, p, u, d_out, entering, leaving)
    return mixed[None], dq[None], dk[None], dv[None], gate_grad[None], weight_grad


def solution(mesh):
    tokens = P("fsdp", "ctx", None)
    return jax.shard_map(
        body,
        mesh=mesh,
        in_specs=(tokens,) * 6 + (P("fsdp", None), tokens, P(), P(), P()),
        out_specs=(tokens,) * 5 + (P(("fsdp", "ctx"), None),),
        check_vma=False,
    )
```

time: 1200 us -> 313 us (0.26); the launches traced: 1180 us -> 311 us
  matrix products: 341 us -> 11.6 us
  local copies, waits for them, and re-layouts: 346 us -> 19.7 us
  waiting for transfers between devices: 447 us -> 127 us
  blocking collectives: 0 us -> 64 us
  Pallas kernels: 0 us -> 62.7 us
    all_gather x5 -> x2, waiting for transfers between devices: 379 us -> 28 us  [the longest x1 28 us: body(): every_normed = lax.all_gather(normed, 'fsdp', axis=0, tiled=True)]
    dot_general x147 -> x3, matrix products: 341 us -> 11.6 us  [the longest x1 4.36 us: body(): lax.dot_general(rows, every_scaled, TN, preferred_element_type=F32)]
    dynamic_slice x124 -> x1, local copies, waits for them, and re-layouts: 203 us -> 1.09 us  [body(): bg = lax.dynamic_slice_in_dim(bg_all, own_seq * tokens, tokens, axis=1)]
    while x268 -> x0, local copies, waits for them, and re-layouts: 102 us -> none
    all_to_all x0 -> x3, blocking collectives: none -> 64 us  [exchange(): return lax.all_to_all(x, axis, split_axis=0, concat_axis=0, tiled=True)]
    pallas_call x0 -> x5, Pallas kernels: none -> 62.7 us  [the longest x1 37.5 us: forward_local(): pl.pallas_call(functools.partial(forward_kernel, heads), grid=(steps,), i...]
    all_gather x1, waiting for transfers between devices: 0.01 us -> 33.6 us  [body(): every_scaled = lax.all_gather(scaled, 'fsdp', axis=0, tiled=True)]
    another operation x9 -> x0, local copies, waits for them, and re-layouts: 12.4 us -> none
  transfers between devices with their start and end apart: 8 -> 6, of which waited for: 7 -> 5; matrix products, arithmetic and copies ran while one was open for 31% -> 2% of each run, Pallas kernels for 0% -> 18%
where the time goes in v1:
time: 313 us; the launch traced here: 311 us
  waiting for transfers between devices  127 us (41%)
  blocking collectives  64 us (20%)
  Pallas kernels  62.7 us (20%)
  local copies, waits for them, and re-layouts  19.7 us (6%)
  between operations  14 us (4%)
  matrix products  11.6 us (4%)
  other arithmetic  7.69 us (2%)
  starting transfers between devices  4.33 us (1%)
    all_to_all x3, blocking collectives, exchange(): return lax.all_to_all(x, axis, split_axis=0, concat_axis=0, tiled=True)  64 us
    pallas_call x1, Pallas kernels, forward_local(): pl.pallas_call(functools.partial(forward_kernel, heads), grid=(steps,), i...  37.5 us
    all_gather x1, waiting for transfers between devices, body(): every_scaled = lax.all_gather(scaled, 'fsdp', axis=0, tiled=True)  33.6 us
    reduce_scatter x1, waiting for transfers between devices, body(): mixed = lax.psum_scatter(mixed, 'fsdp', scatter_dimension=0, tiled=True)  30.6 us
    all_gather x1, waiting for transfers between devices, body(): every_normed = lax.all_gather(normed, 'fsdp', axis=0, tiled=True)  28 us
    reduce_scatter x1, waiting for transfers between devices, body(): lax.psum_scatter(partial, 'ctx', scatter_dimension=0, tiled=True)  24.9 us
    unnamed x60, local copies, waits for them, and re-layouts  17.6 us
    pallas_call x1, Pallas kernels, backward_local(): pl.pallas_call(functools.partial(backward_kernel, heads), grid=(steps,),...  10.7 us
  transfers between devices with their start and end apart: 6, of which 5 were waited for; matrix products, arithmetic and copies ran while one was open for 2% of the time, Pallas kernels for 18%

profile of v1, /device:TPU:0, one launch (start us, length us, event | category | flops | bytes accessed | tf_op | source)
XLA Modules:
  0.0 310.7 jit_solution(1952838480066159931)
XLA Ops:
  7.2 0.0 copy-start
  7.2 0.0 all-gather.5.cloned.1.call-start
  7.2 0.9 reshape.63
  8.1 0.2 slice_reduce_fusion.1
  8.3 0.9 select_reduce_fusion.1
  9.2 1.3 fusion.6
  10.5 0.1 add_reduce_fusion
  10.6 0.6 fusion.7
  11.2 1.3 compare_select_fusion
  12.5 2.0 fusion
  14.5 0.0 all-gather.5.cloned.1.call-update
  14.5 0.0 copy-start.26
  14.5 0.0 copy-start.27
  14.5 0.0 copy-start.6
  14.6 0.0 all-gather.9.cloned.1.call-start
  14.6 33.6 %all-gather.5.cloned.1.call-done = bf16[512,2048]{1,0:T(8,128)(2,1)} async-done(((bf16[128,2048]{1,0:T(8,128)(2,1)}), bf16[512,2048]{1,0:T(8,128)(2,1)}) %all-gather.5.cloned.1.call-update) | async-done | bytes 2097168 | tf_op jit(solution)/shard_map/scaled_cotangent/all_gather | solution.py:350
  48.2 3.7 %convolution_convert_fusion.2 = bf16[512,512]{1,0:T(8,128)(2,1)} fusion(bf16[512,2048]{1,0:T(8,128)(2,1)} %all-gather.5.cloned.1.call-done, bf16[512,2048]{1,0:T(8,128)(2,1)S(1)} %copy-done), kind=kOutput, calls=%fused_computation.2 | convolution fusion | flops 1074003968 | bytes 4718592 | tf_op jit(solution)/shard_map/back_grad/dot_general | solution.py:352
  51.9 0.0 all-gather.9.cloned.1.call-update
  51.9 0.1 copy.23
  52.0 0.1 copy.24
  52.1 1.0 copy-done.14
  53.2 37.5 %forward_local.1 = (bf16[32,208,128]{2,1,0:T(8,128)(2,1)}, bf16[16,128,128]{2,1,0:T(8,128)(2,1)S(1)}, bf16[16,128,128]{2,1,0:T(8,128)(2,1)S(1)}, f32[16,128,128]...) custom-call(bf16[128,1024]{1,0:T(8,128)(2,1)S(1)} %bitcast.29, ...), custom_call_target="tpu_custom_call" | custom-call | tf_op jit(solution)/shard_map/forward_local/pallas_call | solution.py:147
  90.7 1.0 copy-done.3
  91.7 1.1 copy-done.4
  92.7 0.8 copy-done.10
  93.5 0.8 copy-done.18
  94.4 0.8 copy-done.20
  95.2 30.9 %all_to_all.20.ab_ref = bf16[32,208,128]{2,1,0:T(8,128)(2,1)S(1)} all-to-all(bf16[32,208,128]{2,1,0:T(8,128)(2,1)} %get-tuple-element.21), channel_id=1, replica_groups=mesh['fsdp'=4,'ctx'=32] {'ctx'}, dimensions={0} | all-to-all | bytes 3407872 | tf_op jit(solution)/shard_map/all_to_all | solution.py:328
  126.0 4.7 %chain.2 = bf16[32,64,128]{2,1,0:T(8,128)(2,1)} custom-call(bf16[32,208,128]{2,1,0:T(8,128)(2,1)S(1)} %all_to_all.20.ab_ref), custom_call_target="tpu_custom_call" | custom-call | tf_op jit(solution)/shard_map/chain/pallas_call | solution.py:195
  130.8 1.2 copy-done.1
  132.0 4.1 %all-to-all-start.1 = ((bf16[32,64,128]{2,1,0:T(8,128)(2,1)}), bf16[32,64,128]{2,1,0:T(8,128)(2,1)S(1)}, u32[]{:S(2)}, u32[]{:S(2)}) async-start(bf16[32,64,128]{2,1,0:T(8,128)(2,1)} %chain.2), calls=%async_computation.1 | async-start | bytes 1048576 | tf_op jit(solution)/shard_map/all_to_all | solution.py:328
  136.1 0.0 all-gather.7.cloned.1.call-start
  136.2 0.0 all-gather.9.cloned.1.call-done
  136.2 1.1 constant_dynamic-slice_fusion
  137.3 0.4 copy.26
  137.7 0.1 copy.27
  137.8 9.5 %all-to-all-done.1 = bf16[32,64,128]{2,1,0:T(8,128)(2,1)S(1)} async-done(((bf16[32,64,128]{2,1,0:T(8,128)(2,1)}), bf16[32,64,128]{2,1,0:T(8,128)(2,1)S(1)}, u32[]{:S(2)}, u32[]{:S(2)}) %all-to-all-start.1) | async-done | bytes 524320 | tf_op jit(solution)/shard_map/all_to_all | solution.py:328
  147.3 1.2 copy-done.5
  148.5 1.0 copy-done.9
  149.6 1.0 copy-done.11
  150.6 1.0 copy-done.13
  151.7 5.8 %gate_local.1 = (bf16[128,2048]{1,0:T(8,128)(2,1)S(1)}, bf16[128,2048]{1,0:T(8,128)(2,1)}, bf16[16,128,128]{2,1,0:T(8,128)(2,1)S(1)}, bf16[16,128,128]{2,1,0:T(8,128)(2,1)S(1)}, bf16[16,128,128]{2,1,0:T(8,128)(2,1)S(1)}) custom-call(bf16[16,128,128]{2,1,0:T(8,128)(2,1)S(1)} %bitcast.25, bf16[128,2048]{1,0:T(8,128)(2,1)S(1)} %bitcast.37, ...), custom_call_target="tpu_custom_call" | custom-call | tf_op jit(solution)/shard_map/gate_local/pallas_call | solution.py:232
  157.4 0.8 copy-done.15
  158.2 0.8 copy-done.17
  159.0 0.8 copy-done.22
  159.8 0.8 copy-done.24
  160.6 0.0 all-gather.7.cloned.1.call-update
  160.7 0.0 reduce-scatter.5.cloned.1.call-start
  160.7 28.0 %all-gather.7.cloned.1.call-done = bf16[512,2048]{1,0:T(8,128)(2,1)} async-done(((bf16[128,2048]{1,0:T(8,128)(2,1)}), bf16[512,2048]{1,0:T(8,128)(2,1)}) %all-gather.7.cloned.1.call-update) | async-done | bytes 2097168 | tf_op jit(solution)/shard_map/every_normed/all_gather | solution.py:363
  188.7 4.4 %convolution_convert_fusion = bf16[512,2048]{1,0:T(8,128)(2,1)} fusion(bf16[512,2048]{1,0:T(8,128)(2,1)} %all-gather.5.cloned.1.call-done, bf16[512,2048]{1,0:T(8,128)(2,1)} %all-gather.7.cloned.1.call-done, s32[]{:T(128)S(6)} %select_n.17), kind=kOutput, calls=%fused_computation | convolution fusion | flops 1074790400 | bytes 4718596 | tf_op jit(solution)/shard_map/weight_grad/dot_general | solution.py:369
  193.1 0.0 reduce-scatter.5.cloned.1.call-update
  193.1 0.0 reduce-scatter.3.cloned.1.call-start
  193.2 3.6 %convolution_convert_fusion.1 = bf16[512,2048]{1,0:T(8,128)(2,1)} fusion(bf16[512,2048]{1,0:T(8,128)(2,1)S(1)} %copy-done, bf16[512,2048]{1,0:T(8,128)(2,1)} %all-gather.7.cloned.1.call-done, s32[]{:T(128)S(6)} %select_n.17), kind=kOutput, calls=%fused_computation.1 | convolution fusion | flops 1074790400 | bytes 4718596 | tf_op jit(solution)/shard_map/mixed_out/dot_general | solution.py:366
  196.8 0.0 reduce-scatter.3.cloned.1.call-update
  196.8 1.0 copy-done.16
  197.8 18.1 %all_to_all.21.g_ref = bf16[32,64,128]{2,1,0:T(8,128)(2,1)S(1)} all-to-all(bf16[32,64,128]{2,1,0:T(8,128)(2,1)S(1)} %bitcast.39), channel_id=1, replica_groups=mesh['fsdp'=4,'ctx'=32] {'ctx'}, dimensions={0} | all-to-all | bytes 1048576 | tf_op jit(solution)/shard_map/all_to_all | solution.py:328
  215.9 1.5 copy-done.2
  217.4 0.0 copy-start.25
  217.4 4.0 %chain.3 = bf16[32,64,128]{2,1,0:T(8,128)(2,1)S(1)} custom-call(bf16[32,208,128]{2,1,0:T(8,128)(2,1)S(1)} %copy-done.2, bf16[32,64,128]{2,1,0:T(8,128)(2,1)S(1)} %all_to_all.21.g_ref), custom_call_target="tpu_custom_call" | custom-call | tf_op jit(solution)/shard_map/chain/pallas_call | solution.py:195
  221.4 15.0 %all_to_all.22 = bf16[32,64,128]{2,1,0:T(8,128)(2,1)S(1)} all-to-all(bf16[32,64,128]{2,1,0:T(8,128)(2,1)S(1)} %chain.3), channel_id=1, replica_groups=mesh['fsdp'=4,'ctx'=32] {'ctx'}, dimensions={0} | all-to-all | bytes 1048576 | tf_op jit(solution)/shard_map/all_to_all | solution.py:328
  236.4 10.7 %backward_local.1 = (bf16[128,1024]{1,0:T(8,128)(2,1)}, bf16[128,1024]{1,0:T(8,128)(2,1)}, bf16[128,2048]{1,0:T(8,128)(2,1)}) custom-call(bf16[128,1024]{1,0:T(8,128)(2,1)S(1)} %bitcast.30, bf16[128,1024]{1,0:T(8,128)(2,1)S(1)} %bitcast.32, f32[128,16]{1,0:T(8,128)S(1)} %bitcast.34, f32[128,16]{1,0:T(8,128)S(1)} %bitcast.36, ...), custom_call_target="tpu_custom_call" | custom-call | tf_op jit(solution)/shard_map/backward_local/pallas_call | solution.py:297
  247.2 24.9 %reduce-scatter.5.cloned.1.call-done = bf16[16,2048]{1,0:T(8,128)(2,1)} async-done(((bf16[512,2048]{1,0:T(8,128)(2,1)}), bf16[16,2048]{1,0:T(8,128)(2,1)}) %reduce-scatter.5.cloned.1.call-update) | async-done | bytes 65552 | tf_op jit(solution)/shard_map/weight_grad/reduce_scatter | solution.py:370
  272.1 1.5 convert_element_type.30
  273.6 30.6 %reduce-scatter.3.cloned.1.call-done = bf16[128,2048]{1,0:T(8,128)(2,1)} async-done(((bf16[512,2048]{1,0:T(8,128)(2,1)}), bf16[128,2048]{1,0:T(8,128)(2,1)}) %reduce-scatter.3.cloned.1.call-update) | async-done | bytes 524304 | tf_op jit(solution)/shard_map/mixed_out/reduce_scatter | solution.py:367
  (36 shorter events, 0.1 us)
Async XLA Ops:
  7.2 41.0 %copy-start = (bf16[512,2048]{1,0:T(8,128)(2,1)S(1)}, bf16[512,2048]{1,0:T(8,128)(2,1)}, u32[]{:S(2)}) copy-start(bf16[512,2048]{1,0:T(8,128)(2,1)} %param.17) | copy-start | bytes 6291460
  7.2 41.0 %all-gather.5.cloned.1.call-start = ((), (), s32[]{:S(2)}) async-start(), calls=%async_computation.6 | async-start | bytes 2621440 | tf_op jit(solution)/shard_map/scaled_cotangent/all_gather | solution.py:350
  14.5 37.4 %copy-start.26 = (f32[1,128,16]{1,2,0:T(8,128)S(1)}, f32[1,128,16]{1,2,0:T(8,128)}, u32[]{:S(2)}) copy-start(f32[1,128,16]{1,2,0:T(8,128)} %param.15) | copy-start | bytes 24580
  14.5 37.5 %copy-start.27 = (f32[1,128,16]{1,2,0:T(8,128)S(1)}, f32[1,128,16]{1,2,0:T(8,128)}, u32[]{:S(2)}) copy-start(f32[1,128,16]{1,2,0:T(8,128)} %param.16) | copy-start | bytes 24580
  14.5 37.6 %copy-start.6 = (bf16[1,128,1024]{2,1,0:T(8,128)(2,1)S(1)}, bf16[1,128,1024]{2,1,0:T(8,128)(2,1)}, u32[]{:S(2)}) copy-start(bf16[1,128,1024]{2,1,0:T(8,128)(2,1)} %param.11) | copy-start | bytes 786436
  14.6 37.6 %copy-start.7 = (bf16[1,128,1024]{2,1,0:T(8,128)(2,1)S(1)}, bf16[1,128,1024]{2,1,0:T(8,128)(2,1)}, u32[]{:S(2)}) copy-start(bf16[1,128,1024]{2,1,0:T(8,128)(2,1)} %param.12) | copy-start | bytes 786436
  14.6 121.6 %all-gather.9.cloned.1.call-start = ((), (), s32[]{:S(2)}) async-start(), calls=%async_computation.10 | async-start | bytes 2621440 | tf_op jit(solution)/shard_map/back_grad/all_gather | solution.py:354
  52.1 1.0 copy-start.14
  90.7 1.0 copy-start.3
  91.7 1.1 copy-start.4
  92.7 0.8 copy-start.10
  93.5 0.8 copy-start.18
  94.3 0.8 copy-start.20
  95.2 35.6 %copy-start.12 = (bf16[16,128,128]{2,1,0:T(8,128)(2,1)}, bf16[16,128,128]{2,1,0:T(8,128)(2,1)S(1)}, u32[]{:S(2)}) copy-start(bf16[16,128,128]{2,1,0:T(8,128)(2,1)S(1)} %get-tuple-element.25.r_ref) | copy-start | bytes 1572868
  130.8 1.2 copy-start.1
  132.0 15.3 %all-to-all-start.1 = ((bf16[32,64,128]{2,1,0:T(8,128)(2,1)}), bf16[32,64,128]{2,1,0:T(8,128)(2,1)S(1)}, u32[]{:S(2)}, u32[]{:S(2)}) async-start(bf16[32,64,128]{2,1,0:T(8,128)(2,1)} %chain.2), calls=%async_computation.1 | async-start | bytes 1048576 | tf_op jit(solution)/shard_map/all_to_all | solution.py:328
  136.1 52.6 %all-gather.7.cloned.1.call-start = ((), (), s32[]{:S(2)}) async-start(), calls=%async_computation.7 | async-start | bytes 2621440 | tf_op jit(solution)/shard_map/every_normed/all_gather | solution.py:363
  147.3 1.2 copy-start.5
  148.5 1.0 copy-start.9
  149.6 1.0 copy-start.11
  150.6 1.0 copy-start.13
  157.4 0.8 copy-start.15
  158.2 0.8 copy-start.17
  159.0 0.8 copy-start.22
  159.8 0.8 copy-start.24
  160.7 111.4 %reduce-scatter.5.cloned.1.call-start = ((), (), s32[]{:S(2)}) async-start(), calls=%async_computation.9 | async-start | bytes 2162688 | tf_op jit(solution)/shard_map/weight_grad/reduce_scatter | solution.py:370
  193.1 111.1 %reduce-scatter.3.cloned.1.call-start = ((), (), s32[]{:S(2)}) async-start(), calls=%async_computation.8 | async-start | bytes 2621440 | tf_op jit(solution)/shard_map/mixed_out/reduce_scatter | solution.py:367
  196.8 1.0 copy-start.16
  215.9 1.5 copy-start.2
  217.4 19.0 %copy-start.8 = (bf16[1,128,1024]{2,1,0:T(8,128)(2,1)S(1)}, bf16[1,128,1024]{2,1,0:T(8,128)(2,1)}, u32[]{:S(2)}) copy-start(bf16[1,128,1024]{2,1,0:T(8,128)(2,1)} %param.12) | copy-start | bytes 786436
  217.4 19.1 %copy-start.19 = (bf16[16,128,128]{2,1,0:T(8,128)(2,1)S(1)}, bf16[16,128,128]{2,1,0:T(8,128)(2,1)}, u32[]{:S(2)}) copy-start(bf16[16,128,128]{2,1,0:T(8,128)(2,1)} %copy-done.18) | copy-start | bytes 1572868
  217.4 19.1 %copy-start.21 = (bf16[16,128,128]{2,1,0:T(8,128)(2,1)S(1)}, bf16[16,128,128]{2,1,0:T(8,128)(2,1)}, u32[]{:S(2)}) copy-start(bf16[16,128,128]{2,1,0:T(8,128)(2,1)} %copy-done.20) | copy-start | bytes 1572868
  217.4 19.1 %copy-start.23 = (bf16[16,128,128]{2,1,0:T(8,128)(2,1)S(1)}, bf16[16,128,128]{2,1,0:T(8,128)(2,1)}, u32[]{:S(2)}) copy-start(bf16[16,128,128]{2,1,0:T(8,128)(2,1)} %copy-done.22) | copy-start | bytes 1572868
  217.4 19.1 %copy-start.25 = (bf16[16,128,128]{2,1,0:T(8,128)(2,1)S(1)}, bf16[16,128,128]{2,1,0:T(8,128)(2,1)}, u32[]{:S(2)}) copy-start(bf16[16,128,128]{2,1,0:T(8,128)(2,1)} %copy-done.24) | copy-start | bytes 1572868
Sparse Core Ops, SparseCore 0:
  14.6 33.5 all-gather.4
  52.0 31.0 all-gather.8
  160.8 27.8 all-gather.6
  193.2 78.7 reduce-scatter.4
  274.9 29.2 reduce-scatter.2

commit v2 on v1

v2 whole, which is shorter than its diff:
```python
import functools

import jax
import jax.numpy as jnp
from jax import lax
from jax.experimental import pallas as pl
from jax.experimental.pallas import tpu as pltpu
from jax.sharding import PartitionSpec as P

VALUE_HEADS = 16
HK = 8
DK = 128
DV = 128
T = 128
HALF = 64
TAIL = 16
CHI_BETA = 0.5
NORM_EPS = 1e-06
F32 = jnp.float32
BF16 = jnp.bfloat16

NN = (((1,), (0,)), ((), ()))
NT = (((1,), (1,)), ((), ()))
TN = (((0,), (0,)), ((), ()))


def dot1(a, b, dims=NN):
    return lax.dot_general(a.astype(BF16), b.astype(BF16), dims, preferred_element_type=F32)


def split(a):
    high = a.astype(BF16)
    return high, (a - high.astype(F32)).astype(BF16)


def dot3(a, b, dims=NN):
    a_high, a_low = split(a)
    b_high, b_low = split(b)
    return dot1(a_high, b_high, dims) + (dot1(a_low, b_high, dims) + dot1(a_high, b_low, dims))


def grid_index():
    row = lax.broadcasted_iota(jnp.int32, (T, T), 0)
    col = lax.broadcasted_iota(jnp.int32, (T, T), 1)
    return row, col


def unit(x):
    return lax.rsqrt(jnp.sum(x * x, axis=-1, keepdims=True) + NORM_EPS)


def cumulative_decay(decay, row, col):
    lower = (row >= col).astype(BF16)
    first, rest = decay.astype(BF16), decay
    rest = rest - first.astype(F32)
    second = rest.astype(BF16)
    third = (rest - second.astype(F32)).astype(BF16)
    return dot1(lower, first) + (dot1(lower, second) + dot1(lower, third))


def column(table, head):
    lane = lax.broadcasted_iota(jnp.int32, table.shape, 1)
    return jnp.sum(jnp.where(lane == head, table, 0.0), axis=1, keepdims=True)


def as_row(table_t, head):
    sub = lax.broadcasted_iota(jnp.int32, table_t.shape, 0)
    return jnp.sum(jnp.where(sub == head, table_t, 0.0), axis=0, keepdims=True)


def decay_within(cum_col, cum_row, causal):
    return jnp.where(causal, jnp.exp(jnp.where(causal, cum_col - cum_row, 0.0)), 0.0)


def invert(couplings, row, col):
    eye = (row == col).astype(F32)
    pairs = (row >> 1) == (col >> 1)
    inverses = [eye - jnp.where(pairs, c, 0.0) for c in couplings]
    for level in range(1, 7):
        mask = ((row >> (level + 1)) == (col >> (level + 1))) & ((row >> level) != (col >> level))
        offs = [jnp.where(mask, c, 0.0).astype(BF16) for c in couplings]
        low = [i.astype(BF16) for i in inverses]
        inner = [dot1(o, i) for o, i in zip(offs, low)]
        inverses = [x - dot1(i, n) for x, i, n in zip(inverses, low, inner)]
    residuals = [eye - i - dot3(c, i) for c, i in zip(couplings, inverses)]
    return [i + dot1(i, r) for i, r in zip(inverses, residuals)]


def total_rows(total):
    wide = jnp.broadcast_to(total, (TAIL, DK))
    high, low = split(wide)
    low2 = (wide - high.astype(F32) - low.astype(F32)).astype(BF16)
    sub_row = lax.broadcasted_iota(jnp.int32, (TAIL, DK), 0)
    tail = jnp.where(sub_row == 0, high.astype(F32),
                     jnp.where(sub_row == 1, low.astype(F32),
                               jnp.where(sub_row == 2, low2.astype(F32), 0.0)))
    return tail.astype(BF16)


def write_kernel(heads, k_ref, v_ref, ld_ref, be_ref, ab_ref, t_ref, u0_ref, kg_ref):
    group = pl.program_id(0)
    row, col = grid_index()
    causal, strict = row >= col, row > col
    cum = cumulative_decay(ld_ref[...], row, col)
    cum_t = cum.T
    beta = be_ref[...]
    kns, kks = [], []
    for key_head in range(heads):
        k = k_ref[:, key_head * DK:(key_head + 1) * DK].astype(F32)
        kn = k * unit(k)
        kns.append(kn)
        kks.append(dot3(kn, kn, NT))
    cols, rates, couplings = [], [], []
    for local in range(2 * heads):
        head = 2 * heads * group + local
        cum_col = column(cum, head)
        rate = column(beta, head)
        within = decay_within(cum_col, as_row(cum_t, head), causal)
        couplings.append(jnp.where(strict, kks[local // 2] * within, 0.0) * rate)
        cols.append(cum_col)
        rates.append(rate)
    inverses = [i.astype(BF16) for i in invert(couplings, row, col)]
    u0s = [dot1(i, rates[n] * v_ref[:, n * DV:(n + 1) * DV].astype(F32))
           for n, i in enumerate(inverses)]
    kgs = [dot1(i, (rates[n] * jnp.exp(cols[n])) * kns[n // 2]).astype(BF16)
           for n, i in enumerate(inverses)]
    for n in range(2 * heads):
        total = cols[n][T - 1:, :]
        carried = (jnp.exp(total - cols[n]) * kns[n // 2]).astype(BF16)
        transit = dot1(kgs[n], carried, TN).astype(BF16)
        written = dot1(u0s[n], carried, TN).astype(BF16)
        t_ref[n] = inverses[n]
        u0_ref[n] = u0s[n]
        kg_ref[n] = kgs[n]
        tail = total_rows(total)
        for half in range(2):
            slot = 2 * n + half
            ab_ref[slot, 0:DK, :] = transit
            ab_ref[slot, DK:DK + HALF, :] = written[half * HALF:(half + 1) * HALF]
            ab_ref[slot, DK + HALF:, :] = tail


def read_kernel(heads, q_ref, k_ref, ld_ref, u0_ref, kg_ref, p_ref, r_ref, io_ref):
    group = pl.program_id(0)
    row, col = grid_index()
    causal = row >= col
    cum = cumulative_decay(ld_ref[...], row, col)
    cum_t = cum.T
    qns, qks = [], []
    for key_head in range(heads):
        lanes = slice(key_head * DK, (key_head + 1) * DK)
        q = q_ref[:, lanes].astype(F32)
        k = k_ref[:, lanes].astype(F32)
        qn = q * unit(q) * DK ** (-0.5)
        qns.append(qn)
        qks.append(dot3(qn, k * unit(k), NT))
    cols, scores = [], []
    for local in range(2 * heads):
        head = 2 * heads * group + local
        cum_col = column(cum, head)
        cols.append(cum_col)
        scores.append(
            (qks[local // 2] * decay_within(cum_col, as_row(cum_t, head), causal)).astype(BF16))
    for n in range(2 * heads):
        p_ref[n] = scores[n]
        io_ref[n] = dot1(scores[n], u0_ref[n])
        r_ref[n] = (jnp.exp(cols[n]) * qns[n // 2] - dot1(scores[n], kg_ref[n])).astype(BF16)


def per_head(dtype):
    return jax.ShapeDtypeStruct((VALUE_HEADS, T, DK), dtype)


def head_block(count):
    return pl.BlockSpec((count, T, DK), lambda i: (i, 0, 0))


def flat_block(count):
    return pl.BlockSpec((T, count * DK), lambda i: (0, i))


WHOLE = pl.BlockSpec((T, VALUE_HEADS), lambda i: (0, 0))
PARAMS = pltpu.CompilerParams(vmem_limit_bytes=60 << 20)


def cost(gflops):
    return pl.CostEstimate(flops=int(gflops * 1e9), bytes_accessed=4 << 20, transcendentals=0)


def write_local(k, v, ld, be, heads=2):
    nv = 2 * heads
    rows = DK + HALF + TAIL
    return pl.pallas_call(
        functools.partial(write_kernel, heads),
        grid=(HK // heads,),
        in_specs=[flat_block(heads), flat_block(nv), WHOLE, WHOLE],
        out_specs=[pl.BlockSpec((2 * nv, rows, DK), lambda i: (i, 0, 0))] + [head_block(nv)] * 3,
        out_shape=[jax.ShapeDtypeStruct((2 * VALUE_HEADS, rows, DK), BF16),
                   per_head(BF16), per_head(F32), per_head(BF16)],
        compiler_params=PARAMS,
        cost_estimate=cost(20),
        name="write_local",
    )(k, v, ld, be)


def read_local(q, k, ld, u0, kg, heads=2):
    nv = 2 * heads
    return pl.pallas_call(
        functools.partial(read_kernel, heads),
        grid=(HK // heads,),
        in_specs=[flat_block(heads), flat_block(heads), WHOLE, head_block(nv), head_block(nv)],
        out_specs=[head_block(nv)] * 3,
        out_shape=[per_head(BF16), per_head(BF16), per_head(F32)],
        compiler_params=PARAMS,
        cost_estimate=cost(8),
        name="read_local",
    )(q, k, ld, u0, kg)


def chain_up_kernel(count, ab_ref, s_ref):
    def step(i, state):
        s_ref[i] = state.astype(BF16)
        tail = ab_ref[i, DK + HALF:, :].astype(F32)
        decay = jnp.exp(jnp.sum(tail, axis=0, keepdims=True))
        high, low = split(state)
        moved = dot1(jnp.concatenate([high, low], axis=0), ab_ref[i, 0:DK, :])
        written = ab_ref[i, DK:DK + HALF, :].astype(F32)
        return decay * state - (moved[:HALF] + moved[HALF:]) + written

    lax.fori_loop(0, count, step, jnp.zeros((HALF, DK), F32), unroll=True)


def chain_down_kernel(count, ab_ref, g_ref, l_ref):
    def step(j, state):
        i = count - 1 - j
        l_ref[i] = state.astype(BF16)
        tail = ab_ref[i, DK + HALF:, :].astype(F32)
        decay = jnp.exp(jnp.sum(tail, axis=0, keepdims=True))
        high, low = split(state)
        moved = dot1(jnp.concatenate([high, low], axis=0), ab_ref[i, 0:DK, :], NT)
        return decay * state - (moved[:HALF] + moved[HALF:]) + g_ref[i].astype(F32)

    lax.fori_loop(0, count, step, jnp.zeros((HALF, DK), F32), unroll=True)


def chain(kernel, count, *args):
    return pl.pallas_call(
        functools.partial(kernel, count),
        out_shape=jax.ShapeDtypeStruct((count, HALF, DK), BF16),
        compiler_params=PARAMS,
        cost_estimate=cost(4),
        name="chain",
    )(*args)


def gate_kernel(heads, me_ref, s_ref, gate_ref, bg_ref, io_ref, u0_ref, kg_ref, r_ref,
                normed_ref, gg_ref, do_ref, u_ref, g_ref):
    for local in range(heads):
        lanes = slice(local * DV, (local + 1) * DV)
        state = s_ref[local]
        reach = r_ref[local]
        out = io_ref[local] + dot1(reach, state, NT)
        u_ref[local] = (u0_ref[local] - dot1(kg_ref[local], state, NT)).astype(BF16)
        scale = lax.rsqrt(jnp.mean(out * out, axis=-1, keepdims=True) + NORM_EPS)
        z = out * scale
        gate = gate_ref[:, lanes].astype(F32)
        sig = 1.0 / (1.0 + jnp.exp(-gate))
        sil = gate * sig
        normed_ref[0, :, lanes] = (z * sil).astype(BF16)
        bg = bg_ref[0, :, lanes].astype(F32)
        gg_ref[:, lanes] = (bg * z * (sig + sil * (1.0 - sig))).astype(BF16)
        dz = bg * sil
        d_out = scale * (dz - z * jnp.mean(dz * z, axis=-1, keepdims=True))
        d_out = d_out.astype(BF16)
        do_ref[local] = d_out
        g_ref[local] = dot1(d_out, reach, TN).astype(BF16)


def gate_local(me, s, gate, bg, io, u0, kg, r, seqs):
    heads = VALUE_HEADS // seqs
    blocks = pl.BlockSpec((heads, T, DK), lambda i, me: (i, 0, 0))
    flat = pl.BlockSpec((T, heads * DV), lambda i, me: (0, i))
    crossed = pl.BlockSpec((1, T, heads * DV), lambda i, me: (i ^ me[0], 0, 0))
    tokens = jax.ShapeDtypeStruct((T, VALUE_HEADS * DV), BF16)
    return pl.pallas_call(
        functools.partial(gate_kernel, heads),
        grid_spec=pltpu.PrefetchScalarGridSpec(
            num_scalar_prefetch=1,
            grid=(seqs,),
            in_specs=[blocks, flat, crossed] + [blocks] * 4,
            out_specs=[crossed, flat] + [blocks] * 3,
        ),
        out_shape=[jax.ShapeDtypeStruct((seqs, T, heads * DV), BF16), tokens,
                   per_head(BF16), per_head(BF16), per_head(BF16)],
        compiler_params=PARAMS,
        cost_estimate=cost(5),
        name="gate_local",
    )(me, s, gate, bg, io, u0, kg, r)


def early_kernel(heads, q_ref, k_ref, ld_ref, p_ref, u_ref, do_ref, s_ref,
                 dq_ref, dk_ref, du_ref):
    group = pl.program_id(0)
    row, col = grid_index()
    causal = row >= col
    cum = cumulative_decay(ld_ref[...], row, col)
    cum_t = cum.T
    for key_head in range(heads):
        lanes = slice(key_head * DK, (key_head + 1) * DK)
        q = q_ref[:, lanes].astype(F32)
        k = k_ref[:, lanes].astype(F32)
        q_scale = unit(q)
        qn = (q * q_scale * DK ** (-0.5)).astype(BF16)
        kn = (k * unit(k)).astype(BF16)
        dqn = jnp.zeros((T, DK), F32)
        dkn = jnp.zeros((T, DK), F32)
        for sub in range(2):
            n = 2 * key_head + sub
            head = 2 * heads * group + n
            cum_col = column(cum, head)
            within = decay_within(cum_col, as_row(cum_t, head), causal)
            d_out = do_ref[n]
            du_ref[n] = dot1(p_ref[n], d_out, TN)
            d_scores = (dot1(d_out, u_ref[n], NT) * within).astype(BF16)
            dqn += jnp.exp(cum_col) * dot1(d_out, s_ref[n]) + dot1(d_scores, kn)
            dkn += dot1(d_scores, qn, TN)
        dq = q_scale * DK ** (-0.5) * (
            dqn - q * (q_scale * q_scale) * jnp.sum(q * dqn, axis=-1, keepdims=True))
        dq_ref[:, lanes] = dq.astype(BF16)
        dk_ref[:, lanes] = dkn


def late_kernel(heads, k_ref, ld_ref, be_ref, t_ref, u_ref, s_ref, l_ref, dkn_ref, du_ref,
                dk_ref, dv_ref):
    group = pl.program_id(0)
    row, col = grid_index()
    strict = row > col
    cum = cumulative_decay(ld_ref[...], row, col)
    cum_t = cum.T
    beta = be_ref[...]
    for key_head in range(heads):
        lanes = slice(key_head * DK, (key_head + 1) * DK)
        k = k_ref[:, lanes].astype(F32)
        k_scale = unit(k)
        kn = (k * k_scale).astype(BF16)
        dkn = dkn_ref[:, lanes]
        for sub in range(2):
            n = 2 * key_head + sub
            head = 2 * heads * group + n
            cum_col = column(cum, head)
            rate = column(beta, head)
            within = decay_within(cum_col, as_row(cum_t, head), strict)
            fade = jnp.exp(cum_col[T - 1:, :] - cum_col)
            u, leaving = u_ref[n], l_ref[n]
            du = du_ref[n] + fade * dot1(kn, leaving, NT)
            dx = dot1(t_ref[n], du, TN)
            dv_ref[:, n * DV:(n + 1) * DV] = (rate * dx).astype(BF16)
            dx = dx.astype(BF16)
            d_inter = dot1(dx, u, NT) * within * (-rate)
            dkn += (dot1(d_inter + d_inter.T, kn) + fade * dot1(u, leaving)
                    - (rate * jnp.exp(cum_col)) * dot1(dx, s_ref[n]))
        dk = k_scale * (dkn - k * (k_scale * k_scale) * jnp.sum(k * dkn, axis=-1, keepdims=True))
        dk_ref[:, lanes] = dk.astype(BF16)


def early_local(q, k, ld, p, u, d_out, s, heads=2):
    nv = 2 * heads
    keys = flat_block(heads)
    return pl.pallas_call(
        functools.partial(early_kernel, heads),
        grid=(HK // heads,),
        in_specs=[keys, keys, WHOLE] + [head_block(nv)] * 4,
        out_specs=[keys, keys, head_block(nv)],
        out_shape=[jax.ShapeDtypeStruct((T, HK * DK), BF16),
                   jax.ShapeDtypeStruct((T, HK * DK), F32), per_head(F32)],
        compiler_params=PARAMS,
        cost_estimate=cost(6),
        name="early_local",
    )(q, k, ld, p, u, d_out, s)


def late_local(k, ld, be, t, u, s, l, dkn, du, heads=2):
    nv = 2 * heads
    keys = flat_block(heads)
    return pl.pallas_call(
        functools.partial(late_kernel, heads),
        grid=(HK // heads,),
        in_specs=[keys, WHOLE, WHOLE] + [head_block(nv)] * 4 + [keys, head_block(nv)],
        out_specs=[keys, flat_block(nv)],
        out_shape=[jax.ShapeDtypeStruct((T, HK * DK), BF16),
                   jax.ShapeDtypeStruct((T, VALUE_HEADS * DV), BF16)],
        compiler_params=PARAMS,
        cost_estimate=cost(8),
        name="late_local",
    )(k, ld, be, t, u, s, l, dkn, du)


def scale_kernel(lengths_ref, pairing_ref, ratio_ref, cot_ref, scaled_ref):
    own = lax.axis_index("fsdp")
    tokens = cot_ref.shape[0]
    weight = jnp.zeros((8, 128), F32)
    for pair in range(pairing_ref.shape[0] // 2):
        chosen, rejected = pairing_ref[2 * pair], pairing_ref[2 * pair + 1]
        ratio_c = jnp.full((8, 128), ratio_ref[chosen], F32)
        ratio_r = jnp.full((8, 128), ratio_ref[rejected], F32)
        up_c, up_r = jnp.exp(ratio_c), jnp.exp(ratio_r)
        margin = CHI_BETA * (up_c + ratio_c - up_r - ratio_r)
        pull = CHI_BETA / (1.0 + jnp.exp(margin))
        weight = weight + jnp.where(chosen == own, -pull * (up_c + 1.0), 0.0)
        weight = weight + jnp.where(rejected == own, pull * (up_r + 1.0), 0.0)
    position = lax.axis_index("ctx") * tokens + lax.broadcasted_iota(jnp.int32, (tokens, 1), 0)
    live = (position < lengths_ref[own]).astype(F32)
    factor = weight[0:1, 0:1] * live
    scaled_ref[...] = (cot_ref[...].astype(F32) * factor).astype(BF16)


def scale_local(lengths, pairing, ratio, cot):
    scalars = pl.BlockSpec(memory_space=pltpu.SMEM)
    return pl.pallas_call(
        scale_kernel,
        in_specs=[scalars] * 3 + [pl.BlockSpec(memory_space=pltpu.VMEM)],
        out_specs=pl.BlockSpec(memory_space=pltpu.VMEM),
        out_shape=jax.ShapeDtypeStruct(cot.shape, BF16),
        compiler_params=PARAMS,
        cost_estimate=cost(1),
        name="scale_local",
    )(lengths, pairing, ratio, cot)


def weight_kernel(place_ref, rows_ref, scaled_ref, keep_ref, send_ref, part_ref):
    across, along, core = place_ref[0], place_ref[1], place_ref[2]
    part_ref[...] = dot1(rows_ref[...], scaled_ref[...], TN).astype(BF16)
    for x in range(4):
        for y in range(4):
            slot = (x ^ across) * 4 + (y ^ along)
            first = (x * 4 + y) * 32
            keep_ref[slot] = part_ref[pl.ds(pl.multiple_of(first + core * 16, 16), 16), :]
            send_ref[slot] = part_ref[pl.ds(pl.multiple_of(first + 16 - core * 16, 16), 16), :]


def weight_local(place, rows, scaled, width=512):
    features = rows.shape[1]
    tokens, columns = scaled.shape
    out = pl.BlockSpec((16, 16, width), lambda i: (0, 0, i))
    shape = jax.ShapeDtypeStruct((16, 16, columns), BF16)
    return pl.pallas_call(
        weight_kernel,
        grid=(columns // width,),
        in_specs=[pl.BlockSpec(memory_space=pltpu.SMEM),
                  pl.BlockSpec((tokens, features), lambda i: (0, 0)),
                  pl.BlockSpec((tokens, width), lambda i: (0, i))],
        out_specs=[out, out],
        out_shape=[shape, shape],
        scratch_shapes=[pltpu.VMEM((features, width), BF16)],
        compiler_params=PARAMS,
        cost_estimate=cost(4),
        name="weight_local",
    )(place, rows, scaled)


def exchange(x, axis):
    return lax.all_to_all(x, axis, split_axis=0, concat_axis=0, tiled=True)


def cross(x, axis, distance):
    count = lax.axis_size(axis)
    return lax.ppermute(x, axis, [(i, i ^ distance) for i in range(count)])


def tie(*values):
    return lax.optimization_barrier(values)


def add_up(parts):
    return functools.reduce(lambda a, b: a + b, [part.astype(F32) for part in parts])


def body(query_vectors, key_vectors, value_vectors, output_gate, log_decay, write_rate,
         out_weight, cotangent, lengths, pairing, log_ratio):
    q, k, v, gate = query_vectors[0], key_vectors[0], value_vectors[0], output_gate[0]
    ld, be = log_decay[0], write_rate[0]
    tokens = q.shape[0]
    count = lax.axis_size("ctx")
    seqs = lax.axis_size("fsdp")
    features = out_weight.shape[0]
    me = lax.axis_index("fsdp").reshape(1)
    spot = lax.axis_index("ctx")
    place = jnp.stack([spot // 8, (spot // 2) % 4, spot % 2])

    scaled = scale_local(lengths, pairing, log_ratio, cotangent[0])
    with jax.named_scope("every_scaled"):
        others = [cross(scaled, "fsdp", s) for s in range(1, seqs)]
    ab, t, u0, kg = write_local(k, v, ld, be)
    with jax.named_scope("back_grad"):
        others = list(tie(ab, *others)[1:])
        every_scaled = jnp.concatenate([scaled] + others, axis=0)
        bg = lax.dot_general(every_scaled, out_weight, NT, preferred_element_type=F32)
        bg = bg.astype(BF16).reshape(seqs, tokens, features)
    ab = exchange(ab, "ctx")
    p, r, io = read_local(q, k, ld, u0, kg)
    ab, p, r, io, bg = tie(ab, p, r, io, bg)
    with jax.named_scope("back_grad"):
        bg = jnp.stack([bg[0]] + [cross(bg[s], "fsdp", s) for s in range(1, seqs)])
    entering = exchange(chain(chain_up_kernel, count, ab), "ctx").reshape(VALUE_HEADS, DV, DK)
    normed, gate_grad, d_out, u, g = gate_local(me, entering, gate, bg, io, u0, kg, r, seqs)
    with jax.named_scope("every_normed"):
        rows = jnp.concatenate(
            [normed[0]] + [cross(normed[s], "fsdp", s) for s in range(1, seqs)], axis=0)
    g = exchange(g.reshape(count, HALF, DK), "ctx")
    dq, dkn, du = early_local(q, k, ld, p, u, d_out, entering)
    g, dq, dkn, du = tie(g, dq, dkn, du)
    leaving = exchange(chain(chain_down_kernel, count, ab, g), "ctx").reshape(VALUE_HEADS, DV, DK)
    with jax.named_scope("weight_grad"):
        keep, send = weight_local(place, rows, every_scaled)
        both = add_up([keep, cross(send, "ctx", 1)]).astype(BF16).reshape(4, 4, 16, -1)
    with jax.named_scope("mixed_out"):
        mixed = lax.dot_general(rows, out_weight, NN, preferred_element_type=F32)
        mixed = mixed.astype(BF16).reshape(seqs, tokens, -1)
    leaving, both, mixed = tie(leaving, both, mixed)
    with jax.named_scope("weight_grad"):
        line = add_up([both[:, 0]] + [cross(both[:, s], "ctx", 2 * s) for s in range(1, 4)])
        line = line.astype(BF16)
        weight_grad = add_up([line[0]] + [cross(line[s], "ctx", 8 * s) for s in range(1, 4)])
    with jax.named_scope("mixed_out"):
        mixed = add_up([mixed[0]] + [cross(mixed[s], "fsdp", s) for s in range(1, seqs)])
        mixed = mixed.astype(BF16)
    dk, dv = late_local(k, ld, be, t, u, entering, leaving, dkn, du)
    return mixed[None], dq[None], dk[None], dv[None], gate_grad[None], weight_grad


def solution(mesh):
    tokens = P("fsdp", "ctx", None)
    return jax.shard_map(
        body,
        mesh=mesh,
        in_specs=(tokens,) * 6 + (P("fsdp", None), tokens, P(), P(), P()),
        out_specs=(tokens,) * 5 + (P(("fsdp", "ctx"), None),),
        check_vma=False,
    )
```

time: 313 us -> 194 us (0.62)
  waiting for transfers between devices: 127 us -> 50.3 us
  blocking collectives: 64 us -> 0 us
  starting transfers between devices: 4.33 us -> 55.6 us
  between operations: 14 us -> 0.82 us
  local copies, waits for them, and re-layouts: 19.7 us -> 8.89 us
  matrix products: 11.6 us -> 5.08 us
  other arithmetic: 7.69 us -> 10.9 us
    all_to_all x3 -> x0, blocking collectives: 64 us -> none  [exchange(): return lax.all_to_all(x, axis, split_axis=0, concat_axis=0, tiled=True)]
    all_gather x3 -> x0, waiting for transfers between devices: 61.6 us -> none  [the longest x1 33.6 us: body(): every_scaled = lax.all_gather(scaled, 'fsdp', axis=0, tiled=True)]
    reduce_scatter x2 -> x0, waiting for transfers between devices: 55.6 us -> none  [the longest x1 30.6 us: body(): mixed = lax.psum_scatter(mixed, 'fsdp', scatter_dimension=0, tiled=True)]
    ppermute x0 -> x19, waiting for transfers between devices: none -> 42.1 us  [cross(): return lax.ppermute(x, axis, [(i, i ^ distance) for i in range(count)])]
    ppermute x0 -> x19, starting transfers between devices: none -> 25.8 us  [cross(): return lax.ppermute(x, axis, [(i, i ^ distance) for i in range(count)])]
    all_to_all x1 -> x4, starting transfers between devices: 4.12 us -> 29.7 us  [exchange(): return lax.all_to_all(x, axis, split_axis=0, concat_axis=0, tiled=True)]
    unnamed x60 -> x24, local copies, waits for them, and re-layouts: 17.6 us -> 5.77 us
    dot_general x2 -> x1, matrix products: 7.98 us -> 2.6 us  [body(): mixed = lax.dot_general(rows, out_weight, NN, preferred_element_type=F32)]
  transfers between devices with their start and end apart: 6 -> 23, of which waited for: 5 -> 8; matrix products, arithmetic and copies ran while one was open for 2% -> 8% of each run, Pallas kernels for 18% -> 19%
where the time goes in v2:
time: 194 us; the launch traced here: 193 us
  Pallas kernels  61.8 us (32%)
  starting transfers between devices  55.6 us (29%)
  waiting for transfers between devices  50.3 us (26%)
  other arithmetic  10.9 us (6%)
  local copies, waits for them, and re-layouts  8.89 us (5%)
  matrix products  5.08 us (3%)
    ppermute x19, waiting for transfers between devices, cross(): return lax.ppermute(x, axis, [(i, i ^ distance) for i in range(count)])  42.1 us
    all_to_all x4, starting transfers between devices, exchange(): return lax.all_to_all(x, axis, split_axis=0, concat_axis=0, tiled=True)  29.7 us
    ppermute x19, starting transfers between devices, cross(): return lax.ppermute(x, axis, [(i, i ^ distance) for i in range(count)])  25.8 us
    pallas_call x1, Pallas kernels, write_local(): pl.pallas_call(functools.partial(write_kernel, heads), grid=(HK // heads,...  13 us
    pallas_call x2, Pallas kernels, chain(): pl.pallas_call(functools.partial(kernel, count), out_shape=jax.ShapeDtype...  12.5 us
    pallas_call x1, Pallas kernels, late_local(): pl.pallas_call(functools.partial(late_kernel, heads), grid=(HK // heads,)...  11.3 us
    all_to_all x4, waiting for transfers between devices, exchange(): return lax.all_to_all(x, axis, split_axis=0, concat_axis=0, tiled=True)  8.25 us
    pallas_call x1, Pallas kernels, early_local(): pl.pallas_call(functools.partial(early_kernel, heads), grid=(HK // heads,...  6.55 us
  transfers between devices with their start and end apart: 23, of which 8 were waited for; matrix products, arithmetic and copies ran while one was open for 8% of the time, Pallas kernels for 19%

profile of v2, /device:TPU:0, one launch (start us, length us, event | category | flops | bytes accessed | tf_op | source)
XLA Modules:
  0.0 193.3 jit_solution(14963702744398263676)
XLA Ops:
  0.6 0.0 copy-start
  0.6 1.6 copy.17
  2.2 1.4 copy.18
  3.6 13.0 %write_local.1 = (bf16[32,208,128]{2,1,0:T(8,128)(2,1)}, bf16[16,128,128]{2,1,0:T(8,128)(2,1)}, f32[16,128,128]{2,1,0:T(8,128)}, bf16[16,128,128]{2,1,0:T(8,128)(2,1)}) custom-call(bf16[128,1024]{1,0:T(8,128)(2,1)} %bitcast.95, bf16[128,2048]{1,0:T(8,128)(2,1)} %bitcast.90, f32[128,16]{1,0:T(8,128)} %bitcast.84, f32[128,16]{1,0:T(8,128)} %bitcast.88), custom_call_target="tpu_custom_call" | custom-call | flops 20000000000 | bytes 4194304 | tf_op jit(solution)/shard_map/write_local/pallas_call | solution.py:193
  16.7 7.5 %all-to-all-start = ((bf16[32,208,128]{2,1,0:T(8,128)(2,1)}), bf16[32,208,128]{2,1,0:T(8,128)(2,1)}, u32[]{:S(2)}, u32[]{:S(2)}) async-start(bf16[32,208,128]{2,1,0:T(8,128)(2,1)} %get-tuple-element.40), calls=%async_computation | async-start | bytes 3407872 | tf_op jit(solution)/shard_map/all_to_all | solution.py:462
  24.2 2.0 %scale_local.1 = bf16[128,2048]{1,0:T(8,128)(2,1)} custom-call(s32[4]{0:T(128)} %lengths_ref.1, s32[4]{0:T(128)} %pairing_ref.1, f32[4]{0:T(128)} %ratio_ref.1, bf16[128,2048]{1,0:T(8,128)(2,1)} %bitcast.91), custom_call_target="tpu_custom_call" | custom-call | flops 1000000000 | bytes 4194304 | tf_op jit(solution)/shard_map/scale_local/pallas_call | solution.py:419
  26.2 4.0 %collective-permute-start.2 = (bf16[128,2048]{1,0:T(8,128)(2,1)}, bf16[128,2048]{1,0:T(8,128)(2,1)S(1)}, u32[]{:S(2)}, u32[]{:S(2)}) collective-permute-start(bf16[128,2048]{1,0:T(8,128)(2,1)} %scale_local.1), channel_id=1, source_target_pairs={{0,96},{32,64},{64,32},{96,0},{1,97},{33,65},{65,33},{97,1},{2,98}... | collective-permute-start | bytes 1572872 | tf_op jit(solution)/shard_map/every_scaled/ppermute | solution.py:467
  30.2 0.0 collective-permute-start.1
  30.2 0.9 collective-permute-start
  31.1 5.0 %read_local.1 = (bf16[16,128,128]{2,1,0:T(8,128)(2,1)}, bf16[16,128,128]{2,1,0:T(8,128)(2,1)}, f32[16,128,128]{2,1,0:T(8,128)}) custom-call(bf16[128,1024]{1,0:T(8,128)(2,1)} %bitcast.93, bf16[128,1024]{1,0:T(8,128)(2,1)} %bitcast.96, f32[128,16]{1,0:T(8,128)} %bitcast.85, f32[16,128,128]{2,1,0:T(8,128)} %get-tuple-element.41.u0_ref, ...), custom_call_target="tpu_custom_call" | custom-call | flops 8000000000 | bytes 4194304 | tf_op jit(solution)/shard_map/read_local/pallas_call | solution.py:208
  36.0 17.9 %collective-permute-done.2 = bf16[128,2048]{1,0:T(8,128)(2,1)S(1)} collective-permute-done((bf16[128,2048]{1,0:T(8,128)(2,1)}, bf16[128,2048]{1,0:T(8,128)(2,1)S(1)}, u32[]{:S(2)}, u32[]{:S(2)}) %collective-permute-start.2) | collective-permute-done | bytes 524320 | tf_op jit(solution)/shard_map/every_scaled/ppermute | solution.py:467
  54.0 0.0 collective-permute-done.1
  54.0 0.8 copy-done.8
  54.8 0.0 collective-permute-done
  54.8 0.1 copy-done.6
  55.0 2.5 %convolution_convert_fusion.1 = bf16[512,512]{1,0:T(8,128)(2,1)S(1)} fusion(bf16[512,2048]{1,0:T(8,128)(2,1)S(1)} %copy-done, bf16[128,2048]{1,0:T(8,128)(2,1)S(1)} %collective-permute-done.2, bf16[128,2048]{1,0:T(8,128)(2,1)} %copy-done.8, bf16[128,2048]{1,0:T(8,128)(2,1)} %collective-permute-done, bf16[128,2048]{1,0:T(8,128)(2,1)S(1)} %copy-done.4), kind=kOutput, calls=%fused_computation.3 | convolution fusion | flops 1082392576 | bytes 4718592 | tf_op jit(solution)/shard_map/back_grad/dot_general | solution.py:497
  57.5 6.2 %chain.2 = bf16[32,64,128]{2,1,0:T(8,128)(2,1)} custom-call(bf16[32,208,128]{2,1,0:T(8,128)(2,1)} %all-to-all-done.ab_ref), custom_call_target="tpu_custom_call" | custom-call | flops 4000000000 | bytes 4194304 | tf_op jit(solution)/shard_map/chain/pallas_call | solution.py:247
  63.7 7.3 %all-to-all-start.1 = ((bf16[32,64,128]{2,1,0:T(8,128)(2,1)}), bf16[32,64,128]{2,1,0:T(8,128)(2,1)S(1)}, u32[]{:S(2)}, u32[]{:S(2)}) async-start(bf16[32,64,128]{2,1,0:T(8,128)(2,1)} %chain.2), calls=%async_computation.1 | async-start | bytes 1048576 | tf_op jit(solution)/shard_map/all_to_all | solution.py:462
  70.9 0.7 fusion.9
  71.6 2.9 %collective-permute-start.5 = (bf16[128,512]{1,0:T(8,128)(2,1)}, bf16[128,512]{1,0:T(8,128)(2,1)S(1)}, u32[]{:S(2)}, u32[]{:S(2)}) collective-permute-start(bf16[128,512]{1,0:T(8,128)(2,1)} %get-tuple-element.85), channel_id=1, source_target_pairs={{0,96},{32,64},{64,32},{96,0},{1,97},{33,65},{65,33},{97,1},{2,98}... | collective-permute-start | bytes 393224 | tf_op jit(solution)/shard_map/back_grad/ppermute | solution.py:467
  74.6 0.1 collective-permute-start.4
  74.6 1.1 collective-permute-start.3
  75.7 0.7 pad_add_fusion.place_ref
  76.4 4.5 %collective-permute-done.5 = bf16[128,512]{1,0:T(8,128)(2,1)S(1)} collective-permute-done((bf16[128,512]{1,0:T(8,128)(2,1)}, bf16[128,512]{1,0:T(8,128)(2,1)S(1)}, u32[]{:S(2)}, u32[]{:S(2)}) %collective-permute-start.5) | collective-permute-done | bytes 131104 | tf_op jit(solution)/shard_map/back_grad/ppermute | solution.py:467
  80.9 1.5 collective-permute-done.4
  82.4 0.9 pad_maximum_fusion.1.bg_ref
  83.3 0.8 copy-done.3
  84.1 6.5 %gate_local.1 = (bf16[4,128,512]{2,1,0:T(8,128)(2,1)}, bf16[128,2048]{1,0:T(8,128)(2,1)}, bf16[16,128,128]{2,1,0:T(8,128)(2,1)}, bf16[16,128,128]{2,1,0:T(8,128)(2,1)}, bf16[16,128,128]{2,1,0:T(8,128)(2,1)}) custom-call(s32[1]{0:T(128)} %bitcast.7.me_ref, bf16[16,128,128]{2,1,0:T(8,128)(2,1)} %bitcast.77, bf16[128,2048]{1,0:T(8,128)(2,1)} %bitcast.92, ...), custom_call_target="tpu_custom_call" | custom-call | flops 5000000000 | bytes 4194304 | tf_op jit(solution)/shard_map/gate_local/pallas_call | solution.py:285
  90.6 1.1 slice_bitcast_fusion.10
  91.7 2.5 %collective-permute-start.8 = (bf16[128,512]{1,0:T(8,128)(2,1)S(1)}, bf16[128,512]{1,0:T(8,128)(2,1)S(1)}, u32[]{:S(2)}, u32[]{:S(2)}) collective-permute-start(bf16[128,512]{1,0:T(8,128)(2,1)S(1)} %get-tuple-element.81), channel_id=1, source_target_pairs={{0,96},{32,64},{64,32},{96,0},{1,97},{33,65},{65,33},{97,1},{2,98}... | collective-permute-start | bytes 393224 | tf_op jit(solution)/shard_map/every_normed/ppermute | solution.py:467
  94.2 0.3 collective-permute-start.7
  94.6 1.4 collective-permute-start.6
  95.9 2.7 %pad_maximum_fusion.scaled_ref = bf16[512,2048]{1,0:T(8,128)(2,1)} fusion(bf16[128,2048]{1,0:T(8,128)(2,1)S(1)} %copy-done.7, bf16[128,2048]{1,0:T(8,128)(2,1)} %copy-done.8, bf16[128,2048]{1,0:T(8,128)(2,1)} %collective-permute-done, bf16[128,2048]{1,0:T(8,128)(2,1)S(1)} %copy-done.5), kind=kLoop, calls=%fused_computation.1 | loop fusion | flops 8388608 | bytes 4194304 | tf_op jit(solution)/shard_map/back_grad/concatenate | solution.py:496
  98.7 7.5 %all-to-all-start.2 = ((bf16[32,64,128]{2,1,0:T(8,128)(2,1)}), bf16[32,64,128]{2,1,0:T(8,128)(2,1)}, u32[]{:S(2)}, u32[]{:S(2)}) async-start(bf16[32,64,128]{2,1,0:T(8,128)(2,1)} %bitcast.16), calls=%async_computation.2 | async-start | bytes 1048576 | tf_op jit(solution)/shard_map/all_to_all | solution.py:462
  106.2 0.0 copy-start.9
  106.3 0.8 pad_maximum_fusion.2.rows_ref
  107.1 4.9 %weight_local.1 = (bf16[16,16,2048]{2,1,0:T(8,128)(2,1)}, bf16[16,16,2048]{2,1,0:T(8,128)(2,1)}) custom-call(s32[3]{0:T(128)} %pad_add_fusion.place_ref, bf16[512,512]{1,0:T(8,128)(2,1)} %pad_maximum_fusion.2.rows_ref, bf16[512,2048]{1,0:T(8,128)(2,1)} %pad_maximum_fusion.scaled_ref), custom_call_target="tpu_custom_call" | custom-call | flops 4000000000 | bytes 4194304 | tf_op jit(solution)/shard_map/weight_grad/weight_local/pallas_call | solution.py:446
  112.0 0.2 collective-permute-start.9
  112.3 6.6 %early_local.1 = (bf16[128,1024]{1,0:T(8,128)(2,1)}, f32[128,1024]{1,0:T(8,128)}, f32[16,128,128]{2,1,0:T(8,128)}) custom-call(bf16[128,1024]{1,0:T(8,128)(2,1)} %bitcast.94, bf16[128,1024]{1,0:T(8,128)(2,1)} %bitcast.97, f32[128,16]{1,0:T(8,128)} %bitcast.86, bf16[16,128,128]{2,1,0:T(8,128)(2,1)} %get-tuple-element.54.p_ref, ...), custom_call_target="tpu_custom_call" | custom-call | flops 6000000000 | bytes 4194304 | tf_op jit(solution)/shard_map/early_local/pallas_call | solution.py:369
  118.8 2.6 %convolution_convert_fusion = bf16[512,2048]{1,0:T(8,128)(2,1)} fusion(bf16[512,2048]{1,0:T(8,128)(2,1)S(1)} %copy-done, bf16[128,512]{1,0:T(8,128)(2,1)S(1)} %collective-permute-done.8, bf16[128,512]{1,0:T(8,128)(2,1)S(1)} %collective-permute-done.7, bf16[128,512]{1,0:T(8,128)(2,1)S(1)} %copy-done.10, bf16[128,512]{1,0:T(8,128)(2,1)S(1)} %get-tuple-element.80), kind=kOutput, calls=%fused_computation | convolution fusion | flops 1076887552 | bytes 4718592 | tf_op jit(solution)/shard_map/mixed_out/dot_general | solution.py:517
  121.4 6.3 %chain.3 = bf16[32,64,128]{2,1,0:T(8,128)(2,1)} custom-call(bf16[32,208,128]{2,1,0:T(8,128)(2,1)} %all-to-all-done.ab_ref, bf16[32,64,128]{2,1,0:T(8,128)(2,1)} %all-to-all-done.2.g_ref), custom_call_target="tpu_custom_call" | custom-call | flops 4000000000 | bytes 4194304 | tf_op jit(solution)/shard_map/chain/pallas_call | solution.py:247
  127.8 7.4 %all-to-all-start.3 = ((bf16[32,64,128]{2,1,0:T(8,128)(2,1)}), bf16[32,64,128]{2,1,0:T(8,128)(2,1)}, u32[]{:S(2)}, u32[]{:S(2)}) async-start(bf16[32,64,128]{2,1,0:T(8,128)(2,1)} %chain.3), calls=%async_computation.3 | async-start | bytes 1048576 | tf_op jit(solution)/shard_map/all_to_all | solution.py:462
  135.2 1.0 copy-done.2
  136.2 1.9 add_convert_fusion
  138.1 8.2 %all-to-all-done.3 = bf16[32,64,128]{2,1,0:T(8,128)(2,1)} async-done(((bf16[32,64,128]{2,1,0:T(8,128)(2,1)}), bf16[32,64,128]{2,1,0:T(8,128)(2,1)}, u32[]{:S(2)}, u32[]{:S(2)}) %all-to-all-start.3) | async-done | bytes 524320 | tf_op jit(solution)/shard_map/all_to_all | solution.py:462
  146.3 0.1 slice_bitcast_fusion.5
  146.4 0.8 collective-permute-start.13
  147.2 1.6 collective-permute-start.15
  148.8 1.7 collective-permute-start.14
  150.6 5.1 %collective-permute-done.13 = bf16[4,16,2048]{2,1,0:T(8,128)(2,1)S(1)} collective-permute-done((bf16[4,16,2048]{2,1,0:T(8,128)(2,1)S(1)}, bf16[4,16,2048]{2,1,0:T(8,128)(2,1)S(1)}, u32[]{:S(2)}, u32[]{:S(2)}) %collective-permute-start.13) | collective-permute-done | bytes 262176 | tf_op jit(solution)/shard_map/weight_grad/ppermute | solution.py:467
  155.6 6.7 %collective-permute-done.15 = bf16[4,16,2048]{2,1,0:T(8,128)(2,1)S(1)} collective-permute-done((bf16[4,16,2048]{2,1,0:T(8,128)(2,1)S(1)}, bf16[4,16,2048]{2,1,0:T(8,128)(2,1)S(1)}, u32[]{:S(2)}, u32[]{:S(2)}) %collective-permute-start.15) | collective-permute-done | bytes 262176 | tf_op jit(solution)/shard_map/weight_grad/ppermute | solution.py:467
  162.3 0.1 fusion.6
  162.5 0.9 collective-permute-start.16
  163.4 1.2 slice_bitcast_fusion.2
  164.6 0.5 collective-permute-start.10
  165.1 1.9 collective-permute-start.12
  167.1 1.6 collective-permute-start.11
  168.7 1.4 collective-permute-start.18
  170.1 1.9 collective-permute-start.17
  172.0 11.3 %late_local.1 = (bf16[128,1024]{1,0:T(8,128)(2,1)}, bf16[128,2048]{1,0:T(8,128)(2,1)}) custom-call(bf16[128,1024]{1,0:T(8,128)(2,1)} %bitcast.98, f32[128,16]{1,0:T(8,128)} %bitcast.87, f32[128,16]{1,0:T(8,128)} %bitcast.89, bf16[16,128,128]{2,1,0:T(8,128)(2,1)} %get-tuple-element.66.t_ref, bf16[16,128,128]{2,1,0:T(8,128)(2,1)} %get-tuple-element.55.u_ref, ...), custom_call_target="tpu_custom_call" | custom-call | flops 8000000000 | bytes 4194304 | tf_op jit(solution)/shard_map/late_local/pallas_call | solution.py:385
  183.3 1.6 fusion.8
  184.9 4.5 %collective-permute-done.12 = bf16[128,2048]{1,0:T(8,128)(2,1)S(1)} collective-permute-done((bf16[128,2048]{1,0:T(8,128)(2,1)}, bf16[128,2048]{1,0:T(8,128)(2,1)S(1)}, u32[]{:S(2)}, u32[]{:S(2)}) %collective-permute-start.12) | collective-permute-done | bytes 524320 | tf_op jit(solution)/shard_map/mixed_out/ppermute | solution.py:467
  189.4 1.8 collective-permute-done.11
  191.2 2.2 %fusion.3 = bf16[1,128,2048]{2,1,0:T(8,128)(2,1)} fusion(bf16[128,2048]{1,0:T(8,128)(2,1)S(1)} %collective-permute-done.12, bf16[128,2048]{1,0:T(8,128)(2,1)S(1)} %collective-permute-done.11, bf16[128,2048]{1,0:T(8,128)(2,1)S(1)} %collective-permute-done.10, bf16[4,128,2048]{2,1,0:T(8,128)(2,1)} %bitcast.75), kind=kLoop, calls=%fused_computation.8 | loop fusion | flops 2097152 | bytes 2621440 | tf_op jit(solution)/shard_map/broadcast_in_dim | solution.py:528
  (30 shorter events, 0.1 us)
Async XLA Ops:
  0.6 54.3 %copy-start = (bf16[512,2048]{1,0:T(8,128)(2,1)S(1)}, bf16[512,2048]{1,0:T(8,128)(2,1)}, u32[]{:S(2)}) copy-start(bf16[512,2048]{1,0:T(8,128)(2,1)} %param.17) | copy-start | bytes 6291460
  16.7 40.8 %all-to-all-start = ((bf16[32,208,128]{2,1,0:T(8,128)(2,1)}), bf16[32,208,128]{2,1,0:T(8,128)(2,1)}, u32[]{:S(2)}, u32[]{:S(2)}) async-start(bf16[32,208,128]{2,1,0:T(8,128)(2,1)} %get-tuple-element.40), calls=%async_computation | async-start | bytes 3407872 | tf_op jit(solution)/shard_map/all_to_all | solution.py:462
  26.2 27.8 %collective-permute-start.2 = (bf16[128,2048]{1,0:T(8,128)(2,1)}, bf16[128,2048]{1,0:T(8,128)(2,1)S(1)}, u32[]{:S(2)}, u32[]{:S(2)}) collective-permute-start(bf16[128,2048]{1,0:T(8,128)(2,1)} %scale_local.1), channel_id=1, source_target_pairs={{0,96},{32,64},{64,32},{96,0},{1,97},{33,65},{65,33},{97,1},{2,98}... | collective-permute-start | bytes 1572872 | tf_op jit(solution)/shard_map/every_scaled/ppermute | solution.py:467
  30.2 23.7 %collective-permute-start.1 = (bf16[128,2048]{1,0:T(8,128)(2,1)}, bf16[128,2048]{1,0:T(8,128)(2,1)S(1)}, u32[]{:S(2)}, u32[]{:S(2)}) collective-permute-start(bf16[128,2048]{1,0:T(8,128)(2,1)} %scale_local.1), channel_id=1, source_target_pairs={{0,64},{32,96},{64,0},{96,32},{1,65},{33,97},{65,1},{97,33},{2,66}... | collective-permute-start | bytes 1572872 | tf_op jit(solution)/shard_map/every_scaled/ppermute | solution.py:467
  30.2 24.6 %collective-permute-start = (bf16[128,2048]{1,0:T(8,128)(2,1)}, bf16[128,2048]{1,0:T(8,128)(2,1)}, u32[]{:S(2)}, u32[]{:S(2)}) collective-permute-start(bf16[128,2048]{1,0:T(8,128)(2,1)} %scale_local.1), channel_id=1, source_target_pairs={{0,32},{32,0},{64,96},{96,64},{1,33},{33,1},{65,97},{97,65},{2,34}... | collective-permute-start | bytes 1572872 | tf_op jit(solution)/shard_map/every_scaled/ppermute | solution.py:467
  31.1 23.9 %copy-start.4 = (bf16[128,2048]{1,0:T(8,128)(2,1)S(1)}, bf16[128,2048]{1,0:T(8,128)(2,1)}, u32[]{:S(2)}) copy-start(bf16[128,2048]{1,0:T(8,128)(2,1)} %scale_local.1) | copy-start | bytes 1572868
  54.0 1.0 copy-start.6
  54.0 0.8 copy-start.8
  63.7 19.7 %all-to-all-start.1 = ((bf16[32,64,128]{2,1,0:T(8,128)(2,1)}), bf16[32,64,128]{2,1,0:T(8,128)(2,1)S(1)}, u32[]{:S(2)}, u32[]{:S(2)}) async-start(bf16[32,64,128]{2,1,0:T(8,128)(2,1)} %chain.2), calls=%async_computation.1 | async-start | bytes 1048576 | tf_op jit(solution)/shard_map/all_to_all | solution.py:462
  71.6 9.3 %collective-permute-start.5 = (bf16[128,512]{1,0:T(8,128)(2,1)}, bf16[128,512]{1,0:T(8,128)(2,1)S(1)}, u32[]{:S(2)}, u32[]{:S(2)}) collective-permute-start(bf16[128,512]{1,0:T(8,128)(2,1)} %get-tuple-element.85), channel_id=1, source_target_pairs={{0,96},{32,64},{64,32},{96,0},{1,97},{33,65},{65,33},{97,1},{2,98}... | collective-permute-start | bytes 393224 | tf_op jit(solution)/shard_map/back_grad/ppermute | solution.py:467
  74.6 7.9 %collective-permute-start.4 = (bf16[128,512]{1,0:T(8,128)(2,1)S(1)}, bf16[128,512]{1,0:T(8,128)(2,1)S(1)}, u32[]{:S(2)}, u32[]{:S(2)}) collective-permute-start(bf16[128,512]{1,0:T(8,128)(2,1)S(1)} %get-tuple-element.86), channel_id=1, source_target_pairs={{0,64},{32,96},{64,0},{96,32},{1,65},{33,97},{65,1},{97,33},{2,66}... | collective-permute-start | bytes 393224 | tf_op jit(solution)/shard_map/back_grad/ppermute | solution.py:467
  74.6 7.8 %collective-permute-start.3 = (bf16[128,512]{1,0:T(8,128)(2,1)S(1)}, bf16[128,512]{1,0:T(8,128)(2,1)S(1)}, u32[]{:S(2)}, u32[]{:S(2)}) collective-permute-start(bf16[128,512]{1,0:T(8,128)(2,1)S(1)} %get-tuple-element.87), channel_id=1, source_target_pairs={{0,32},{32,0},{64,96},{96,64},{1,33},{33,1},{65,97},{97,65},{2,34}... | collective-permute-start | bytes 393224 | tf_op jit(solution)/shard_map/back_grad/ppermute | solution.py:467
  83.3 0.8 copy-start.3
  84.1 11.8 %copy-start.5 = (bf16[128,2048]{1,0:T(8,128)(2,1)S(1)}, bf16[128,2048]{1,0:T(8,128)(2,1)}, u32[]{:S(2)}) copy-start(bf16[128,2048]{1,0:T(8,128)(2,1)} %scale_local.1) | copy-start | bytes 1572868
  84.1 11.8 %copy-start.7 = (bf16[128,2048]{1,0:T(8,128)(2,1)S(1)}, bf16[128,2048]{1,0:T(8,128)(2,1)}, u32[]{:S(2)}) copy-start(bf16[128,2048]{1,0:T(8,128)(2,1)} %copy-done.6) | copy-start | bytes 1572868
  91.7 14.5 %collective-permute-start.8 = (bf16[128,512]{1,0:T(8,128)(2,1)S(1)}, bf16[128,512]{1,0:T(8,128)(2,1)S(1)}, u32[]{:S(2)}, u32[]{:S(2)}) collective-permute-start(bf16[128,512]{1,0:T(8,128)(2,1)S(1)} %get-tuple-element.81), channel_id=1, source_target_pairs={{0,96},{32,64},{64,32},{96,0},{1,97},{33,65},{65,33},{97,1},{2,98}... | collective-permute-start | bytes 393224 | tf_op jit(solution)/shard_map/every_normed/ppermute | solution.py:467
  94.2 12.0 %collective-permute-start.7 = (bf16[128,512]{1,0:T(8,128)(2,1)S(1)}, bf16[128,512]{1,0:T(8,128)(2,1)S(1)}, u32[]{:S(2)}, u32[]{:S(2)}) collective-permute-start(bf16[128,512]{1,0:T(8,128)(2,1)S(1)} %get-tuple-element.82), channel_id=1, source_target_pairs={{0,64},{32,96},{64,0},{96,32},{1,65},{33,97},{65,1},{97,33},{2,66}... | collective-permute-start | bytes 393224 | tf_op jit(solution)/shard_map/every_normed/ppermute | solution.py:467
  94.6 11.7 %collective-permute-start.6 = (bf16[128,512]{1,0:T(8,128)(2,1)S(1)}, bf16[128,512]{1,0:T(8,128)(2,1)S(1)}, u32[]{:S(2)}, u32[]{:S(2)}) collective-permute-start(bf16[128,512]{1,0:T(8,128)(2,1)S(1)} %get-tuple-element.83), channel_id=1, source_target_pairs={{0,32},{32,0},{64,96},{96,64},{1,33},{33,1},{65,97},{97,65},{2,34}... | collective-permute-start | bytes 393224 | tf_op jit(solution)/shard_map/every_normed/ppermute | solution.py:467
  98.7 22.8 %all-to-all-start.2 = ((bf16[32,64,128]{2,1,0:T(8,128)(2,1)}), bf16[32,64,128]{2,1,0:T(8,128)(2,1)}, u32[]{:S(2)}, u32[]{:S(2)}) async-start(bf16[32,64,128]{2,1,0:T(8,128)(2,1)} %bitcast.16), calls=%async_computation.2 | async-start | bytes 1048576 | tf_op jit(solution)/shard_map/all_to_all | solution.py:462
  106.2 5.8 %copy-start.9 = (bf16[128,512]{1,0:T(8,128)(2,1)}, bf16[128,512]{1,0:T(8,128)(2,1)S(1)}, u32[]{:S(2)}) copy-start(bf16[128,512]{1,0:T(8,128)(2,1)S(1)} %collective-permute-done.6) | copy-start | bytes 393220
  112.0 23.1 %collective-permute-start.9 = (bf16[16,16,2048]{2,1,0:T(8,128)(2,1)}, bf16[16,16,2048]{2,1,0:T(8,128)(2,1)S(1)}, u32[]{:S(2)}, u32[]{:S(2)}) collective-permute-start(bf16[16,16,2048]{2,1,0:T(8,128)(2,1)} %get-tuple-element.63), channel_id=1, source_target_pairs={{0,1},{1,0},{2,3},{3,2},{4,5},{5,4},{6,7},{7,6},{8,9},{9,8},{10,11... | collective-permute-start | bytes 3145736 | tf_op jit(solution)/shard_map/weight_grad/ppermute | solution.py:467
  112.3 6.6 %copy-start.10 = (bf16[128,512]{1,0:T(8,128)(2,1)S(1)}, bf16[128,512]{1,0:T(8,128)(2,1)}, u32[]{:S(2)}) copy-start(bf16[128,512]{1,0:T(8,128)(2,1)} %copy-done.9) | copy-start | bytes 393220
  127.8 18.6 %all-to-all-start.3 = ((bf16[32,64,128]{2,1,0:T(8,128)(2,1)}), bf16[32,64,128]{2,1,0:T(8,128)(2,1)}, u32[]{:S(2)}, u32[]{:S(2)}) async-start(bf16[32,64,128]{2,1,0:T(8,128)(2,1)} %chain.3), calls=%async_computation.3 | async-start | bytes 1048576 | tf_op jit(solution)/shard_map/all_to_all | solution.py:462
  135.2 1.0 copy-start.2
  146.3 17.1 %copy-start.1 = (bf16[512,2048]{1,0:T(8,128)(2,1)S(1)}, bf16[512,2048]{1,0:T(8,128)(2,1)}, u32[]{:S(2)}) copy-start(bf16[512,2048]{1,0:T(8,128)(2,1)} %convolution_convert_fusion) | copy-start | bytes 6291460
  146.4 9.3 %collective-permute-start.13 = (bf16[4,16,2048]{2,1,0:T(8,128)(2,1)S(1)}, bf16[4,16,2048]{2,1,0:T(8,128)(2,1)S(1)}, u32[]{:S(2)}, u32[]{:S(2)}) collective-permute-start(bf16[4,16,2048]{2,1,0:T(8,128)(2,1)S(1)} %get-tuple-element.77), channel_id=1, source_target_pairs={{0,2},{1,3},{2,0},{3,1},{4,6},{5,7},{6,4},{7,5},{8,10},{9,11},{10,... | collective-permute-start | bytes 786440 | tf_op jit(solution)/shard_map/weight_grad/ppermute | solution.py:467
  147.2 15.1 %collective-permute-start.15 = (bf16[4,16,2048]{2,1,0:T(8,128)(2,1)S(1)}, bf16[4,16,2048]{2,1,0:T(8,128)(2,1)S(1)}, u32[]{:S(2)}, u32[]{:S(2)}) collective-permute-start(bf16[4,16,2048]{2,1,0:T(8,128)(2,1)S(1)} %get-tuple-element.78), channel_id=1, source_target_pairs={{0,6},{1,7},{2,4},{3,5},{4,2},{5,3},{6,0},{7,1},{8,14},{9,15},{10,... | collective-permute-start | bytes 786440 | tf_op jit(solution)/shard_map/weight_grad/ppermute | solution.py:467
  148.8 13.5 %collective-permute-start.14 = (bf16[4,16,2048]{2,1,0:T(8,128)(2,1)S(1)}, bf16[4,16,2048]{2,1,0:T(8,128)(2,1)S(1)}, u32[]{:S(2)}, u32[]{:S(2)}) collective-permute-start(bf16[4,16,2048]{2,1,0:T(8,128)(2,1)S(1)} %get-tuple-element.79), channel_id=1, source_target_pairs={{0,4},{1,5},{2,6},{3,7},{4,0},{5,1},{6,2},{7,3},{8,12},{9,13},{10,... | collective-permute-start | bytes 786440 | tf_op jit(solution)/shard_map/weight_grad/ppermute | solution.py:467
  162.5 7.6 %collective-permute-start.16 = (bf16[16,2048]{1,0:T(8,128)(2,1)S(1)}, bf16[16,2048]{1,0:T(8,128)(2,1)S(1)}, u32[]{:S(2)}, u32[]{:S(2)}) collective-permute-start(bf16[16,2048]{1,0:T(8,128)(2,1)S(1)} %get-tuple-element.88), channel_id=1, source_target_pairs={{0,8},{1,9},{2,10},{3,11},{4,12},{5,13},{6,14},{7,15},{8,0},{9,1},... | collective-permute-start | bytes 196616 | tf_op jit(solution)/shard_map/weight_grad/ppermute | solution.py:467
  164.6 20.3 %collective-permute-start.10 = (bf16[128,2048]{1,0:T(8,128)(2,1)}, bf16[128,2048]{1,0:T(8,128)(2,1)S(1)}, u32[]{:S(2)}, u32[]{:S(2)}) collective-permute-start(bf16[128,2048]{1,0:T(8,128)(2,1)} %get-tuple-element.74), channel_id=1, source_target_pairs={{0,32},{32,0},{64,96},{96,64},{1,33},{33,1},{65,97},{97,65},{2,34}... | collective-permute-start | bytes 1572872 | tf_op jit(solution)/shard_map/mixed_out/ppermute | solution.py:467
  165.1 24.3 %collective-permute-start.12 = (bf16[128,2048]{1,0:T(8,128)(2,1)}, bf16[128,2048]{1,0:T(8,128)(2,1)S(1)}, u32[]{:S(2)}, u32[]{:S(2)}) collective-permute-start(bf16[128,2048]{1,0:T(8,128)(2,1)} %get-tuple-element.75), channel_id=1, source_target_pairs={{0,96},{32,64},{64,32},{96,0},{1,97},{33,65},{65,33},{97,1},{2,98}... | collective-permute-start | bytes 1572872 | tf_op jit(solution)/shard_map/mixed_out/ppermute | solution.py:467
  167.1 24.1 %collective-permute-start.11 = (bf16[128,2048]{1,0:T(8,128)(2,1)}, bf16[128,2048]{1,0:T(8,128)(2,1)S(1)}, u32[]{:S(2)}, u32[]{:S(2)}) collective-permute-start(bf16[128,2048]{1,0:T(8,128)(2,1)} %get-tuple-element.76), channel_id=1, source_target_pairs={{0,64},{32,96},{64,0},{96,32},{1,65},{33,97},{65,1},{97,33},{2,66}... | collective-permute-start | bytes 1572872 | tf_op jit(solution)/shard_map/mixed_out/ppermute | solution.py:467
  168.7 14.6 %collective-permute-start.18 = (bf16[16,2048]{1,0:T(8,128)(2,1)S(1)}, bf16[16,2048]{1,0:T(8,128)(2,1)}, u32[]{:S(2)}, u32[]{:S(2)}) collective-permute-start(bf16[16,2048]{1,0:T(8,128)(2,1)S(1)} %get-tuple-element.89), channel_id=1, source_target_pairs={{0,24},{1,25},{2,26},{3,27},{4,28},{5,29},{6,30},{7,31},{8,16},{9,... | collective-permute-start | bytes 196616 | tf_op jit(solution)/shard_map/weight_grad/ppermute | solution.py:467
  170.1 13.2 %collective-permute-start.17 = (bf16[16,2048]{1,0:T(8,128)(2,1)S(1)}, bf16[16,2048]{1,0:T(8,128)(2,1)}, u32[]{:S(2)}, u32[]{:S(2)}) collective-permute-start(bf16[16,2048]{1,0:T(8,128)(2,1)S(1)} %get-tuple-element.90), channel_id=1, source_target_pairs={{0,16},{1,17},{2,18},{3,19},{4,20},{5,21},{6,22},{7,23},{8,24},{9,... | collective-permute-start | bytes 196616 | tf_op jit(solution)/shard_map/weight_grad/ppermute | solution.py:467

commit v3 on v2

v3 whole, which is shorter than its diff:
```python
import functools

import jax
import jax.numpy as jnp
from jax import lax
from jax.experimental import pallas as pl
from jax.experimental.pallas import tpu as pltpu
from jax.sharding import PartitionSpec as P

VALUE_HEADS = 16
HK = 8
DK = 128
DV = 128
T = 128
HALF = 64
TAIL = 16
CHI_BETA = 0.5
NORM_EPS = 1e-06
F32 = jnp.float32
BF16 = jnp.bfloat16

NN = (((1,), (0,)), ((), ()))
NT = (((1,), (1,)), ((), ()))
TN = (((0,), (0,)), ((), ()))


def dot1(a, b, dims=NN):
    return lax.dot_general(a.astype(BF16), b.astype(BF16), dims, preferred_element_type=F32)


def split(a):
    high = a.astype(BF16)
    return high, (a - high.astype(F32)).astype(BF16)


def dot3(a, b, dims=NN):
    a_high, a_low = split(a)
    b_high, b_low = split(b)
    return dot1(a_high, b_high, dims) + (dot1(a_low, b_high, dims) + dot1(a_high, b_low, dims))


def grid_index():
    row = lax.broadcasted_iota(jnp.int32, (T, T), 0)
    col = lax.broadcasted_iota(jnp.int32, (T, T), 1)
    return row, col


def unit(x):
    return lax.rsqrt(jnp.sum(x * x, axis=-1, keepdims=True) + NORM_EPS)


def dot_exact_left(a, b):
    first = a.astype(BF16)
    rest = a - first.astype(F32)
    second = rest.astype(BF16)
    third = (rest - second.astype(F32)).astype(BF16)
    return dot1(first, b) + (dot1(second, b) + dot1(third, b))


def in_order(sc_ref, own, other):
    is_first = sc_ref[0] == 0
    return jnp.where(is_first, own, other), jnp.where(is_first, other, own)


def decay_tables(sc_ref, own_ref, other_ref, row, col):
    upper = (row <= col).astype(BF16)
    tables = []
    for table in in_order(sc_ref, own_ref[...], other_ref[...]):
        cum_t = dot_exact_left(table[:VALUE_HEADS], upper)
        tables.append((cum_t, cum_t.T, table[VALUE_HEADS:].T))
    return tables


def column(table, head):
    lane = lax.broadcasted_iota(jnp.int32, table.shape, 1)
    return jnp.sum(jnp.where(lane == head, table, 0.0), axis=1, keepdims=True)


def as_row(table_t, head):
    sub = lax.broadcasted_iota(jnp.int32, table_t.shape, 0)
    return jnp.sum(jnp.where(sub == head, table_t, 0.0), axis=0, keepdims=True)


def decay_within(cum_col, cum_row, mask):
    return jnp.where(mask, jnp.exp(jnp.where(mask, cum_col - cum_row, 0.0)), 0.0)


def invert(couplings, row, col):
    eye = (row == col).astype(F32)
    pairs = (row >> 1) == (col >> 1)
    inverses = [eye - jnp.where(pairs, c, 0.0) for c in couplings]
    for level in range(1, 7):
        mask = ((row >> (level + 1)) == (col >> (level + 1))) & ((row >> level) != (col >> level))
        offs = [jnp.where(mask, c, 0.0).astype(BF16) for c in couplings]
        low = [i.astype(BF16) for i in inverses]
        inner = [dot1(o, i) for o, i in zip(offs, low)]
        inverses = [x - dot1(i, n) for x, i, n in zip(inverses, low, inner)]
    residuals = [eye - i - dot3(c, i) for c, i in zip(couplings, inverses)]
    return [i + dot1(i, r) for i, r in zip(inverses, residuals)]


def total_rows(total):
    wide = jnp.broadcast_to(total, (TAIL, DK))
    high, low = split(wide)
    low2 = (wide - high.astype(F32) - low.astype(F32)).astype(BF16)
    sub_row = lax.broadcasted_iota(jnp.int32, (TAIL, DK), 0)
    tail = jnp.where(sub_row == 0, high.astype(F32),
                     jnp.where(sub_row == 1, low.astype(F32),
                               jnp.where(sub_row == 2, low2.astype(F32), 0.0)))
    return tail.astype(BF16)


UNITS = [(sub, block) for sub in range(2) for block in range(2)]


def first_head(sc_ref):
    return (VALUE_HEADS // 2) * sc_ref[0] + 2 * pl.program_id(0)


def write_kernel(sc_ref, ko_ref, vo_ref, lo_ref, kx_ref, vx_ref, lx_ref,
                 ab_ref, t_ref, u0_ref, kg_ref, a_ref, b_ref):
    row, col = grid_index()
    causal, strict = row >= col, row > col
    tables = decay_tables(sc_ref, lo_ref, lx_ref, row, col)
    ks = in_order(sc_ref, ko_ref[...].astype(F32), kx_ref[...].astype(F32))
    vs = in_order(sc_ref, vo_ref[...].astype(F32), vx_ref[...].astype(F32))
    kns = [k * unit(k) for k in ks]
    kks = [dot3(kn, kn, NT) for kn in kns]
    cols, rates, couplings = [], [], []
    for sub, block in UNITS:
        cum_t, cum, beta = tables[block]
        h = first_head(sc_ref) + sub
        cum_col, rate = column(cum, h), column(beta, h)
        within = decay_within(cum_col, as_row(cum_t, h), causal)
        couplings.append(jnp.where(strict, kks[block] * within, 0.0) * rate)
        cols.append(cum_col)
        rates.append(rate)
    inverses = [i.astype(BF16) for i in invert(couplings, row, col)]
    u0s, kgs, transits, writtens, totals = [], [], [], [], []
    for n, (sub, block) in enumerate(UNITS):
        u0s.append(dot1(inverses[n], rates[n] * vs[block][:, sub * DV:(sub + 1) * DV]))
        kgs.append(dot1(inverses[n], (rates[n] * jnp.exp(cols[n])) * kns[block]).astype(BF16))
    for n, (sub, block) in enumerate(UNITS):
        total = cols[n][T - 1:, :]
        carried = (jnp.exp(total - cols[n]) * kns[block]).astype(BF16)
        transits.append(dot1(kgs[n], carried, TN))
        writtens.append(dot1(u0s[n], carried, TN))
        totals.append(total)
        t_ref[n] = inverses[n]
        u0_ref[n] = u0s[n].astype(BF16)
        kg_ref[n] = kgs[n]
        a_ref[n] = transits[n].astype(BF16)
    for sub in range(2):
        f, s = 2 * sub, 2 * sub + 1
        e_f, e_s = jnp.exp(totals[f]), jnp.exp(totals[s])
        stacked = jnp.concatenate([transits[f], writtens[f]], axis=0)
        moved = dot3(stacked, transits[s])
        transit = (e_f * transits[s] + e_s * transits[f] - moved[:DK]).astype(BF16)
        written = (e_s * writtens[f] - moved[DK:] + writtens[s]).astype(BF16)
        b_ref[sub] = writtens[f].astype(BF16)
        tail = total_rows(totals[f] + totals[s])
        for half in range(2):
            slot = 2 * sub + half
            ab_ref[slot, 0:DK, :] = transit
            ab_ref[slot, DK:DK + HALF, :] = written[half * HALF:(half + 1) * HALF]
            ab_ref[slot, DK + HALF:, :] = tail


def read_kernel(sc_ref, qo_ref, ko_ref, lo_ref, qx_ref, kx_ref, lx_ref, u0_ref, kg_ref,
                p_ref, r_ref, io_ref):
    row, col = grid_index()
    causal = row >= col
    tables = decay_tables(sc_ref, lo_ref, lx_ref, row, col)
    qs = in_order(sc_ref, qo_ref[...].astype(F32), qx_ref[...].astype(F32))
    ks = in_order(sc_ref, ko_ref[...].astype(F32), kx_ref[...].astype(F32))
    qns = [q * unit(q) * DK ** (-0.5) for q in qs]
    qks = [dot3(qn, k * unit(k), NT) for qn, k in zip(qns, ks)]
    cols, scores = [], []
    for sub, block in UNITS:
        cum_t, cum, _ = tables[block]
        h = first_head(sc_ref) + sub
        cum_col = column(cum, h)
        cols.append(cum_col)
        scores.append((qks[block] * decay_within(cum_col, as_row(cum_t, h), causal)).astype(BF16))
    for n, (sub, block) in enumerate(UNITS):
        p_ref[n] = scores[n]
        io_ref[n] = dot1(scores[n], u0_ref[n]).astype(BF16)
        r_ref[n] = (jnp.exp(cols[n]) * qns[block] - dot1(scores[n], kg_ref[n])).astype(BF16)


def gate_kernel(sc_ref, s_ref, go_ref, lo_ref, gx_ref, lx_ref, bo_ref, bx_ref,
                a_ref, b_ref, io_ref, u0_ref, kg_ref, r_ref,
                n0_ref, n1_ref, n2_ref, n3_ref, no_ref, nx_ref, gg_ref, ggx_ref, do_ref, u_ref, ss_ref, g_ref, gs_ref):
    gates = in_order(sc_ref, go_ref[...].astype(F32), gx_ref[...].astype(F32))
    me, step = sc_ref[1], pl.program_id(0)
    bgs = in_order(sc_ref, bo_ref[...].astype(F32), bx_ref[...].astype(F32))
    decays = in_order(sc_ref, lo_ref[:VALUE_HEADS], lx_ref[:VALUE_HEADS])[0]
    states, fades = [], []
    for sub in range(2):
        state = s_ref[sub]
        fade = jnp.exp(jnp.sum(as_row(decays, first_head(sc_ref) + sub), axis=1, keepdims=True))
        second = (fade * state.astype(F32) - dot1(state, a_ref[2 * sub])
                  + b_ref[sub].astype(F32)).astype(BF16)
        ss_ref[sub] = second
        states += [state, second]
        fades.append(fade)
    outs = [io_ref[n] + dot1(r_ref[n], states[n], NT) for n in range(4)]
    normeds, gate_grads, d_outs = [], [], []
    for n, (sub, block) in enumerate(UNITS):
        lanes = slice(sub * DV, (sub + 1) * DV)
        u_ref[n] = (u0_ref[n] - dot1(kg_ref[n], states[n], NT)).astype(BF16)
        out = outs[n]
        scale = lax.rsqrt(jnp.mean(out * out, axis=-1, keepdims=True) + NORM_EPS)
        z = out * scale
        gate = gates[block][:, lanes]
        sig = 1.0 / (1.0 + jnp.exp(-gate))
        sil = gate * sig
        normeds.append(z * sil)
        bg = bgs[block][:, lanes]
        gate_grads.append(bg * z * (sig + sil * (1.0 - sig)))
        dz = bg * sil
        d_out = scale * (dz - z * jnp.mean(dz * z, axis=-1, keepdims=True))
        d_outs.append(d_out.astype(BF16))
        do_ref[n] = d_outs[n]
    grads = [dot1(d_outs[n], r_ref[n], TN) for n in range(4)]
    for sub in range(2):
        lanes = slice(sub * DV, (sub + 1) * DV)
        f, s = 2 * sub, 2 * sub + 1
        g_ref[sub] = (grads[f] + fades[sub] * grads[s]
                      - dot1(grads[s], a_ref[f], NT)).astype(BF16)
        gs_ref[sub] = grads[s].astype(BF16)
        own, other = in_order(sc_ref, gate_grads[f], gate_grads[s])
        gg_ref[:, lanes] = own.astype(BF16)
        ggx_ref[:, lanes] = other.astype(BF16)
    columns = pl.ds(pl.multiple_of((step % 2) * 2 * DV, 2 * DV), 2 * DV)
    blocks = [jnp.concatenate([normeds[tau], normeds[2 + tau]], axis=1).astype(BF16)
              for tau in range(2)]
    no_ref[...], nx_ref[...] = in_order(sc_ref, *blocks)
    for n, ref in enumerate((n0_ref, n1_ref, n2_ref, n3_ref)):
        code = me ^ n

        @pl.when(code // 2 == step // 2)
        def _():
            ref[:, columns] = jnp.where(code % 2 == 0, blocks[0], blocks[1])


def early_kernel(sc_ref, qo_ref, ko_ref, lo_ref, qx_ref, kx_ref, lx_ref,
                 p_ref, u_ref, do_ref, s_ref, ss_ref,
                 dq_ref, dqx_ref, dk_ref, du_ref):
    row, col = grid_index()
    causal = row >= col
    tables = decay_tables(sc_ref, lo_ref, lx_ref, row, col)
    qs = in_order(sc_ref, qo_ref[...].astype(F32), qx_ref[...].astype(F32))
    ks = in_order(sc_ref, ko_ref[...].astype(F32), kx_ref[...].astype(F32))
    q_scales = [unit(q) for q in qs]
    qns = [(q * scale * DK ** (-0.5)).astype(BF16) for q, scale in zip(qs, q_scales)]
    kns = [(k * unit(k)).astype(BF16) for k in ks]
    raw = [dot1(do_ref[n], u_ref[n], NT) for n in range(4)]
    cols, d_scores = [], []
    for n, (sub, block) in enumerate(UNITS):
        cum_t, cum, _ = tables[block]
        h = first_head(sc_ref) + sub
        cols.append(column(cum, h))
        d_scores.append((raw[n] * decay_within(cols[n], as_row(cum_t, h), causal)).astype(BF16))
    dqs, dkns = [], []
    for n, (sub, block) in enumerate(UNITS):
        state = s_ref[sub] if block == 0 else ss_ref[sub]
        du_ref[n] = dot1(p_ref[n], do_ref[n], TN).astype(BF16)
        dqs.append(jnp.exp(cols[n]) * dot1(do_ref[n], state) + dot1(d_scores[n], kns[block]))
        dkns.append(dot1(d_scores[n], qns[block], TN))
    results = []
    for block in range(2):
        q, scale, dqn = qs[block], q_scales[block], dqs[block] + dqs[2 + block]
        dk_ref[block] = dkns[block] + dkns[2 + block]
        results.append(scale * DK ** (-0.5) * (
            dqn - q * (scale * scale) * jnp.sum(q * dqn, axis=-1, keepdims=True)))
    own, other = in_order(sc_ref, *results)
    dq_ref[...] = own.astype(BF16)
    dqx_ref[...] = other.astype(BF16)


def late_kernel(sc_ref, ko_ref, lo_ref, kx_ref, lx_ref, t_ref, u_ref, a_ref, s_ref, ss_ref,
                l_ref, gs_ref, dkn_ref, du_ref,
                dk_ref, dv_ref, dkx_ref, dvx_ref):
    row, col = grid_index()
    strict = row > col
    tables = decay_tables(sc_ref, lo_ref, lx_ref, row, col)
    ks = in_order(sc_ref, ko_ref[...].astype(F32), kx_ref[...].astype(F32))
    scales = [unit(k) for k in ks]
    kns = [(k * scale).astype(BF16) for k, scale in zip(ks, scales)]
    cols, rates, withins, leavings = [], [], [], []
    for n, (sub, block) in enumerate(UNITS):
        cum_t, cum, beta = tables[block]
        h = first_head(sc_ref) + sub
        cols.append(column(cum, h))
        rates.append(column(beta, h))
        withins.append(decay_within(cols[n], as_row(cum_t, h), strict) * (-rates[n]))
    for sub in range(2):
        last = l_ref[sub]
        fade = jnp.exp(cols[2 * sub + 1][T - 1:, :])
        leavings.append((gs_ref[sub].astype(F32) + fade * last.astype(F32)
                         - dot1(last, a_ref[2 * sub + 1], NT)).astype(BF16))
        leavings.append(last)
    fades = [jnp.exp(c[T - 1:, :] - c) for c in cols]
    dus = [du_ref[n] + fades[n] * dot1(kns[block], leavings[n], NT)
           for n, (sub, block) in enumerate(UNITS)]
    dxs = [dot1(t_ref[n], dus[n], TN) for n in range(4)]
    dx_bs = [dx.astype(BF16) for dx in dxs]
    d_inters = [dot1(dx_bs[n], u_ref[n], NT) * withins[n] for n in range(4)]
    dkns = []
    for n, (sub, block) in enumerate(UNITS):
        state = s_ref[sub] if block == 0 else ss_ref[sub]
        dkns.append(dot1(d_inters[n] + d_inters[n].T, kns[block])
                    + fades[n] * dot1(u_ref[n], leavings[n])
                    - (rates[n] * jnp.exp(cols[n])) * dot1(dx_bs[n], state))
    results = []
    for block in range(2):
        k, scale = ks[block], scales[block]
        dkn = dkn_ref[block] + dkns[block] + dkns[2 + block]
        results.append(
            scale * (dkn - k * (scale * scale) * jnp.sum(k * dkn, axis=-1, keepdims=True)))
    own, other = in_order(sc_ref, *results)
    dk_ref[...] = own.astype(BF16)
    dkx_ref[...] = other.astype(BF16)
    for sub in range(2):
        lanes = slice(sub * DV, (sub + 1) * DV)
        f, s = 2 * sub, 2 * sub + 1
        own, other = in_order(sc_ref, rates[f] * dxs[f], rates[s] * dxs[s])
        dv_ref[:, lanes] = own.astype(BF16)
        dvx_ref[:, lanes] = other.astype(BF16)


HEADS = VALUE_HEADS // 2
KEYS = HK // 2
PARAMS = pltpu.CompilerParams(vmem_limit_bytes=64 << 20)


def shape(dims, dtype=BF16):
    return jax.ShapeDtypeStruct(dims, dtype)


def block(dims, place):
    return pl.BlockSpec(dims, place)


OWN_KEY = block((T, DK), lambda i, sc: (0, KEYS * sc[0] + i))
OTHER_KEY = block((T, DK), lambda i, sc: (0, i))
OWN_VALUE = block((T, 2 * DV), lambda i, sc: (0, KEYS * sc[0] + i))
OTHER_VALUE = block((T, 2 * DV), lambda i, sc: (0, i))
PACKED_VALUE = block((T, 2 * DV), lambda i, sc: (0, KEYS // 2 + i))
TABLE = block((2 * VALUE_HEADS, T), lambda i, sc: (0, 0))
UNIT = block((4, T, DK), lambda i, sc: (i, 0, 0))
PAIR = block((2, T, DK), lambda i, sc: (i, 0, 0))
SLICE = block((T, 4 * DV), lambda i, sc: (0, 0))
UNIT_SHAPE, PAIR_SHAPE = (2 * HEADS, T, DK), (HEADS, T, DK)


def cost(gflops):
    return pl.CostEstimate(flops=int(gflops * 1e9), bytes_accessed=4 << 20, transcendentals=0)


def per_key(kernel, name, gflops, in_specs, out_specs, out_shape):
    return pl.pallas_call(
        kernel,
        grid_spec=pltpu.PrefetchScalarGridSpec(
            num_scalar_prefetch=1, grid=(KEYS,), in_specs=in_specs, out_specs=out_specs),
        out_shape=out_shape,
        compiler_params=PARAMS,
        cost_estimate=cost(gflops),
        name=name,
    )


ROWS = DK + HALF + TAIL
write_local = per_key(
    write_kernel, "write_local", 18,
    [OWN_KEY, OWN_VALUE, TABLE, OTHER_KEY, PACKED_VALUE, TABLE],
    [block((4, ROWS, DK), lambda i, sc: (i, 0, 0)), UNIT, UNIT, UNIT, UNIT, PAIR],
    [shape((2 * HEADS, ROWS, DK)), shape(UNIT_SHAPE), shape(UNIT_SHAPE), shape(UNIT_SHAPE),
     shape(UNIT_SHAPE), shape(PAIR_SHAPE)])
read_local = per_key(
    read_kernel, "read_local", 6,
    [OWN_KEY, OWN_KEY, TABLE, OTHER_KEY, OTHER_KEY, TABLE, UNIT, UNIT],
    [UNIT] * 3,
    [shape(UNIT_SHAPE)] * 3)
gate_local = per_key(
    gate_kernel, "gate_local", 7,
    [PAIR, OWN_VALUE, TABLE, PACKED_VALUE, TABLE, OTHER_VALUE, OTHER_VALUE, UNIT, PAIR]
    + [UNIT] * 4,
    [SLICE] * 4 + [OTHER_VALUE, OTHER_VALUE, OWN_VALUE, OTHER_VALUE, UNIT, UNIT]
    + [PAIR] * 3,
    [shape((T, 4 * DV))] * 4 + [shape((T, HEADS * DV))] * 2
    + [shape((T, VALUE_HEADS * DV)),
     shape((T, HEADS * DV)), shape(UNIT_SHAPE), shape(UNIT_SHAPE), shape(PAIR_SHAPE),
     shape(PAIR_SHAPE), shape(PAIR_SHAPE)])
BLOCK_KEY = block((2, T, DK), lambda i, sc: (0, 0, i))
early_local = per_key(
    early_kernel, "early_local", 7,
    [OWN_KEY, OWN_KEY, TABLE, OTHER_KEY, OTHER_KEY, TABLE, UNIT, UNIT, UNIT, PAIR, PAIR],
    [OWN_KEY, OTHER_KEY, BLOCK_KEY, UNIT],
    [shape((T, HK * DK)), shape((T, KEYS * DK)), shape((2, T, KEYS * DK), F32),
     shape(UNIT_SHAPE)])
late_local = per_key(
    late_kernel, "late_local", 9,
    [OWN_KEY, TABLE, OTHER_KEY, TABLE, UNIT, UNIT, UNIT, PAIR, PAIR, PAIR, PAIR, BLOCK_KEY, UNIT],
    [OWN_KEY, OWN_VALUE, OTHER_KEY, OTHER_VALUE],
    [shape((T, HK * DK)), shape((T, VALUE_HEADS * DV)), shape((T, KEYS * DK)),
     shape((T, HEADS * DV))])


def chain_up_kernel(count, ab_ref, s_ref):
    def step(i, state):
        s_ref[i] = state.astype(BF16)
        tail = ab_ref[i, DK + HALF:, :].astype(F32)
        decay = jnp.exp(jnp.sum(tail, axis=0, keepdims=True))
        high, low = split(state)
        moved = dot1(jnp.concatenate([high, low], axis=0), ab_ref[i, 0:DK, :])
        written = ab_ref[i, DK:DK + HALF, :].astype(F32)
        return decay * state - (moved[:HALF] + moved[HALF:]) + written

    lax.fori_loop(0, count, step, jnp.zeros((HALF, DK), F32), unroll=True)


def chain_down_kernel(count, ab_ref, g_ref, l_ref):
    def step(j, state):
        i = count - 1 - j
        l_ref[i] = state.astype(BF16)
        tail = ab_ref[i, DK + HALF:, :].astype(F32)
        decay = jnp.exp(jnp.sum(tail, axis=0, keepdims=True))
        high, low = split(state)
        moved = dot1(jnp.concatenate([high, low], axis=0), ab_ref[i, 0:DK, :], NT)
        return decay * state - (moved[:HALF] + moved[HALF:]) + g_ref[i].astype(F32)

    lax.fori_loop(0, count, step, jnp.zeros((HALF, DK), F32), unroll=True)


def chain(kernel, count, *args):
    return pl.pallas_call(
        functools.partial(kernel, count),
        out_shape=shape((count, HALF, DK)),
        compiler_params=PARAMS,
        cost_estimate=cost(3),
        name="chain",
    )(*args)


def pack_kernel(sc_ref, lengths_ref, pairing_ref, ratio_ref, cot_ref, ld_ref, be_ref,
                q_ref, k_ref, v_ref, gate_ref,
                scaled_ref, kv_ref, qg_ref, table_ref):
    own = sc_ref[1]
    tokens = cot_ref.shape[0]
    start = sc_ref[2] * T + pl.program_id(0) * tokens
    weight = jnp.zeros((8, 128), F32)
    for pair in range(pairing_ref.shape[0] // 2):
        chosen, rejected = pairing_ref[2 * pair], pairing_ref[2 * pair + 1]
        ratio_c = jnp.full((8, 128), ratio_ref[chosen], F32)
        ratio_r = jnp.full((8, 128), ratio_ref[rejected], F32)
        up_c, up_r = jnp.exp(ratio_c), jnp.exp(ratio_r)
        margin = CHI_BETA * (up_c + ratio_c - up_r - ratio_r)
        pull = CHI_BETA / (1.0 + jnp.exp(margin))
        weight = weight + jnp.where(chosen == own, -pull * (up_c + 1.0), 0.0)
        weight = weight + jnp.where(rejected == own, pull * (up_r + 1.0), 0.0)
    position = start + lax.broadcasted_iota(jnp.int32, (tokens, 1), 0)
    live = (position < lengths_ref[own]).astype(F32)
    factor = weight[0:1, 0:1] * live
    scaled_ref[...] = (cot_ref[...].astype(F32) * factor).astype(BF16)
    keys = KEYS * DK
    kv_ref[:, :keys] = k_ref[...]
    kv_ref[:, keys:] = v_ref[...]
    qg_ref[:, :keys] = q_ref[...]
    qg_ref[:, keys:] = gate_ref[...]
    table_ref[:VALUE_HEADS] = ld_ref[...]
    table_ref[VALUE_HEADS:] = be_ref[...]


def pack_local(sc, lengths, pairing, ratio, cot, ld, be, q, k, v, gate):
    scalars = pl.BlockSpec(memory_space=pltpu.SMEM)
    whole = lambda dims: block(dims, lambda i, sc: (0, 0))
    some = T // 2
    rows = lambda dims: block((some,) + dims[1:], lambda i, sc: (i, 0))
    half = lambda width: block((some, width), lambda i, sc: (i, 1 - sc[0]))
    keys, values = KEYS * DK, HEADS * DV
    packed = (T, keys + values)
    table = (2 * VALUE_HEADS, T)
    return pl.pallas_call(
        pack_kernel,
        grid_spec=pltpu.PrefetchScalarGridSpec(
            num_scalar_prefetch=1,
            grid=(T // some,),
            in_specs=[scalars] * 3 + [rows(cot.shape), whole(ld.shape), whole(be.shape),
                                      half(keys), half(keys), half(values), half(values)],
            out_specs=[rows(cot.shape), rows(packed), rows(packed), whole(table)],
        ),
        out_shape=[shape(cot.shape), shape(packed), shape(packed), shape(table, F32)],
        compiler_params=PARAMS,
        cost_estimate=cost(1),
        name="pack_local",
    )(sc, lengths, pairing, ratio, cot, ld, be, q, k, v, gate)


def turn(sc_ref):
    core, me = sc_ref[0], sc_ref[1]
    return (2 * (me % 2) + core) ^ me


def back_kernel(sc_ref, own_ref, other_ref, *refs):
    bo_ref, bx_ref = refs[8:]
    scaled = jnp.concatenate([own_ref[...], other_ref[...]], axis=0)
    first = pl.program_id(0) < 2
    weight = jnp.concatenate(
        [jnp.where(first, refs[n][...], refs[4 + n][...]) for n in range(4)], axis=1)
    product = dot1(scaled, weight, NT).astype(BF16)
    bo_ref[...] = product[:T]
    bx_ref[...] = product[T:]


def back_local(sc, own, other, weights):
    features, columns = weights[0].shape
    width, part = features // 2, columns // 4
    tokens = block((T, columns), lambda i, sc: (0, 0))
    out = block((T, width), lambda i, sc: (0, 2 * ((i // 2) ^ (sc[1] % 2)) + i % 2))
    early = [block((width, part), lambda i, sc, n=n: (jnp.minimum(i, 1), n)) for n in range(4)]
    late = [block((width, part), lambda i, sc, n=n: (jnp.maximum(i - 2, 0), n)) for n in range(4)]
    return pl.pallas_call(
        back_kernel,
        grid_spec=pltpu.PrefetchScalarGridSpec(
            num_scalar_prefetch=1,
            grid=(4,),
            in_specs=[tokens, tokens] + early + late,
            out_specs=[out, out],
        ),
        out_shape=[shape((T, 2 * features))] * 2,
        compiler_params=PARAMS,
        cost_estimate=cost(3),
        name="back_local",
    )(sc, own, other, *[weights[0]] * 4, *[weights[1]] * 4)


def mixed_kernel(sc_ref, no_ref, nx_ref, *refs):
    own_ref, other_ref = refs[8:]
    features = 4 * refs[0].shape[0]
    odd = sc_ref[1] % 2
    first = pl.ds(pl.multiple_of(odd * features, features), features)
    second = pl.ds(pl.multiple_of((1 - odd) * features, features), features)
    weights = [jnp.concatenate([ref[...] for ref in refs[4 * n:4 * n + 4]], axis=0)
               for n in range(2)]
    product = (dot1(jnp.concatenate([no_ref[:, first], nx_ref[:, first]], axis=0), weights[0])
               + dot1(jnp.concatenate([no_ref[:, second], nx_ref[:, second]], axis=0), weights[1]))
    own_ref[...] = product[:T]
    other_ref[...] = product[T:].astype(BF16)


def mixed_local(sc, own, other, weights, width=512):
    features, columns = weights[0].shape
    tokens = block((T, 2 * features), lambda i, sc: (0, 0))
    rows = [block((features // 4, width), lambda i, sc, n=n: (n, i)) for n in range(4)]
    out = block((T, width), lambda i, sc: (0, i))
    return pl.pallas_call(
        mixed_kernel,
        grid_spec=pltpu.PrefetchScalarGridSpec(
            num_scalar_prefetch=1,
            grid=(columns // width,),
            in_specs=[tokens, tokens] + rows + rows,
            out_specs=[out, out],
        ),
        out_shape=[shape((T, columns), F32), shape((T, columns))],
        compiler_params=PARAMS,
        cost_estimate=cost(3),
        name="mixed_local",
    )(sc, own, other, *[weights[0]] * 4, *[weights[1]] * 4)


def weight_kernel(sc_ref, *refs):
    keep_ref, send_ref, rows_ref, part_ref, sems = refs[8:]
    for n in range(4):
        rows_ref[n ^ turn(sc_ref)] = refs[n][...]
    rows = rows_ref[...].reshape(4 * T, rows_ref.shape[2])
    chips, cores, height, columns = part_ref.shape
    width, some = columns // 4, chips // 2
    core = lax.axis_index("ctx") % 2
    copies = []
    for n in range(4):
        lanes = slice(n * width, (n + 1) * width)
        scaled = jnp.concatenate([ref[:, lanes] for ref in refs[4:8]], axis=0)
        part_ref[:, :, :, lanes] = dot1(rows, scaled, TN).astype(BF16).reshape(
            chips, cores, height, width)
        for m in range(2):
            group, lane = pl.ds(m * some, some), pl.ds(n * width, width)
            for to_ref, row in ((keep_ref, core), (send_ref, 1 - core)):
                copies.append(pltpu.make_async_copy(
                    part_ref.at[group, row, :, lane], to_ref.at[group, :, lane],
                    sems.at[len(copies)]))
                copies[-1].start()
    for copy in copies:
        copy.wait()


def weight_local(sc, rows, scaled):
    features, columns = rows[0].shape[1], scaled[0].shape[1]
    same = lambda part: block(part.shape, lambda i, sc: (0, 0))
    return pl.pallas_call(
        weight_kernel,
        grid_spec=pltpu.PrefetchScalarGridSpec(
            num_scalar_prefetch=1,
            grid=(1,),
            in_specs=[same(part) for part in rows + scaled],
            out_specs=[pl.BlockSpec(memory_space=pl.ANY)] * 2,
            scratch_shapes=[pltpu.VMEM((4, T, features), BF16),
                            pltpu.VMEM((features // 32, 2, 16, columns), BF16),
                            pltpu.SemaphoreType.DMA((16,))],
        ),
        out_shape=[shape((features // 32, 16, columns))] * 2,
        compiler_params=PARAMS,
        cost_estimate=cost(4),
        name="weight_local",
    )(sc, *rows, *scaled)


def join_kernel(*refs):
    for n in range(2):
        refs[4][4 * n:4 * n + 4] = (
            refs[n][...].astype(F32) + refs[2 + n][...].astype(F32)).astype(BF16)


def join(a, b):
    streams = [block((4,) + a.shape[1:], lambda i, n=n: (2 * i + n, 0, 0)) for n in range(2)]
    return pl.pallas_call(
        join_kernel,
        grid=(a.shape[0] // 8,),
        in_specs=streams * 2,
        out_specs=block((8,) + a.shape[1:], lambda i: (i, 0, 0)),
        out_shape=shape(a.shape),
        compiler_params=PARAMS,
        cost_estimate=cost(1),
        name="join",
    )(a, a, b, b)


def total_kernel(*refs):
    refs[-1][...] = functools.reduce(
        lambda a, b: a + b, [jnp.sum(ref[...].astype(F32), axis=0) for ref in refs[:-1]])


def total(parts, streams=8):
    count, rows, columns = parts.shape
    return pl.pallas_call(
        total_kernel,
        grid=(1,),
        in_specs=[block((count // streams, rows, columns), lambda i, n=n: (n, 0, 0))
                  for n in range(streams)],
        out_specs=block((rows, columns), lambda i: (0, 0)),
        out_shape=shape((rows, columns), F32),
        compiler_params=PARAMS,
        cost_estimate=cost(1),
        name="total",
    )(*[parts] * streams)


def fill_kernel(sc_ref, *refs):
    count = (len(refs) - 4) // 3
    owns, other_ref, mixed_ref = refs[:2], refs[2], refs[3 + 2 * count]
    for part_ref, out_ref in zip(refs[3 + count:3 + 2 * count], refs[4 + 2 * count:]):
        out_ref[...] = part_ref[...]
    width = owns[0].shape[1]
    for n in range(2):
        lanes = slice(n * width, (n + 1) * width)
        mixed_ref[:, lanes] = (owns[n][...] + other_ref[:, lanes].astype(F32)).astype(BF16)


def fill(sc, mixed, wholes, parts):
    count, steps = len(wholes), 2
    columns = mixed[1].shape[1]
    some = lambda part: block((T, part.shape[1] // steps), lambda i, sc: (0, i))
    return pl.pallas_call(
        fill_kernel,
        grid_spec=pltpu.PrefetchScalarGridSpec(
            num_scalar_prefetch=1,
            grid=(steps,),
            in_specs=[block((T, columns // 4), lambda i, sc, n=n: (0, 2 * i + n))
                      for n in range(2)]
            + [some(mixed[1])] + [pl.BlockSpec(memory_space=pl.ANY)] * count
            + [some(part) for part in parts],
            out_specs=[some(mixed[1])]
            + [block((T, part.shape[1] // steps), lambda i, sc: (0, steps * (1 - sc[0]) + i))
               for part in parts],
        ),
        out_shape=[shape(mixed[1].shape)] + [shape(whole.shape) for whole in wholes],
        input_output_aliases={4 + n: 1 + n for n in range(count)},
        compiler_params=PARAMS,
        cost_estimate=cost(1),
        name="fill",
    )(sc, mixed[0], *mixed, *wholes, *parts)


def exchange(x):
    count = lax.axis_size("ctx")
    groups = [list(range(core, count, 2)) for core in range(2)]
    return lax.all_to_all(x, "ctx", split_axis=0, concat_axis=0, tiled=True,
                          axis_index_groups=groups)


def cross(x, axis, distance):
    count = lax.axis_size(axis)
    return lax.ppermute(x, axis, [(i, i ^ distance) for i in range(count)])


def sibling(x):
    return cross(x, "ctx", 1)


def tie(*values):
    return lax.optimization_barrier(values)


def place_of(z, chip, core, chips):
    return (z * chips + chip) * 2 + core


def feature_round(x, n, seqs):
    chips = lax.axis_size("ctx") // 2
    pairs = [(place_of(z, chip, core, chips),
              place_of(2 * core + (z ^ n) // 2, chip, (z ^ n) % 2, chips))
             for z in range(seqs) for chip in range(chips) for core in range(2)]
    return lax.ppermute(x, ("fsdp", "ctx"), pairs)


def weight_round(x, n, seqs):
    chips = lax.axis_size("ctx") // 2
    pairs = [(place_of(2 * core + (z ^ n) % 2, chip, 1 - z // 2, chips),
              place_of(z, chip, core, chips))
             for z in range(seqs) for chip in range(chips) for core in range(2)]
    return lax.ppermute(x, ("fsdp", "ctx"), pairs)


def body(query_vectors, key_vectors, value_vectors, output_gate, log_decay, write_rate,
         out_weight, cotangent, lengths, pairing, log_ratio):
    q, k, v, gate = query_vectors[0], key_vectors[0], value_vectors[0], output_gate[0]
    spot = lax.axis_index("ctx")
    core, chips = spot % 2, lax.axis_size("ctx") // 2
    me = lax.axis_index("fsdp")
    seqs = lax.axis_size("fsdp")
    sc = jnp.stack([core, me, spot])

    scaled, kv, qg, table = pack_local(
        sc, lengths, pairing, log_ratio, cotangent[0], log_decay[0].T, write_rate[0].T,
        q, k, v, gate)
    with jax.named_scope("swap_heads"):
        kv_x, table_x, qg_x, scaled_x = sibling(kv), sibling(table), sibling(qg), sibling(scaled)
    with jax.named_scope("out_weight"):
        heads_weight = [weight_round(out_weight, n, seqs) for n in range(2)]
    ab, t, u0, kg, a, b = write_local(sc, k, v, table, kv_x, kv_x, table_x)
    with jax.named_scope("every_scaled"):
        own_scaled = tie(ab, scaled)[1]
        every_scaled = [scaled] + [cross(own_scaled, "fsdp", s) for s in range(1, seqs)]
    ab = exchange(ab)
    p, r, io = read_local(sc, q, k, table, qg_x, kv_x, table_x, u0, kg)
    ab, p, r, io = tie(ab, p, r, io)
    states = chain(chain_up_kernel, chips, ab)
    entering = exchange(states).reshape(PAIR_SHAPE)
    with jax.named_scope("back_grad"):
        bg = back_local(sc, tie(states, scaled)[1], scaled_x, heads_weight)
    *rows, normed, normed_x, gate_grad, gate_grad_x, d_out, u, second, g, gs = gate_local(
        sc, entering, gate, table, qg_x, table_x, *bg, a, b, io, u0, kg, r)
    g = exchange(g.reshape(2 * HEADS, HALF, DK))
    with jax.named_scope("every_normed"):
        rows = [feature_round(rows[n], n, seqs) for n in range(seqs)]
    dq, dq_x, dkn, du = early_local(sc, q, k, table, qg_x, kv_x, table_x, p, u, d_out,
                                    entering, second)
    with jax.named_scope("weight_grad"):
        keep, send = weight_local(sc, rows, every_scaled)
    g, dq, dq_x, dkn, du, send = tie(g, dq, dq_x, dkn, du, send)
    leaving = exchange(chain(chain_down_kernel, chips, ab, g)).reshape(PAIR_SHAPE)
    with jax.named_scope("weight_grad"):
        leaving, terms = tie(leaving, join(keep, sibling(send)))
        weight_grad = total(exchange(terms))
    with jax.named_scope("swap_back"):
        others = [sibling(gate_grad_x), sibling(dq_x)]
    dk, dv, dk_x, dv_x = late_local(sc, k, table, kv_x, table_x, t, u, a, entering, second,
                                    leaving, gs, dkn, du)
    with jax.named_scope("mixed_out"):
        mixed, mixed_x = mixed_local(sc, normed, normed_x, heads_weight)
        mixed_x = sibling(mixed_x)
    with jax.named_scope("swap_back"):
        mixed, gate_grad, dq, dk, dv = fill(
            sc, [mixed, mixed_x], [gate_grad, dq, dk, dv], others + [sibling(dk_x), sibling(dv_x)])
    return mixed[None], dq[None], dk[None], dv[None], gate_grad[None], weight_grad


def solution(mesh):
    tokens = P("fsdp", "ctx", None)
    return jax.shard_map(
        body,
        mesh=mesh,
        in_specs=(tokens,) * 6 + (P("fsdp", None), tokens, P(), P(), P()),
        out_specs=(tokens,) * 5 + (P(("fsdp", "ctx"), None),),
        check_vma=False,
    )
```

time: 194 us -> 148 us (0.76)
  waiting for transfers between devices: 50.3 us -> 15.9 us
  Pallas kernels: 61.8 us -> 77.2 us
  other arithmetic: 10.9 us -> 0.66 us
  local copies, waits for them, and re-layouts: 8.89 us -> 0 us
  matrix products: 5.08 us -> 0 us
  starting transfers between devices: 55.6 us -> 52.4 us
    ppermute x19 -> x13, waiting for transfers between devices: 42.1 us -> 1.67 us  [cross(): return lax.ppermute(x, axis, [(i, i ^ distance) for i in range(count)])]
    ppermute x19 -> x13, starting transfers between devices: 25.8 us -> 9.56 us  [cross(): return lax.ppermute(x, axis, [(i, i ^ distance) for i in range(count)])]
    pallas_call x9 -> x14, Pallas kernels: 61.8 us -> 77.2 us  [the longest x1 14.7 us: body(): ab, t, u0, kg, a, b = write_local(sc, k, v, table, kv_x, kv_x, table_x)]
    ppermute x0 -> x6, starting transfers between devices: none -> 10.5 us  [the longest x4 6.32 us: feature_round(): return lax.ppermute(x, ('fsdp', 'ctx'), pairs)]
    unnamed x24 -> x0, local copies, waits for them, and re-layouts: 5.77 us -> none
    dot_general x2 -> x0, matrix products: 5.08 us -> none  [the longest x1 2.6 us: body(): mixed = lax.dot_general(rows, out_weight, NN, preferred_element_type=F32)]
    all_to_all x4 -> x5, waiting for transfers between devices: 8.25 us -> 13.1 us  [exchange(): lax.all_to_all(x, 'ctx', split_axis=0, concat_axis=0, tiled=True, axis_in...]
    concatenate x2 -> x0, other arithmetic: 3.58 us -> none  [the longest x1 2.75 us: body(): every_scaled = jnp.concatenate([scaled] + others, axis=0)]
  transfers between devices with their start and end apart: 23 -> 24, of which waited for: 8 -> 7; matrix products, arithmetic and copies ran while one was open for 8% -> 0% of each run, Pallas kernels for 19% -> 49%
where the time goes in v3:
time: 148 us; the launch traced here: 147 us
  Pallas kernels  77.2 us (52%)
  starting transfers between devices  52.4 us (35%)
  waiting for transfers between devices  15.9 us (11%)
    all_to_all x5, starting transfers between devices, exchange(): lax.all_to_all(x, 'ctx', split_axis=0, concat_axis=0, tiled=True, axis_in...  32.3 us
    pallas_call x1, Pallas kernels, body(): ab, t, u0, kg, a, b = write_local(sc, k, v, table, kv_x, kv_x, table_x)  14.7 us
    all_to_all x5, waiting for transfers between devices, exchange(): lax.all_to_all(x, 'ctx', split_axis=0, concat_axis=0, tiled=True, axis_in...  13.1 us
    ppermute x13, starting transfers between devices, cross(): return lax.ppermute(x, axis, [(i, i ^ distance) for i in range(count)])  9.56 us
    pallas_call x1, Pallas kernels, body(): late_local(sc, k, table, kv_x, table_x, t, u, a, entering, second, leavin...  7.91 us
    pallas_call x2, Pallas kernels, chain(): pl.pallas_call(functools.partial(kernel, count), out_shape=shape((count,...  7.63 us
    pallas_call x1, Pallas kernels, body(): gate_local(sc, entering, gate, table, qg_x, table_x, *bg, a, b, io, u0, k...  7.44 us
    ppermute x4, starting transfers between devices, feature_round(): return lax.ppermute(x, ('fsdp', 'ctx'), pairs)  6.32 us
  transfers between devices with their start and end apart: 24, of which 7 were waited for; matrix products, arithmetic and copies ran while one was open for 0% of the time, Pallas kernels for 49%

profile of v3, /device:TPU:0, one launch (start us, length us, event | category | flops | bytes accessed | tf_op | source)
XLA Modules:
  0.0 147.0 jit_solution(16393044151918624258)
XLA Ops:
  0.6 0.7 pad_add_fusion.sc_ref
  1.3 2.9 %pack_local.1 = (bf16[128,2048]{1,0:T(8,128)(2,1)}, bf16[128,1536]{1,0:T(8,128)(2,1)}, bf16[128,1536]{1,0:T(8,128)(2,1)}, f32[32,128]{1,0:T(8,128)}) custom-call(s32[3]{0:T(128)} %pad_add_fusion.sc_ref, s32[4]{0:T(128)} %lengths_ref.1, s32[4]{0:T(128)} %pairing_ref.1, f32[4]{0:T(128)} %ratio_ref.1, bf16[128,2048]{1,0:T(8,128)(2,1)} %bitcast.27, ...), custom_call_target="tpu_custom_call" | custom-call | flops 1000000000 | bytes 4194304 | tf_op jit(solution)/shard_map/pack_local/pallas_call | solution.py:485
  4.2 0.1 collective-permute-start
  4.3 0.5 collective-permute-start.1
  4.8 4.0 %collective-permute-start.4 = (bf16[512,2048]{1,0:T(8,128)(2,1)}, bf16[512,2048]{1,0:T(8,128)(2,1)}, u32[]{:S(2)}, u32[]{:S(2)}) collective-permute-start(bf16[512,2048]{1,0:T(8,128)(2,1)} %param.17), channel_id=1, source_target_pairs={{1,0},{65,1},{3,2},{67,3},{5,4},{69,5},{7,6},{71,7},{9,8},{73,9},{... | collective-permute-start | bytes 6291464 | tf_op jit(solution)/shard_map/out_weight/ppermute | solution.py:732
  8.8 0.3 collective-permute-start.5
  9.0 0.9 collective-permute-start.2
  9.9 0.0 collective-permute-done.1.lx_ref
  9.9 0.0 collective-permute-done.kx_ref.vx_ref
  9.9 14.7 %write_local.1 = (bf16[16,208,128]{2,1,0:T(8,128)(2,1)}, bf16[16,128,128]{2,1,0:T(8,128)(2,1)}, bf16[16,128,128]{2,1,0:T(8,128)(2,1)}, bf16[16,128,128]{2,1,0:T(...) custom-call(s32[3]{0:T(128)} %pad_add_fusion.sc_ref, bf16[128,1024]{1,0:T(8,128)(2,1)} %bitcast.37, ...), custom_call_target="tpu_custom_call" | custom-call | flops 17999998976 | bytes 4194304 | tf_op jit(solution)/shard_map/write_local/pallas_call | solution.py:751
  24.6 7.1 %all-to-all-start = ((bf16[16,208,128]{2,1,0:T(8,128)(2,1)}), bf16[16,208,128]{2,1,0:T(8,128)(2,1)}, u32[]{:S(2)}, u32[]{:S(2)}) async-start(bf16[16,208,128]{2,1,0:T(8,128)(2,1)} %get-tuple-element.67), calls=%async_computation | async-start | bytes 1703936 | tf_op jit(solution)/shard_map/all_to_all | solution.py:698
  31.7 0.1 collective-permute-start.3
  31.8 1.1 collective-permute-start.11
  32.9 0.0 collective-permute-done.2.qx_ref.gx_ref
  32.9 1.1 collective-permute-start.12
  33.9 5.3 %read_local.1 = (bf16[16,128,128]{2,1,0:T(8,128)(2,1)}, bf16[16,128,128]{2,1,0:T(8,128)(2,1)}, bf16[16,128,128]{2,1,0:T(8,128)(2,1)}) custom-call(s32[3]{0:T(128)} %pad_add_fusion.sc_ref, bf16[128,1024]{1,0:T(8,128)(2,1)} %bitcast.34, bf16[128,1024]{1,0:T(8,128)(2,1)} %bitcast.38, f32[32,128]{1,0:T(8,128)} %get-tuple-element.65.lo_ref, ...), custom_call_target="tpu_custom_call" | custom-call | flops 6000000000 | bytes 4194304 | tf_op jit(solution)/shard_map/read_local/pallas_call | solution.py:756
  39.3 8.0 %all-to-all-done.ab_ref = bf16[16,208,128]{2,1,0:T(8,128)(2,1)} async-done(((bf16[16,208,128]{2,1,0:T(8,128)(2,1)}), bf16[16,208,128]{2,1,0:T(8,128)(2,1)}, u32[]{:S(2)}, u32[]{:S(2)}) %all-to-all-start) | async-done | bytes 852000 | tf_op jit(solution)/shard_map/all_to_all | solution.py:698
  47.3 3.8 %chain.2 = bf16[16,64,128]{2,1,0:T(8,128)(2,1)} custom-call(bf16[16,208,128]{2,1,0:T(8,128)(2,1)} %all-to-all-done.ab_ref), custom_call_target="tpu_custom_call" | custom-call | flops 3000000000 | bytes 4194304 | tf_op jit(solution)/shard_map/chain/pallas_call | solution.py:438
  51.0 4.2 %all-to-all-start.1 = ((bf16[16,64,128]{2,1,0:T(8,128)(2,1)}), bf16[16,64,128]{2,1,0:T(8,128)(2,1)}, u32[]{:S(2)}, u32[]{:S(2)}) async-start(bf16[16,64,128]{2,1,0:T(8,128)(2,1)} %chain.2), calls=%async_computation.1 | async-start | bytes 524288 | tf_op jit(solution)/shard_map/all_to_all | solution.py:698
  55.2 0.0 collective-permute-done.3.other_ref
  55.2 0.9 collective-permute-start.13
  56.1 0.0 collective-permute-done.4.refs_0_.refs_1_.refs_2_.refs_3_
  56.1 0.8 collective-permute-done.5.refs_4_.refs_5_.refs_6_.refs_7_
  56.9 6.3 %back_local.1 = (bf16[128,1024]{1,0:T(8,128)(2,1)}, bf16[128,1024]{1,0:T(8,128)(2,1)}) custom-call(s32[3]{0:T(128)} %pad_add_fusion.sc_ref, bf16[128,2048]{1,0:T(8,128)(2,1)} %get-tuple-element.101.own_ref.refs_4_, bf16[128,2048]{1,0:T(8,128)(2,1)} %collective-permute-done.3.other_ref, ...), custom_call_target="tpu_custom_call" | custom-call | flops 3000000000 | bytes 4194304 | tf_op jit(solution)/shard_map/back_grad/back_local/pallas_call | solution.py:524
  63.2 0.5 all-to-all-done.1
  63.7 7.4 %gate_local.1 = (bf16[128,512]{1,0:T(8,128)(2,1)}, bf16[128,512]{1,0:T(8,128)(2,1)}, bf16[128,512]{1,0:T(8,128)(2,1)}, bf16[128,512]{1,0:T(8,128)(2,1)}, bf16[12...) custom-call(s32[3]{0:T(128)} %pad_add_fusion.sc_ref, ...), custom_call_target="tpu_custom_call" | custom-call | flops 7000000000 | bytes 4194304 | tf_op jit(solution)/shard_map/gate_local/pallas_call | solution.py:762
  71.2 1.9 %collective-permute-start.10 = (bf16[128,512]{1,0:T(8,128)(2,1)}, bf16[128,512]{1,0:T(8,128)(2,1)}, u32[]{:S(2)}, u32[]{:S(2)}) collective-permute-start(bf16[128,512]{1,0:T(8,128)(2,1)} %get-tuple-element.100), channel_id=1, source_target_pairs={{0,33},{1,97},{2,35},{3,99},{4,37},{5,101},{6,39},{7,103},{8,41},{... | collective-permute-start | bytes 393224 | tf_op jit(solution)/shard_map/every_normed/ppermute | solution.py:724
  73.1 2.2 %collective-permute-start.7 = (bf16[128,512]{1,0:T(8,128)(2,1)}, bf16[128,512]{1,0:T(8,128)(2,1)}, u32[]{:S(2)}, u32[]{:S(2)}) collective-permute-start(bf16[128,512]{1,0:T(8,128)(2,1)} %get-tuple-element.97), channel_id=1, source_target_pairs={{0,0},{1,64},{2,2},{3,66},{4,4},{5,68},{6,6},{7,70},{8,8},{9,72},{... | collective-permute-start | bytes 393224 | tf_op jit(solution)/shard_map/every_normed/ppermute | solution.py:724
  75.3 6.6 %all-to-all-start.2 = ((bf16[16,64,128]{2,1,0:T(8,128)(2,1)}), bf16[16,64,128]{2,1,0:T(8,128)(2,1)}, u32[]{:S(2)}, u32[]{:S(2)}) async-start(bf16[16,64,128]{2,1,0:T(8,128)(2,1)} %bitcast.26), calls=%async_computation.2 | async-start | bytes 524288 | tf_op jit(solution)/shard_map/all_to_all | solution.py:698
  81.9 0.0 collective-permute-done.11.refs_5_
  81.9 1.9 %collective-permute-start.8 = (bf16[128,512]{1,0:T(8,128)(2,1)}, bf16[128,512]{1,0:T(8,128)(2,1)}, u32[]{:S(2)}, u32[]{:S(2)}) collective-permute-start(bf16[128,512]{1,0:T(8,128)(2,1)} %get-tuple-element.98), channel_id=1, source_target_pairs={{0,1},{1,65},{2,3},{3,67},{4,5},{5,69},{6,7},{7,71},{8,9},{9,73},{... | collective-permute-start | bytes 393224 | tf_op jit(solution)/shard_map/every_normed/ppermute | solution.py:724
  83.8 0.0 collective-permute-done.12.refs_6_
  83.8 0.3 collective-permute-start.9
  84.1 6.1 %early_local.1 = (bf16[128,1024]{1,0:T(8,128)(2,1)}, bf16[128,512]{1,0:T(8,128)(2,1)}, f32[2,128,512]{2,1,0:T(8,128)}, bf16[16,128,128]{2,1,0:T(8,128)(2,1)}) custom-call(s32[3]{0:T(128)} %pad_add_fusion.sc_ref, bf16[128,1024]{1,0:T(8,128)(2,1)} %bitcast.35, bf16[128,1024]{1,0:T(8,128)(2,1)} %bitcast.39, f32[32,128]{1,0:T(8,128)} %get-tuple-element.65.lo_ref, ...), custom_call_target="tpu_custom_call" | custom-call | flops 7000000000 | bytes 4194304 | tf_op jit(solution)/shard_map/early_local/pallas_call | solution.py:767
  90.3 0.0 collective-permute-done.13.refs_7_
  90.3 0.0 collective-permute-done.10.refs_3_
  90.3 0.0 collective-permute-done.7.refs_0_
  90.3 0.0 collective-permute-done.8.refs_1_
  90.3 0.3 collective-permute-done.9.refs_2_
  90.6 5.2 %weight_local.1 = (bf16[16,16,2048]{2,1,0:T(8,128)(2,1)}, bf16[16,16,2048]{2,1,0:T(8,128)(2,1)}) custom-call(s32[3]{0:T(128)} %pad_add_fusion.sc_ref, bf16[128,512]{1,0:T(8,128)(2,1)} %collective-permute-done.7.refs_0_, bf16[128,512]{1,0:T(8,128)(2,1)} %collective-permute-done.8.refs_1_, bf16[128,512]{1,0:T(8,128)(2,1)} %collective-permute-done.9.refs_2_, ...), custom_call_target="tpu_custom_call" | custom-call | flops 4000000000 | bytes 4194304 | tf_op jit(solution)/shard_map/weight_grad/weight_local/pallas_call | solution.py:601
  95.8 0.0 all-to-all-done.2.g_ref
  95.8 3.7 %collective-permute-start.14 = (bf16[16,16,2048]{2,1,0:T(8,128)(2,1)}, bf16[16,16,2048]{2,1,0:T(8,128)(2,1)}, u32[]{:S(2)}, u32[]{:S(2)}) collective-permute-start(bf16[16,16,2048]{2,1,0:T(8,128)(2,1)} %get-tuple-element.107), channel_id=1, source_target_pairs={{0,1},{1,0},{2,3},{3,2},{4,5},{5,4},{6,7},{7,6},{8,9},{9,8},{10,11... | collective-permute-start | bytes 3145736 | tf_op jit(solution)/shard_map/weight_grad/ppermute | solution.py:704
  99.6 3.8 %chain.3 = bf16[16,64,128]{2,1,0:T(8,128)(2,1)} custom-call(bf16[16,208,128]{2,1,0:T(8,128)(2,1)} %all-to-all-done.ab_ref, bf16[16,64,128]{2,1,0:T(8,128)(2,1)} %all-to-all-done.2.g_ref), custom_call_target="tpu_custom_call" | custom-call | flops 3000000000 | bytes 4194304 | tf_op jit(solution)/shard_map/chain/pallas_call | solution.py:438
  103.4 7.2 %all-to-all-start.3 = ((bf16[16,64,128]{2,1,0:T(8,128)(2,1)}), bf16[16,64,128]{2,1,0:T(8,128)(2,1)}, u32[]{:S(2)}, u32[]{:S(2)}) async-start(bf16[16,64,128]{2,1,0:T(8,128)(2,1)} %chain.3), calls=%async_computation.3 | async-start | bytes 524288 | tf_op jit(solution)/shard_map/all_to_all | solution.py:698
  110.7 5.9 %mixed_local.1 = (f32[128,2048]{1,0:T(8,128)}, bf16[128,2048]{1,0:T(8,128)(2,1)}) custom-call(s32[3]{0:T(128)} %pad_add_fusion.sc_ref, bf16[128,1024]{1,0:T(8,128)(2,1)} %get-tuple-element.83.no_ref, bf16[128,1024]{1,0:T(8,128)(2,1)} %get-tuple-element.84.nx_ref, bf16[512,2048]{1,0:T(8,128)(2,1)} %collective-permute-done.4.refs_0_.refs_1_.refs_2_.refs_3_, ...), custom_call_target="tpu_custom_call" | custom-call | flops 3000000000 | bytes 4194304 | tf_op jit(solution)/shard_map/mixed_out/mixed_local/pallas_call | solution.py:558
  116.6 0.1 collective-permute-start.6
  116.7 0.5 collective-permute-start.15
  117.2 0.0 collective-permute-done.14.refs_2_.refs_3_
  117.2 2.4 %join.1 = bf16[16,16,2048]{2,1,0:T(8,128)(2,1)} custom-call(bf16[16,16,2048]{2,1,0:T(8,128)(2,1)} %get-tuple-element.106.refs_0_.refs_1_, bf16[16,16,2048]{2,1,0:T(8,128)(2,1)} %get-tuple-element.106.refs_0_.refs_1_, bf16[16,16,2048]{2,1,0:T(8,128)(2,1)} %collective-permute-done.14.refs_2_.refs_3_, bf16[16,16,2048]{2,1,0:T(8,128)(2,1)} %collective-permute-done.14.refs_2_.refs_3_), custom_call_target="tpu_custom_call" | custom-call | flops 1000000000 | bytes 4194304 | tf_op jit(solution)/shard_map/weight_grad/join/pallas_call | solution.py:627
  119.6 0.0 all-to-all-done.3
  119.6 7.2 %all-to-all-start.4 = ((bf16[16,16,2048]{2,1,0:T(8,128)(2,1)}), bf16[16,16,2048]{2,1,0:T(8,128)(2,1)}, u32[]{:S(2)}, u32[]{:S(2)}) async-start(bf16[16,16,2048]{2,1,0:T(8,128)(2,1)} %join.1), calls=%async_computation.4 | async-start | bytes 2097152 | tf_op jit(solution)/shard_map/weight_grad/all_to_all | solution.py:698
  126.9 7.9 %late_local.1 = (bf16[128,1024]{1,0:T(8,128)(2,1)}, bf16[128,2048]{1,0:T(8,128)(2,1)}, bf16[128,512]{1,0:T(8,128)(2,1)}, bf16[128,1024]{1,0:T(8,128)(2,1)}) custom-call(s32[3]{0:T(128)} %pad_add_fusion.sc_ref, bf16[128,1024]{1,0:T(8,128)(2,1)} %bitcast.40, f32[32,128]{1,0:T(8,128)} %get-tuple-element.65.lo_ref, ...), custom_call_target="tpu_custom_call" | custom-call | flops 8999999488 | bytes 4194304 | tf_op jit(solution)/shard_map/late_local/pallas_call | solution.py:778
  134.8 0.1 collective-permute-start.18
  134.9 0.5 collective-permute-start.16
  135.4 0.1 collective-permute-start.17
  135.4 0.0 collective-permute-done.15.refs_7_
  135.5 1.5 collective-permute-done.16.refs_8_
  136.9 0.0 collective-permute-done.6.refs_2_
  136.9 0.2 collective-permute-done.17.refs_9_
  137.1 0.0 collective-permute-done.18.refs_10_
  137.1 3.2 %fill.1 = (bf16[128,2048]{1,0:T(8,128)(2,1)}, bf16[128,2048]{1,0:T(8,128)(2,1)}, bf16[128,1024]{1,0:T(8,128)(2,1)}, bf16[128,1024]{1,0:T(8,128)(2,1)}, bf16[128,2048]{1,0:T(8,128)(2,1)}) custom-call(s32[3]{0:T(128)} %pad_add_fusion.sc_ref, ...), custom_call_target="tpu_custom_call", output_to_operand_aliasing={{1}: (4, {}), {2}: (5, {}), {3}: (6, {}), {4}: (7, {})} | custom-call | flops 1000000000 | bytes 4194304 | tf_op jit(solution)/shard_map/swap_back/fill/pallas_call | solution.py:674
  140.3 4.6 %all-to-all-done.4.refs_0_.refs_1_.refs_2_.refs_3_.refs_4_.refs_5_.refs_6_.refs_7_ = bf16[16,16,2048]{2,1,0:T(8,128)(2,1)} async-done(((bf16[16,16,2048]{2,1,0:T(8,128)(2,1)}), bf16[16,16,2048]{2,1,0:T(8,128)(2,1)}, u32[]{:S(2)}, u32[]{:S(2)}) %all-to-all-start.4) | async-done | bytes 1048608 | tf_op jit(solution)/shard_map/weight_grad/all_to_all | solution.py:698
  145.0 2.1 %total.1 = f32[16,2048]{1,0:T(8,128)} custom-call(bf16[16,16,2048]{2,1,0:T(8,128)(2,1)} %all-to-all-done.4.refs_0_.refs_1_.refs_2_.refs_3_.refs_4_.refs_5_.refs_6_.refs_7_, bf16[16,16,2048]{2,1,0:T(8,128)(2,1)} %all-to-all-done.4.refs_0_.refs_1_.refs_2_.refs_3_.refs_4_.refs_5_.refs_6_.refs_7_, ...), custom_call_target="tpu_custom_call" | custom-call | flops 1000000000 | bytes 4194304 | tf_op jit(solution)/shard_map/weight_grad/total/pallas_call | solution.py:646
Async XLA Ops:
  4.2 5.7 %collective-permute-start = (bf16[128,1536]{1,0:T(8,128)(2,1)}, bf16[128,1536]{1,0:T(8,128)(2,1)}, u32[]{:S(2)}, u32[]{:S(2)}) collective-permute-start(bf16[128,1536]{1,0:T(8,128)(2,1)} %get-tuple-element.66), channel_id=1, source_target_pairs={{0,1},{1,0},{2,3},{3,2},{4,5},{5,4},{6,7},{7,6},{8,9},{9,8},{10,11... | collective-permute-start | bytes 1179656 | tf_op jit(solution)/shard_map/swap_heads/ppermute | solution.py:704
  4.3 5.6 %collective-permute-start.1 = (f32[32,128]{1,0:T(8,128)}, f32[32,128]{1,0:T(8,128)}, u32[]{:S(2)}, u32[]{:S(2)}) collective-permute-start(f32[32,128]{1,0:T(8,128)} %get-tuple-element.65.lo_ref), channel_id=1, source_target_pairs={{0,1},{1,0},{2,3},{3,2},{4,5},{5,4},{6,7},{7,6},{8,9},{9,8},{10,11... | collective-permute-start | bytes 49160 | tf_op jit(solution)/shard_map/swap_heads/ppermute | solution.py:704
  4.8 51.3 %collective-permute-start.4 = (bf16[512,2048]{1,0:T(8,128)(2,1)}, bf16[512,2048]{1,0:T(8,128)(2,1)}, u32[]{:S(2)}, u32[]{:S(2)}) collective-permute-start(bf16[512,2048]{1,0:T(8,128)(2,1)} %param.17), channel_id=1, source_target_pairs={{1,0},{65,1},{3,2},{67,3},{5,4},{69,5},{7,6},{71,7},{9,8},{73,9},{... | collective-permute-start | bytes 6291464 | tf_op jit(solution)/shard_map/out_weight/ppermute | solution.py:732
  8.8 48.2 %collective-permute-start.5 = (bf16[512,2048]{1,0:T(8,128)(2,1)}, bf16[512,2048]{1,0:T(8,128)(2,1)}, u32[]{:S(2)}, u32[]{:S(2)}) collective-permute-start(bf16[512,2048]{1,0:T(8,128)(2,1)} %param.17), channel_id=1, source_target_pairs={{33,0},{97,1},{35,2},{99,3},{37,4},{101,5},{39,6},{103,7},{41,8},{... | collective-permute-start | bytes 6291464 | tf_op jit(solution)/shard_map/out_weight/ppermute | solution.py:732
  9.0 23.9 %collective-permute-start.2 = (bf16[128,1536]{1,0:T(8,128)(2,1)}, bf16[128,1536]{1,0:T(8,128)(2,1)}, u32[]{:S(2)}, u32[]{:S(2)}) collective-permute-start(bf16[128,1536]{1,0:T(8,128)(2,1)} %get-tuple-element.68), channel_id=1, source_target_pairs={{0,1},{1,0},{2,3},{3,2},{4,5},{5,4},{6,7},{7,6},{8,9},{9,8},{10,11... | collective-permute-start | bytes 1179656 | tf_op jit(solution)/shard_map/swap_heads/ppermute | solution.py:704
  24.6 22.7 %all-to-all-start = ((bf16[16,208,128]{2,1,0:T(8,128)(2,1)}), bf16[16,208,128]{2,1,0:T(8,128)(2,1)}, u32[]{:S(2)}, u32[]{:S(2)}) async-start(bf16[16,208,128]{2,1,0:T(8,128)(2,1)} %get-tuple-element.67), calls=%async_computation | async-start | bytes 1703936 | tf_op jit(solution)/shard_map/all_to_all | solution.py:698
  31.7 23.5 %collective-permute-start.3 = (bf16[128,2048]{1,0:T(8,128)(2,1)}, bf16[128,2048]{1,0:T(8,128)(2,1)}, u32[]{:S(2)}, u32[]{:S(2)}) collective-permute-start(bf16[128,2048]{1,0:T(8,128)(2,1)} %get-tuple-element.101.own_ref.refs_4_), channel_id=1, source_target_pairs={{0,1},{1,0},{2,3},{3,2},{4,5},{5,4},{6,7},{7,6},{8,9},{9,8},{10,11... | collective-permute-start | bytes 1572872 | tf_op jit(solution)/shard_map/swap_heads/ppermute | solution.py:704
  31.8 50.1 %collective-permute-start.11 = (bf16[128,2048]{1,0:T(8,128)(2,1)}, bf16[128,2048]{1,0:T(8,128)(2,1)}, u32[]{:S(2)}, u32[]{:S(2)}) collective-permute-start(bf16[128,2048]{1,0:T(8,128)(2,1)} %get-tuple-element.101.own_ref.refs_4_), channel_id=1, source_target_pairs={{0,32},{32,0},{64,96},{96,64},{1,33},{33,1},{65,97},{97,65},{2,34}... | collective-permute-start | bytes 1572872 | tf_op jit(solution)/shard_map/every_scaled/ppermute | solution.py:704
  32.9 51.0 %collective-permute-start.12 = (bf16[128,2048]{1,0:T(8,128)(2,1)}, bf16[128,2048]{1,0:T(8,128)(2,1)}, u32[]{:S(2)}, u32[]{:S(2)}) collective-permute-start(bf16[128,2048]{1,0:T(8,128)(2,1)} %get-tuple-element.101.own_ref.refs_4_), channel_id=1, source_target_pairs={{0,64},{32,96},{64,0},{96,32},{1,65},{33,97},{65,1},{97,33},{2,66}... | collective-permute-start | bytes 1572872 | tf_op jit(solution)/shard_map/every_scaled/ppermute | solution.py:704
  51.0 12.7 %all-to-all-start.1 = ((bf16[16,64,128]{2,1,0:T(8,128)(2,1)}), bf16[16,64,128]{2,1,0:T(8,128)(2,1)}, u32[]{:S(2)}, u32[]{:S(2)}) async-start(bf16[16,64,128]{2,1,0:T(8,128)(2,1)} %chain.2), calls=%async_computation.1 | async-start | bytes 524288 | tf_op jit(solution)/shard_map/all_to_all | solution.py:698
  55.2 35.0 %collective-permute-start.13 = (bf16[128,2048]{1,0:T(8,128)(2,1)}, bf16[128,2048]{1,0:T(8,128)(2,1)}, u32[]{:S(2)}, u32[]{:S(2)}) collective-permute-start(bf16[128,2048]{1,0:T(8,128)(2,1)} %get-tuple-element.101.own_ref.refs_4_), channel_id=1, source_target_pairs={{0,96},{32,64},{64,32},{96,0},{1,97},{33,65},{65,33},{97,1},{2,98}... | collective-permute-start | bytes 1572872 | tf_op jit(solution)/shard_map/every_scaled/ppermute | solution.py:704
  71.2 19.1 %collective-permute-start.10 = (bf16[128,512]{1,0:T(8,128)(2,1)}, bf16[128,512]{1,0:T(8,128)(2,1)}, u32[]{:S(2)}, u32[]{:S(2)}) collective-permute-start(bf16[128,512]{1,0:T(8,128)(2,1)} %get-tuple-element.100), channel_id=1, source_target_pairs={{0,33},{1,97},{2,35},{3,99},{4,37},{5,101},{6,39},{7,103},{8,41},{... | collective-permute-start | bytes 393224 | tf_op jit(solution)/shard_map/every_normed/ppermute | solution.py:724
  73.1 17.2 %collective-permute-start.7 = (bf16[128,512]{1,0:T(8,128)(2,1)}, bf16[128,512]{1,0:T(8,128)(2,1)}, u32[]{:S(2)}, u32[]{:S(2)}) collective-permute-start(bf16[128,512]{1,0:T(8,128)(2,1)} %get-tuple-element.97), channel_id=1, source_target_pairs={{0,0},{1,64},{2,2},{3,66},{4,4},{5,68},{6,6},{7,70},{8,8},{9,72},{... | collective-permute-start | bytes 393224 | tf_op jit(solution)/shard_map/every_normed/ppermute | solution.py:724
  75.3 20.6 %all-to-all-start.2 = ((bf16[16,64,128]{2,1,0:T(8,128)(2,1)}), bf16[16,64,128]{2,1,0:T(8,128)(2,1)}, u32[]{:S(2)}, u32[]{:S(2)}) async-start(bf16[16,64,128]{2,1,0:T(8,128)(2,1)} %bitcast.26), calls=%async_computation.2 | async-start | bytes 524288 | tf_op jit(solution)/shard_map/all_to_all | solution.py:698
  81.9 8.4 %collective-permute-start.8 = (bf16[128,512]{1,0:T(8,128)(2,1)}, bf16[128,512]{1,0:T(8,128)(2,1)}, u32[]{:S(2)}, u32[]{:S(2)}) collective-permute-start(bf16[128,512]{1,0:T(8,128)(2,1)} %get-tuple-element.98), channel_id=1, source_target_pairs={{0,1},{1,65},{2,3},{3,67},{4,5},{5,69},{6,7},{7,71},{8,9},{9,73},{... | collective-permute-start | bytes 393224 | tf_op jit(solution)/shard_map/every_normed/ppermute | solution.py:724
  83.8 6.8 %collective-permute-start.9 = (bf16[128,512]{1,0:T(8,128)(2,1)}, bf16[128,512]{1,0:T(8,128)(2,1)}, u32[]{:S(2)}, u32[]{:S(2)}) collective-permute-start(bf16[128,512]{1,0:T(8,128)(2,1)} %get-tuple-element.99), channel_id=1, source_target_pairs={{0,32},{1,96},{2,34},{3,98},{4,36},{5,100},{6,38},{7,102},{8,40},{... | collective-permute-start | bytes 393224 | tf_op jit(solution)/shard_map/every_normed/ppermute | solution.py:724
  95.8 21.3 %collective-permute-start.14 = (bf16[16,16,2048]{2,1,0:T(8,128)(2,1)}, bf16[16,16,2048]{2,1,0:T(8,128)(2,1)}, u32[]{:S(2)}, u32[]{:S(2)}) collective-permute-start(bf16[16,16,2048]{2,1,0:T(8,128)(2,1)} %get-tuple-element.107), channel_id=1, source_target_pairs={{0,1},{1,0},{2,3},{3,2},{4,5},{5,4},{6,7},{7,6},{8,9},{9,8},{10,11... | collective-permute-start | bytes 3145736 | tf_op jit(solution)/shard_map/weight_grad/ppermute | solution.py:704
  103.4 16.2 %all-to-all-start.3 = ((bf16[16,64,128]{2,1,0:T(8,128)(2,1)}), bf16[16,64,128]{2,1,0:T(8,128)(2,1)}, u32[]{:S(2)}, u32[]{:S(2)}) async-start(bf16[16,64,128]{2,1,0:T(8,128)(2,1)} %chain.3), calls=%async_computation.3 | async-start | bytes 524288 | tf_op jit(solution)/shard_map/all_to_all | solution.py:698
  116.6 20.3 %collective-permute-start.6 = (bf16[128,2048]{1,0:T(8,128)(2,1)}, bf16[128,2048]{1,0:T(8,128)(2,1)}, u32[]{:S(2)}, u32[]{:S(2)}) collective-permute-start(bf16[128,2048]{1,0:T(8,128)(2,1)} %get-tuple-element.86), channel_id=1, source_target_pairs={{0,1},{1,0},{2,3},{3,2},{4,5},{5,4},{6,7},{7,6},{8,9},{9,8},{10,11... | collective-permute-start | bytes 1572872 | tf_op jit(solution)/shard_map/mixed_out/ppermute | solution.py:704
  116.7 18.8 %collective-permute-start.15 = (bf16[128,1024]{1,0:T(8,128)(2,1)}, bf16[128,1024]{1,0:T(8,128)(2,1)}, u32[]{:S(2)}, u32[]{:S(2)}) collective-permute-start(bf16[128,1024]{1,0:T(8,128)(2,1)} %get-tuple-element.114), channel_id=1, source_target_pairs={{0,1},{1,0},{2,3},{3,2},{4,5},{5,4},{6,7},{7,6},{8,9},{9,8},{10,11... | collective-permute-start | bytes 786440 | tf_op jit(solution)/shard_map/swap_back/ppermute | solution.py:704
  119.6 25.3 %all-to-all-start.4 = ((bf16[16,16,2048]{2,1,0:T(8,128)(2,1)}), bf16[16,16,2048]{2,1,0:T(8,128)(2,1)}, u32[]{:S(2)}, u32[]{:S(2)}) async-start(bf16[16,16,2048]{2,1,0:T(8,128)(2,1)} %join.1), calls=%async_computation.4 | async-start | bytes 2097152 | tf_op jit(solution)/shard_map/weight_grad/all_to_all | solution.py:698
  134.8 2.3 %collective-permute-start.18 = (bf16[128,1024]{1,0:T(8,128)(2,1)}, bf16[128,1024]{1,0:T(8,128)(2,1)}, u32[]{:S(2)}, u32[]{:S(2)}) collective-permute-start(bf16[128,1024]{1,0:T(8,128)(2,1)} %get-tuple-element.117), channel_id=1, source_target_pairs={{0,1},{1,0},{2,3},{3,2},{4,5},{5,4},{6,7},{7,6},{8,9},{9,8},{10,11... | collective-permute-start | bytes 786440 | tf_op jit(solution)/shard_map/swap_back/ppermute | solution.py:704
  134.9 2.1 %collective-permute-start.16 = (bf16[128,512]{1,0:T(8,128)(2,1)}, bf16[128,512]{1,0:T(8,128)(2,1)}, u32[]{:S(2)}, u32[]{:S(2)}) collective-permute-start(bf16[128,512]{1,0:T(8,128)(2,1)} %get-tuple-element.115), channel_id=1, source_target_pairs={{0,1},{1,0},{2,3},{3,2},{4,5},{5,4},{6,7},{7,6},{8,9},{9,8},{10,11... | collective-permute-start | bytes 393224 | tf_op jit(solution)/shard_map/swap_back/ppermute | solution.py:704
  135.4 1.7 %collective-permute-start.17 = (bf16[128,512]{1,0:T(8,128)(2,1)}, bf16[128,512]{1,0:T(8,128)(2,1)}, u32[]{:S(2)}, u32[]{:S(2)}) collective-permute-start(bf16[128,512]{1,0:T(8,128)(2,1)} %get-tuple-element.116), channel_id=1, source_target_pairs={{0,1},{1,0},{2,3},{3,2},{4,5},{5,4},{6,7},{7,6},{8,9},{9,8},{10,11... | collective-permute-start | bytes 393224 | tf_op jit(solution)/shard_map/swap_back/ppermute | solution.py:704

commit v4 on v3

v4 whole, which is shorter than its diff:
```python
import functools

import jax
import jax.numpy as jnp
from jax import lax
from jax.experimental import pallas as pl
from jax.experimental.pallas import tpu as pltpu
from jax.sharding import PartitionSpec as P

VALUE_HEADS = 16
HK = 8
DK = 128
DV = 128
T = 128
HALF = 64
TAIL = 16
CHI_BETA = 0.5
NORM_EPS = 1e-06
F32 = jnp.float32
BF16 = jnp.bfloat16

NN = (((1,), (0,)), ((), ()))
NT = (((1,), (1,)), ((), ()))
TN = (((0,), (0,)), ((), ()))


def dot1(a, b, dims=NN):
    return lax.dot_general(a.astype(BF16), b.astype(BF16), dims, preferred_element_type=F32)


def split(a):
    high = a.astype(BF16)
    return high, (a - high.astype(F32)).astype(BF16)


def dot3(a, b, dims=NN):
    a_high, a_low = split(a)
    b_high, b_low = split(b)
    return dot1(a_high, b_high, dims) + (dot1(a_low, b_high, dims) + dot1(a_high, b_low, dims))


def grid_index():
    row = lax.broadcasted_iota(jnp.int32, (T, T), 0)
    col = lax.broadcasted_iota(jnp.int32, (T, T), 1)
    return row, col


def unit(x):
    return lax.rsqrt(jnp.sum(x * x, axis=-1, keepdims=True) + NORM_EPS)


def dot_exact_left(a, b):
    first = a.astype(BF16)
    rest = a - first.astype(F32)
    second = rest.astype(BF16)
    third = (rest - second.astype(F32)).astype(BF16)
    return dot1(first, b) + (dot1(second, b) + dot1(third, b))


def in_order(sc_ref, own, other):
    is_first = sc_ref[0] == 0
    return jnp.where(is_first, own, other), jnp.where(is_first, other, own)


def decay_tables(sc_ref, lo_ref, ro_ref, lx_ref, rx_ref, row, col):
    upper = (row <= col).astype(BF16)
    tables = []
    for decay, rate in zip(in_order(sc_ref, lo_ref[...], lx_ref[...]),
                           in_order(sc_ref, ro_ref[...], rx_ref[...])):
        cum_t = dot_exact_left(decay, upper)
        tables.append((cum_t, cum_t.T, rate.T))
    return tables


def column(table, head):
    lane = lax.broadcasted_iota(jnp.int32, table.shape, 1)
    return jnp.sum(jnp.where(lane == head, table, 0.0), axis=1, keepdims=True)


def as_row(table_t, head):
    sub = lax.broadcasted_iota(jnp.int32, table_t.shape, 0)
    return jnp.sum(jnp.where(sub == head, table_t, 0.0), axis=0, keepdims=True)


def decay_within(cum_col, cum_row, mask):
    return jnp.where(mask, jnp.exp(jnp.where(mask, cum_col - cum_row, 0.0)), 0.0)


def stripes(x, size, first):
    return jnp.concatenate(
        [x[start:start + size] for start in range(first * size, T, 2 * size)], axis=0)


def weave(even, odd, size):
    parts = []
    for start in range(0, T // 2, size):
        parts += [even[start:start + size], odd[start:start + size]]
    return jnp.concatenate(parts, axis=0)


def invert(couplings, row, col):
    eye = (row == col).astype(F32)
    pairs = (row >> 1) == (col >> 1)
    inverses = [eye - jnp.where(pairs, c, 0.0) for c in couplings]
    for level in range(1, 3):
        mask = ((row >> (level + 1)) == (col >> (level + 1))) & ((row >> level) != (col >> level))
        offs = [jnp.where(mask, c, 0.0).astype(BF16) for c in couplings]
        low = [i.astype(BF16) for i in inverses]
        inner = [dot1(o, i) for o, i in zip(offs, low)]
        inverses = [x - dot1(i, n) for x, i, n in zip(inverses, low, inner)]
    for level in range(3, 7):
        size = 1 << level
        mask = (stripes(row, size, 1) >> level) == (stripes(col, size, 1) >> level) + 1
        zeros = jnp.zeros((T // 2, T), F32)
        odds = [stripes(i, size, 1) for i in inverses]
        inner = [dot1(jnp.where(mask, stripes(c, size, 1), 0.0), i)
                 for c, i in zip(couplings, inverses)]
        odds = [o - dot1(o, weave(zeros, n, size)) for o, n in zip(odds, inner)]
        inverses = [weave(stripes(i, size, 0), o, size) for i, o in zip(inverses, odds)]
    return inverses


def total_rows(total):
    wide = jnp.broadcast_to(total, (TAIL, DK))
    high, low = split(wide)
    low2 = (wide - high.astype(F32) - low.astype(F32)).astype(BF16)
    sub_row = lax.broadcasted_iota(jnp.int32, (TAIL, DK), 0)
    tail = jnp.where(sub_row == 0, high.astype(F32),
                     jnp.where(sub_row == 1, low.astype(F32),
                               jnp.where(sub_row == 2, low2.astype(F32), 0.0)))
    return tail.astype(BF16)


def units(keys):
    return [(sub, block, 2 * (sub // 2) + block) for sub in range(2 * keys) for block in range(2)]


def first_head(sc_ref, keys):
    return (VALUE_HEADS // 2) * sc_ref[0] + 2 * keys * pl.program_id(0)


def per_head(sc_ref, keys, own_ref, other_ref):
    found = []
    for key in range(keys):
        lanes = slice(key * DK, (key + 1) * DK)
        found += in_order(sc_ref, own_ref[:, lanes].astype(F32), other_ref[:, lanes].astype(F32))
    return found


def write_kernel(keys, sc_ref, ko_ref, vo_ref, lo_ref, ro_ref, kx_ref, vx_ref, lx_ref, rx_ref,
                 ab_ref, t_ref, u0_ref, kg_ref, a_ref, b_ref):
    row, col = grid_index()
    causal, strict = row >= col, row > col
    tables = decay_tables(sc_ref, lo_ref, ro_ref, lx_ref, rx_ref, row, col)
    ks = per_head(sc_ref, keys, ko_ref, kx_ref)
    vs = in_order(sc_ref, vo_ref[...].astype(F32), vx_ref[...].astype(F32))
    kns = [k * unit(k) for k in ks]
    kks = [dot3(kn, kn, NT) for kn in kns]
    cols, rates, couplings = [], [], []
    for sub, block, kb in units(keys):
        cum_t, cum, beta = tables[block]
        h = first_head(sc_ref, keys) + sub
        cum_col, rate = column(cum, h), column(beta, h)
        within = decay_within(cum_col, as_row(cum_t, h), causal)
        couplings.append(jnp.where(strict, kks[kb] * within, 0.0) * rate)
        cols.append(cum_col)
        rates.append(rate)
    inverses = [i.astype(BF16) for i in invert(couplings, row, col)]
    u0s, kgs, transits, writtens, totals = [], [], [], [], []
    for n, (sub, block, kb) in enumerate(units(keys)):
        u0s.append(dot1(inverses[n], rates[n] * vs[block][:, sub * DV:(sub + 1) * DV]))
        kgs.append(dot1(inverses[n], (rates[n] * jnp.exp(cols[n])) * kns[kb]).astype(BF16))
    for n, (sub, block, kb) in enumerate(units(keys)):
        total = cols[n][T - 1:, :]
        carried = (jnp.exp(total - cols[n]) * kns[kb]).astype(BF16)
        transits.append(dot1(kgs[n], carried, TN))
        writtens.append(dot1(u0s[n], carried, TN))
        totals.append(total)
        t_ref[n] = inverses[n]
        u0_ref[n] = u0s[n].astype(BF16)
        kg_ref[n] = kgs[n]
        a_ref[n] = transits[n].astype(BF16)
    for sub in range(2 * keys):
        f, s = 2 * sub, 2 * sub + 1
        e_f, e_s = jnp.exp(totals[f]), jnp.exp(totals[s])
        stacked = jnp.concatenate([transits[f], writtens[f]], axis=0)
        moved = dot3(stacked, transits[s])
        transit = (e_f * transits[s] + e_s * transits[f] - moved[:DK]).astype(BF16)
        written = (e_s * writtens[f] - moved[DK:] + writtens[s]).astype(BF16)
        b_ref[sub] = writtens[f].astype(BF16)
        tail = total_rows(totals[f] + totals[s])
        for half in range(2):
            slot = 2 * sub + half
            ab_ref[slot, 0:DK, :] = transit
            ab_ref[slot, DK:DK + HALF, :] = written[half * HALF:(half + 1) * HALF]
            ab_ref[slot, DK + HALF:, :] = tail


def read_kernel(keys, sc_ref, qo_ref, ko_ref, lo_ref, ro_ref, qx_ref, kx_ref, lx_ref, rx_ref, u0_ref, kg_ref,
                p_ref, r_ref, io_ref):
    row, col = grid_index()
    causal = row >= col
    tables = decay_tables(sc_ref, lo_ref, ro_ref, lx_ref, rx_ref, row, col)
    qs = per_head(sc_ref, keys, qo_ref, qx_ref)
    ks = per_head(sc_ref, keys, ko_ref, kx_ref)
    qns = [q * unit(q) * DK ** (-0.5) for q in qs]
    qks = [dot3(qn, k * unit(k), NT) for qn, k in zip(qns, ks)]
    cols, scores = [], []
    for sub, block, kb in units(keys):
        cum_t, cum, _ = tables[block]
        h = first_head(sc_ref, keys) + sub
        cum_col = column(cum, h)
        cols.append(cum_col)
        scores.append((qks[kb] * decay_within(cum_col, as_row(cum_t, h), causal)).astype(BF16))
    for n, (sub, block, kb) in enumerate(units(keys)):
        p_ref[n] = scores[n]
        io_ref[n] = dot1(scores[n], u0_ref[n]).astype(BF16)
        r_ref[n] = (jnp.exp(cols[n]) * qns[kb] - dot1(scores[n], kg_ref[n])).astype(BF16)


def gate_kernel(keys, sc_ref, s_ref, go_ref, lo_ref, ro_ref, gx_ref, lx_ref, rx_ref, bo_ref, bx_ref,
                a_ref, b_ref, io_ref, u0_ref, kg_ref, r_ref, p_ref, qo_ref, ko_ref, qx_ref, kx_ref,
                n0_ref, n1_ref, n2_ref, n3_ref, no_ref, nx_ref, gg_ref, ggx_ref,
                u_ref, ss_ref, g_ref, gs_ref, dq_ref, dqx_ref, dk_ref, du_ref):
    gates = in_order(sc_ref, go_ref[...].astype(F32), gx_ref[...].astype(F32))
    me, step = sc_ref[1], pl.program_id(0)
    steps = KEYS // (2 * keys)
    bgs = in_order(sc_ref, bo_ref[...].astype(F32), bx_ref[...].astype(F32))
    row, col = grid_index()
    causal = row >= col
    tables = decay_tables(sc_ref, lo_ref, ro_ref, lx_ref, rx_ref, row, col)
    qs = per_head(sc_ref, keys, qo_ref, qx_ref)
    ks = per_head(sc_ref, keys, ko_ref, kx_ref)
    q_scales = [unit(q) for q in qs]
    qns = [(q * scale * DK ** (-0.5)).astype(BF16) for q, scale in zip(qs, q_scales)]
    kns = [(k * unit(k)).astype(BF16) for k in ks]
    cols = [column(tables[block][1], first_head(sc_ref, keys) + sub) for sub, block, kb in units(keys)]
    states, fades = [], []
    for sub in range(2 * keys):
        state = s_ref[sub]
        fade = jnp.exp(cols[2 * sub][T - 1:, :])
        second = (fade * state.astype(F32) - dot1(state, a_ref[2 * sub])
                  + b_ref[sub].astype(F32)).astype(BF16)
        ss_ref[sub] = second
        states += [state, second]
        fades.append(fade)
    outs = [io_ref[n] + dot1(r_ref[n], states[n], NT) for n in range(4 * keys)]
    normeds, gate_grads, d_outs, us = [], [], [], []
    for n, (sub, block, kb) in enumerate(units(keys)):
        lanes = slice(sub * DV, (sub + 1) * DV)
        us.append((u0_ref[n] - dot1(kg_ref[n], states[n], NT)).astype(BF16))
        u_ref[n] = us[n]
        out = outs[n]
        scale = lax.rsqrt(jnp.mean(out * out, axis=-1, keepdims=True) + NORM_EPS)
        z = out * scale
        gate = gates[block][:, lanes]
        sig = 1.0 / (1.0 + jnp.exp(-gate))
        sil = gate * sig
        normeds.append(z * sil)
        bg = bgs[block][:, lanes]
        gate_grads.append(bg * z * (sig + sil * (1.0 - sig)))
        dz = bg * sil
        d_out = scale * (dz - z * jnp.mean(dz * z, axis=-1, keepdims=True))
        d_outs.append(d_out.astype(BF16))
    grads = [dot1(d_outs[n], r_ref[n], TN) for n in range(4 * keys)]
    for sub in range(2 * keys):
        lanes = slice(sub * DV, (sub + 1) * DV)
        f, s = 2 * sub, 2 * sub + 1
        g_ref[sub] = (grads[f] + fades[sub] * grads[s]
                      - dot1(grads[s], a_ref[f], NT)).astype(BF16)
        gs_ref[sub] = grads[s].astype(BF16)
        own, other = in_order(sc_ref, gate_grads[f], gate_grads[s])
        gg_ref[:, lanes] = own.astype(BF16)
        ggx_ref[:, lanes] = other.astype(BF16)
    width = 2 * keys * DV
    columns = pl.ds(pl.multiple_of((step % steps) * width, width), width)
    blocks = [jnp.concatenate(normeds[tau::2], axis=1).astype(BF16) for tau in range(2)]
    no_ref[...], nx_ref[...] = in_order(sc_ref, *blocks)
    for n, ref in enumerate((n0_ref, n1_ref, n2_ref, n3_ref)):
        code = me ^ n

        @pl.when(code // 2 == step // steps)
        def _():
            ref[:, columns] = jnp.where(code % 2 == 0, blocks[0], blocks[1])
    raw = [dot1(d_outs[n], us[n], NT) for n in range(4 * keys)]
    d_scores = []
    for n, (sub, block, kb) in enumerate(units(keys)):
        cum_t, h = tables[block][0], first_head(sc_ref, keys) + sub
        d_scores.append((raw[n] * decay_within(cols[n], as_row(cum_t, h), causal)).astype(BF16))
    dqs, dkns = [], []
    for n, (sub, block, kb) in enumerate(units(keys)):
        du_ref[n] = dot1(p_ref[n], d_outs[n], TN).astype(BF16)
        dqs.append(jnp.exp(cols[n]) * dot1(d_outs[n], states[n]) + dot1(d_scores[n], kns[kb]))
        dkns.append(dot1(d_scores[n], qns[kb], TN))
    for key in range(keys):
        lanes = slice(key * DK, (key + 1) * DK)
        results = []
        for block in range(2):
            n, kb = 4 * key + block, 2 * key + block
            q, scale, dqn = qs[kb], q_scales[kb], dqs[n] + dqs[n + 2]
            dk_ref[block, :, lanes] = dkns[n] + dkns[n + 2]
            results.append(scale * DK ** (-0.5) * (
                dqn - q * (scale * scale) * jnp.sum(q * dqn, axis=-1, keepdims=True)))
        own, other = in_order(sc_ref, *results)
        dq_ref[:, lanes] = own.astype(BF16)
        dqx_ref[:, lanes] = other.astype(BF16)


def late_kernel(keys, sc_ref, ko_ref, lo_ref, ro_ref, kx_ref, lx_ref, rx_ref, t_ref, u_ref, a_ref, s_ref, ss_ref,
                l_ref, gs_ref, dkn_ref, du_ref,
                dk_ref, dv_ref, dkx_ref, dvx_ref):
    row, col = grid_index()
    strict = row > col
    tables = decay_tables(sc_ref, lo_ref, ro_ref, lx_ref, rx_ref, row, col)
    ks = per_head(sc_ref, keys, ko_ref, kx_ref)
    scales = [unit(k) for k in ks]
    kns = [(k * scale).astype(BF16) for k, scale in zip(ks, scales)]
    cols, rates, withins, leavings = [], [], [], []
    for n, (sub, block, kb) in enumerate(units(keys)):
        cum_t, cum, beta = tables[block]
        h = first_head(sc_ref, keys) + sub
        cols.append(column(cum, h))
        rates.append(column(beta, h))
        withins.append(decay_within(cols[n], as_row(cum_t, h), strict) * (-rates[n]))
    for sub in range(2 * keys):
        last = l_ref[sub]
        fade = jnp.exp(cols[2 * sub + 1][T - 1:, :])
        leavings.append((gs_ref[sub].astype(F32) + fade * last.astype(F32)
                         - dot1(last, a_ref[2 * sub + 1], NT)).astype(BF16))
        leavings.append(last)
    fades = [jnp.exp(c[T - 1:, :] - c) for c in cols]
    dus = [du_ref[n] + fades[n] * dot1(kns[kb], leavings[n], NT)
           for n, (sub, block, kb) in enumerate(units(keys))]
    dxs = [dot1(t_ref[n], dus[n], TN) for n in range(4 * keys)]
    dx_bs = [dx.astype(BF16) for dx in dxs]
    d_inters = [dot1(dx_bs[n], u_ref[n], NT) * withins[n] for n in range(4 * keys)]
    dkns = []
    for n, (sub, block, kb) in enumerate(units(keys)):
        state = s_ref[sub] if block == 0 else ss_ref[sub]
        dkns.append(dot1(d_inters[n] + d_inters[n].T, kns[kb])
                    + fades[n] * dot1(u_ref[n], leavings[n])
                    - (rates[n] * jnp.exp(cols[n])) * dot1(dx_bs[n], state))
    for key in range(keys):
        lanes = slice(key * DK, (key + 1) * DK)
        results = []
        for block in range(2):
            n, kb = 4 * key + block, 2 * key + block
            k, scale = ks[kb], scales[kb]
            dkn = dkn_ref[block, :, lanes] + dkns[n] + dkns[n + 2]
            results.append(
                scale * (dkn - k * (scale * scale) * jnp.sum(k * dkn, axis=-1, keepdims=True)))
        own, other = in_order(sc_ref, *results)
        dk_ref[:, lanes] = own.astype(BF16)
        dkx_ref[:, lanes] = other.astype(BF16)
    for sub in range(2 * keys):
        lanes = slice(sub * DV, (sub + 1) * DV)
        f, s = 2 * sub, 2 * sub + 1
        own, other = in_order(sc_ref, rates[f] * dxs[f], rates[s] * dxs[s])
        dv_ref[:, lanes] = own.astype(BF16)
        dvx_ref[:, lanes] = other.astype(BF16)


HEADS = VALUE_HEADS // 2
KEYS = HK // 2
PARAMS = pltpu.CompilerParams(vmem_limit_bytes=64 << 20)


def shape(dims, dtype=BF16):
    return jax.ShapeDtypeStruct(dims, dtype)


def block(dims, place):
    return pl.BlockSpec(dims, place)


def own(keys, width):
    return block((T, keys * width), lambda i, sc: (0, KEYS // keys * sc[0] + i))


def other(keys, width):
    return block((T, keys * width), lambda i, sc: (0, i))


def leading(count):
    return block((count, T, DK), lambda i, sc: (i, 0, 0))


TABLE = block((VALUE_HEADS, T), lambda i, sc: (0, 0))
SLICE = block((T, 4 * DV), lambda i, sc: (0, 0))
UNIT_SHAPE, PAIR_SHAPE = (2 * HEADS, T, DK), (HEADS, T, DK)


def cost(gflops):
    return pl.CostEstimate(flops=int(gflops * 1e9), bytes_accessed=1 << 16, transcendentals=0)


def per_key(kernel, name, gflops, keys, in_specs, out_specs, out_shape):
    return pl.pallas_call(
        functools.partial(kernel, keys),
        grid_spec=pltpu.PrefetchScalarGridSpec(
            num_scalar_prefetch=1, grid=(KEYS // keys,), in_specs=in_specs, out_specs=out_specs),
        out_shape=out_shape,
        compiler_params=PARAMS,
        cost_estimate=cost(gflops),
        name=name,
    )


ROWS = DK + HALF + TAIL
write_local = per_key(
    write_kernel, "write_local", 18, 2,
    [own(2, DK), own(2, 2 * DV), TABLE, TABLE, own(2, DK), own(2, 2 * DV), TABLE, TABLE],
    [block((8, ROWS, DK), lambda i, sc: (i, 0, 0)), leading(8), leading(8), leading(8), leading(8), leading(4)],
    [shape((2 * HEADS, ROWS, DK)), shape(UNIT_SHAPE), shape(UNIT_SHAPE), shape(UNIT_SHAPE),
     shape(UNIT_SHAPE), shape(PAIR_SHAPE)])
read_local = per_key(
    read_kernel, "read_local", 0.01, 2,
    [own(2, DK), own(2, DK), TABLE, TABLE, own(2, DK), own(2, DK), TABLE, TABLE, leading(8), leading(8)],
    [leading(8)] * 3,
    [shape(UNIT_SHAPE)] * 3)
gate_local = per_key(
    gate_kernel, "gate_local", 12, 2,
    [leading(4), own(2, 2 * DV), TABLE, TABLE, own(2, 2 * DV), TABLE, TABLE, other(2, 2 * DV), other(2, 2 * DV), leading(8), leading(4)]
    + [leading(8)] * 5 + [own(2, DK)] * 4,
    [SLICE] * 4 + [other(2, 2 * DV), other(2, 2 * DV), own(2, 2 * DV), other(2, 2 * DV), leading(8)] + [leading(4)] * 3
    + [own(2, DK), other(2, DK), block((2, T, 2 * DK), lambda i, sc: (0, 0, i)), leading(8)],
    [shape((T, 4 * DV))] * 4 + [shape((T, HEADS * DV))] * 2
    + [shape((T, VALUE_HEADS * DV)), shape((T, HEADS * DV)), shape(UNIT_SHAPE)]
    + [shape(PAIR_SHAPE)] * 3
    + [shape((T, HK * DK)), shape((T, KEYS * DK)), shape((2, T, KEYS * DK), F32),
       shape(UNIT_SHAPE)])
late_local = per_key(
    late_kernel, "late_local", 50, 2,
    [own(2, DK), TABLE, TABLE, own(2, DK), TABLE, TABLE, leading(8), leading(8), leading(8), leading(4), leading(4), leading(4), leading(4), block((2, T, 2 * DK), lambda i, sc: (0, 0, i)), leading(8)],
    [own(2, DK), own(2, 2 * DV), other(2, DK), other(2, 2 * DV)],
    [shape((T, HK * DK)), shape((T, VALUE_HEADS * DV)), shape((T, KEYS * DK)),
     shape((T, HEADS * DV))])


STREAMS = 4


def chain_step(ab_ref, i, state, dims, added):
    tail = ab_ref[i, DK + HALF:, :].astype(F32)
    decay = jnp.exp(jnp.sum(tail, axis=0, keepdims=True))
    high, low = split(state)
    moved = dot1(jnp.concatenate([high, low], axis=0), ab_ref[i, 0:DK, :], dims)
    return decay * state - (moved[:HALF] + moved[HALF:]) + added.astype(F32)


def chain_up_kernel(*refs):
    count = refs[0].shape[0]
    state = jnp.zeros((HALF, DK), F32)
    for i in range(STREAMS * count):
        refs[-1][i] = state.astype(BF16)
        ab_ref, n = refs[i // count], i % count
        state = chain_step(ab_ref, n, state, NN, ab_ref[n, DK:DK + HALF, :])


def chain_down_kernel(*refs):
    count = refs[0].shape[0]
    state = jnp.zeros((HALF, DK), F32)
    for i in reversed(range(STREAMS * count)):
        refs[-1][i] = state.astype(BF16)
        state = chain_step(refs[i // count], i % count, state, NT, refs[STREAMS][i])


def chain(kernel, ab, *args):
    count = ab.shape[0]
    streams = [block((count // STREAMS,) + ab.shape[1:], lambda i, n=n: (n, 0, 0))
               for n in range(STREAMS)]
    whole = block((count, HALF, DK), lambda i: (0, 0, 0))
    return pl.pallas_call(
        kernel,
        grid=(1,),
        in_specs=streams + [whole] * len(args),
        out_specs=whole,
        out_shape=shape((count, HALF, DK)),
        compiler_params=PARAMS,
        cost_estimate=cost(0.01),
        name="chain",
    )(*[ab] * STREAMS, *args)


def scale_kernel(sc_ref, lengths_ref, pairing_ref, ratio_ref, cot_ref, scaled_ref):
    own = sc_ref[1]
    tokens = cot_ref.shape[0]
    start = sc_ref[2] * T + pl.program_id(0) * tokens
    weight = jnp.zeros((8, 128), F32)
    for pair in range(pairing_ref.shape[0] // 2):
        chosen, rejected = pairing_ref[2 * pair], pairing_ref[2 * pair + 1]
        ratio_c = jnp.full((8, 128), ratio_ref[chosen], F32)
        ratio_r = jnp.full((8, 128), ratio_ref[rejected], F32)
        up_c, up_r = jnp.exp(ratio_c), jnp.exp(ratio_r)
        margin = CHI_BETA * (up_c + ratio_c - up_r - ratio_r)
        pull = CHI_BETA / (1.0 + jnp.exp(margin))
        weight = weight + jnp.where(chosen == own, -pull * (up_c + 1.0), 0.0)
        weight = weight + jnp.where(rejected == own, pull * (up_r + 1.0), 0.0)
    position = start + lax.broadcasted_iota(jnp.int32, (tokens, 1), 0)
    live = (position < lengths_ref[own]).astype(F32)
    factor = weight[0:1, 0:1] * live
    scaled_ref[...] = (cot_ref[...].astype(F32) * factor).astype(BF16)


def scale_local(sc, lengths, pairing, ratio, cot, steps=2):
    scalars = pl.BlockSpec(memory_space=pltpu.SMEM)
    rows = block((T // steps,) + cot.shape[1:], lambda i, sc: (i, 0))
    return pl.pallas_call(
        scale_kernel,
        grid_spec=pltpu.PrefetchScalarGridSpec(
            num_scalar_prefetch=1,
            grid=(steps,),
            in_specs=[scalars] * 3 + [rows],
            out_specs=rows,
        ),
        out_shape=shape(cot.shape),
        compiler_params=PARAMS,
        cost_estimate=cost(0.01),
        name="scale_local",
    )(sc, lengths, pairing, ratio, cot)


def turn(sc_ref):
    core, me = sc_ref[0], sc_ref[1]
    return (2 * (me % 2) + core) ^ me


def back_kernel(sc_ref, own_ref, other_ref, *refs):
    bo_ref, bx_ref = refs[8:]
    scaled = jnp.concatenate([own_ref[...], other_ref[...]], axis=0)
    first = pl.program_id(0) < 2
    weight = jnp.concatenate(
        [jnp.where(first, refs[n][...], refs[4 + n][...]) for n in range(4)], axis=1)
    product = dot1(scaled, weight, NT).astype(BF16)
    bo_ref[...] = product[:T]
    bx_ref[...] = product[T:]


def back_local(sc, own, other, weights):
    features, columns = weights[0].shape
    width, part = features // 2, columns // 4
    tokens = block((T, columns), lambda i, sc: (0, 0))
    out = block((T, width), lambda i, sc: (0, 2 * ((i // 2) ^ (sc[1] % 2)) + i % 2))
    early = [block((width, part), lambda i, sc, n=n: (jnp.minimum(i, 1), n)) for n in range(4)]
    late = [block((width, part), lambda i, sc, n=n: (jnp.maximum(i - 2, 0), n)) for n in range(4)]
    return pl.pallas_call(
        back_kernel,
        grid_spec=pltpu.PrefetchScalarGridSpec(
            num_scalar_prefetch=1,
            grid=(4,),
            in_specs=[tokens, tokens] + early + late,
            out_specs=[out, out],
        ),
        out_shape=[shape((T, 2 * features))] * 2,
        compiler_params=PARAMS,
        cost_estimate=cost(0.01),
        name="back_local",
    )(sc, own, other, *[weights[0]] * 4, *[weights[1]] * 4)


def mixed_kernel(sc_ref, no_ref, nx_ref, *refs):
    own_ref, other_ref = refs[8:]
    features = 4 * refs[0].shape[0]
    odd = sc_ref[1] % 2
    first = pl.ds(pl.multiple_of(odd * features, features), features)
    second = pl.ds(pl.multiple_of((1 - odd) * features, features), features)
    weights = [jnp.concatenate([ref[...] for ref in refs[4 * n:4 * n + 4]], axis=0)
               for n in range(2)]
    product = (dot1(jnp.concatenate([no_ref[:, first], nx_ref[:, first]], axis=0), weights[0])
               + dot1(jnp.concatenate([no_ref[:, second], nx_ref[:, second]], axis=0), weights[1]))
    own_ref[...] = product[:T]
    other_ref[...] = product[T:].astype(BF16)


def mixed_local(sc, own, other, weights, width=512):
    features, columns = weights[0].shape
    tokens = block((T, 2 * features), lambda i, sc: (0, 0))
    rows = [block((features // 4, width), lambda i, sc, n=n: (n, i)) for n in range(4)]
    out = block((T, width), lambda i, sc: (0, i))
    return pl.pallas_call(
        mixed_kernel,
        grid_spec=pltpu.PrefetchScalarGridSpec(
            num_scalar_prefetch=1,
            grid=(columns // width,),
            in_specs=[tokens, tokens] + rows + rows,
            out_specs=[out, out],
        ),
        out_shape=[shape((T, columns), F32), shape((T, columns))],
        compiler_params=PARAMS,
        cost_estimate=cost(0.01),
        name="mixed_local",
    )(sc, own, other, *[weights[0]] * 4, *[weights[1]] * 4)


def weight_kernel(sc_ref, *refs):
    keep_ref, send_ref, rows_ref, part_ref, sems = refs[8:]
    for n in range(4):
        rows_ref[n ^ turn(sc_ref)] = refs[n][...]
    rows = rows_ref[...].reshape(4 * T, rows_ref.shape[2])
    chips, cores, height, columns = part_ref.shape
    width, some = columns // 4, chips // 2
    core = lax.axis_index("ctx") % 2
    copies = []
    for n in range(4):
        lanes = slice(n * width, (n + 1) * width)
        scaled = jnp.concatenate([ref[:, lanes] for ref in refs[4:8]], axis=0)
        part_ref[:, :, :, lanes] = dot1(rows, scaled, TN).astype(BF16).reshape(
            chips, cores, height, width)
        for m in range(2):
            group, lane = pl.ds(m * some, some), pl.ds(n * width, width)
            for to_ref, row in ((keep_ref, core), (send_ref, 1 - core)):
                copies.append(pltpu.make_async_copy(
                    part_ref.at[group, row, :, lane], to_ref.at[group, :, lane],
                    sems.at[len(copies)]))
                copies[-1].start()
    for copy in copies:
        copy.wait()


def weight_local(sc, rows, scaled):
    features, columns = rows[0].shape[1], scaled[0].shape[1]
    same = lambda part: block(part.shape, lambda i, sc: (0, 0))
    return pl.pallas_call(
        weight_kernel,
        grid_spec=pltpu.PrefetchScalarGridSpec(
            num_scalar_prefetch=1,
            grid=(1,),
            in_specs=[same(part) for part in rows + scaled],
            out_specs=[pl.BlockSpec(memory_space=pl.ANY)] * 2,
            scratch_shapes=[pltpu.VMEM((4, T, features), BF16),
                            pltpu.VMEM((features // 32, 2, 16, columns), BF16),
                            pltpu.SemaphoreType.DMA((16,))],
        ),
        out_shape=[shape((features // 32, 16, columns))] * 2,
        compiler_params=PARAMS,
        cost_estimate=cost(4),
        name="weight_local",
    )(sc, *rows, *scaled)


def join_kernel(*refs):
    for n in range(2):
        refs[4][4 * n:4 * n + 4] = (
            refs[n][...].astype(F32) + refs[2 + n][...].astype(F32)).astype(BF16)


def join(a, b):
    streams = [block((4,) + a.shape[1:], lambda i, n=n: (2 * i + n, 0, 0)) for n in range(2)]
    return pl.pallas_call(
        join_kernel,
        grid=(a.shape[0] // 8,),
        in_specs=streams * 2,
        out_specs=block((8,) + a.shape[1:], lambda i: (i, 0, 0)),
        out_shape=shape(a.shape),
        compiler_params=PARAMS,
        cost_estimate=cost(0.01),
        name="join",
    )(a, a, b, b)


def total_kernel(*refs):
    refs[-1][...] = functools.reduce(
        lambda a, b: a + b, [jnp.sum(ref[...].astype(F32), axis=0) for ref in refs[:-1]])


def total(parts, streams=8):
    count, rows, columns = parts.shape
    return pl.pallas_call(
        total_kernel,
        grid=(1,),
        in_specs=[block((count // streams, rows, columns), lambda i, n=n: (n, 0, 0))
                  for n in range(streams)],
        out_specs=block((rows, columns), lambda i: (0, 0)),
        out_shape=shape((rows, columns), F32),
        compiler_params=PARAMS,
        cost_estimate=cost(0.01),
        name="total",
    )(*[parts] * streams)


def fill_kernel(sc_ref, *refs):
    count = len(refs) // 3
    for part_ref, out_ref in zip(refs[count:2 * count], refs[2 * count:]):
        out_ref[...] = part_ref[...]


def fill(sc, wholes, parts):
    count = len(wholes)
    return pl.pallas_call(
        fill_kernel,
        grid_spec=pltpu.PrefetchScalarGridSpec(
            num_scalar_prefetch=1,
            grid=(1,),
            in_specs=[pl.BlockSpec(memory_space=pl.ANY)] * count
            + [block(part.shape, lambda i, sc: (0, 0)) for part in parts],
            out_specs=[block(part.shape, lambda i, sc: (0, 1 - sc[0])) for part in parts],
        ),
        out_shape=[shape(whole.shape) for whole in wholes],
        input_output_aliases={1 + n: n for n in range(count)},
        compiler_params=PARAMS,
        cost_estimate=cost(0.01),
        name="fill",
    )(sc, *wholes, *parts)


def sum_kernel(a_ref, b_ref, c_ref, out_ref):
    width = a_ref.shape[1]
    out_ref[:, :width] = (a_ref[...] + c_ref[:, :width].astype(F32)).astype(BF16)
    out_ref[:, width:] = (b_ref[...] + c_ref[:, width:].astype(F32)).astype(BF16)


def sum_shares(own, other, steps=2):
    rows, columns = own.shape
    part = columns // (2 * steps)
    halves = [block((rows, part), lambda i, n=n: (0, 2 * i + n)) for n in range(2)]
    whole = block((rows, 2 * part), lambda i: (0, i))
    return pl.pallas_call(
        sum_kernel,
        grid=(steps,),
        in_specs=halves + [whole],
        out_specs=whole,
        out_shape=shape(own.shape),
        compiler_params=PARAMS,
        cost_estimate=cost(0.01),
        name="sum_shares",
    )(own, own, other)


def exchange(x):
    count = lax.axis_size("ctx")
    groups = [list(range(core, count, 2)) for core in range(2)]
    return lax.all_to_all(x, "ctx", split_axis=0, concat_axis=0, tiled=True,
                          axis_index_groups=groups)


def cross(x, axis, distance):
    count = lax.axis_size(axis)
    return lax.ppermute(x, axis, [(i, i ^ distance) for i in range(count)])


def sibling(x):
    return cross(x, "ctx", 1)


def tie(*values):
    return lax.optimization_barrier(values)


def place_of(z, chip, core, chips):
    return (z * chips + chip) * 2 + core


def feature_round(x, n, seqs):
    chips = lax.axis_size("ctx") // 2
    pairs = [(place_of(z, chip, core, chips),
              place_of(2 * core + (z ^ n) // 2, chip, (z ^ n) % 2, chips))
             for z in range(seqs) for chip in range(chips) for core in range(2)]
    return lax.ppermute(x, ("fsdp", "ctx"), pairs)


def weight_round(x, n, seqs):
    chips = lax.axis_size("ctx") // 2
    pairs = [(place_of(2 * core + (z ^ n) % 2, chip, 1 - z // 2, chips),
              place_of(z, chip, core, chips))
             for z in range(seqs) for chip in range(chips) for core in range(2)]
    return lax.ppermute(x, ("fsdp", "ctx"), pairs)


def body(query_vectors, key_vectors, value_vectors, output_gate, log_decay, write_rate,
         out_weight, cotangent, lengths, pairing, log_ratio):
    q, k, v, gate = query_vectors[0], key_vectors[0], value_vectors[0], output_gate[0]
    spot = lax.axis_index("ctx")
    core, chips = spot % 2, lax.axis_size("ctx") // 2
    me = lax.axis_index("fsdp")
    seqs = lax.axis_size("fsdp")
    sc = jnp.stack([core, me, spot])

    with jax.named_scope("swap_heads"):
        ld, be = log_decay[0].T, write_rate[0].T
        k_x, v_x, ld_x, be_x = (sibling(part) for part in (k, v, ld, be))
    with jax.named_scope("out_weight"):
        heads_weight = [weight_round(out_weight, n, seqs) for n in range(2)]
    ab, t, u0, kg, a, b = write_local(sc, k, v, ld, be, k_x, v_x, ld_x, be_x)
    with jax.named_scope("every_scaled"):
        cotangent = tie(ab, cotangent)[1]
        scaled = scale_local(sc, lengths, pairing, log_ratio, cotangent[0])
    with jax.named_scope("swap_heads"):
        q_x, gate_x, scaled_x = sibling(q), sibling(gate), sibling(scaled)
    ab = exchange(ab)
    p, r, io = read_local(sc, q, k, ld, be, q_x, k_x, ld_x, be_x, u0, kg)
    ab, p, r, io, scaled = tie(ab, p, r, io, scaled)
    states = chain(chain_up_kernel, ab)
    entering = exchange(states).reshape(PAIR_SHAPE)
    with jax.named_scope("back_grad"):
        bg = back_local(sc, scaled, scaled_x, heads_weight)
    with jax.named_scope("every_scaled"):
        own_scaled = tie(heads_weight[0], heads_weight[1], scaled)[2]
        every_scaled = [scaled] + [cross(own_scaled, "fsdp", s) for s in range(1, seqs)]
    *rows, normed, normed_x, gate_grad, gate_grad_x, u, second, g, gs, dq, dq_x, dkn, du = gate_local(
        sc, entering, gate, ld, be, gate_x, ld_x, be_x, *bg, a, b, io, u0, kg, r, p, q, k, q_x, k_x)
    g = exchange(g.reshape(2 * HEADS, HALF, DK))
    with jax.named_scope("every_normed"):
        rows = [feature_round(rows[n], n, seqs) for n in range(seqs)]
    g, *every_scaled = tie(g, *every_scaled)
    states = chain(chain_down_kernel, ab, g)
    leaving = exchange(states).reshape(PAIR_SHAPE)
    with jax.named_scope("weight_grad"):
        rows = list(tie(states, *rows)[1:])
        keep, send = weight_local(sc, rows, every_scaled)
        send = sibling(send)
    with jax.named_scope("swap_back"):
        others = [sibling(gate_grad_x), sibling(dq_x)]
    dk, dv, dk_x, dv_x = late_local(sc, k, ld, be, k_x, ld_x, be_x, t, u, a, entering, second,
                                    leaving, gs, dkn, du)
    with jax.named_scope("weight_grad"):
        dk, keep = tie(dk, keep)
        weight_grad = total(exchange(join(keep, send)))
    with jax.named_scope("mixed_out"):
        dk, normed, normed_x = tie(dk, normed, normed_x)
        mixed, mixed_x = mixed_local(sc, normed, normed_x, heads_weight)
    with jax.named_scope("swap_back"):
        gate_grad, dq, dk, dv = fill(
            sc, [gate_grad, dq, dk, dv], others + [sibling(dk_x), sibling(dv_x)])
    with jax.named_scope("mixed_out"):
        mixed = sum_shares(mixed, sibling(mixed_x))
    return mixed[None], dq[None], dk[None], dv[None], gate_grad[None], weight_grad


def solution(mesh):
    tokens = P("fsdp", "ctx", None)
    return jax.shard_map(
        body,
        mesh=mesh,
        in_specs=(tokens,) * 6 + (P("fsdp", None), tokens, P(), P(), P()),
        out_specs=(tokens,) * 5 + (P(("fsdp", "ctx"), None),),
        check_vma=False,
    )
```

time: 148 us -> 141 us (0.953)
  Pallas kernels: 77.2 us -> 63.8 us
  waiting for transfers between devices: 15.9 us -> 24 us
  starting transfers between devices: 52.4 us -> 50.3 us
    pallas_call x8, Pallas kernels: 52 us -> 39.1 us  [the longest x1 8.52 us: body(): ab, t, u0, kg, a, b = write_local(sc, k, v, ld, be, k_x, v_x, ld_x, be_x)]
    ppermute x2, waiting for transfers between devices: 0.83 us -> 6.28 us  [weight_round(): return lax.ppermute(x, ('fsdp', 'ctx'), pairs)]
    ppermute x13 -> x16, waiting for transfers between devices: 1.67 us -> 5.15 us  [cross(): return lax.ppermute(x, axis, [(i, i ^ distance) for i in range(count)])]
    all_to_all x5, starting transfers between devices: 32.3 us -> 28.9 us  [exchange(): lax.all_to_all(x, 'ctx', split_axis=0, concat_axis=0, tiled=True, axis_in...]
    ppermute x4, starting transfers between devices: 6.32 us -> 7.82 us  [feature_round(): return lax.ppermute(x, ('fsdp', 'ctx'), pairs)]
    ppermute x13 -> x16, starting transfers between devices: 9.56 us -> 8.28 us  [cross(): return lax.ppermute(x, axis, [(i, i ^ distance) for i in range(count)])]
  transfers between devices with their start and end apart: 24 -> 27, of which waited for: 7 -> 8; matrix products, arithmetic and copies ran while one was open for 0% -> 0% of each run, Pallas kernels for 49% -> 42%
where the time goes in v4:
time: 141 us; the launch traced here: 140 us
  Pallas kernels  63.8 us (45%)
  starting transfers between devices  50.3 us (36%)
  waiting for transfers between devices  24 us (17%)
    all_to_all x5, starting transfers between devices, exchange(): lax.all_to_all(x, 'ctx', split_axis=0, concat_axis=0, tiled=True, axis_in...  28.9 us
    all_to_all x5, waiting for transfers between devices, exchange(): lax.all_to_all(x, 'ctx', split_axis=0, concat_axis=0, tiled=True, axis_in...  12.6 us
    pallas_call x1, Pallas kernels, body(): ab, t, u0, kg, a, b = write_local(sc, k, v, ld, be, k_x, v_x, ld_x, be_x)  8.52 us
    ppermute x16, starting transfers between devices, cross(): return lax.ppermute(x, axis, [(i, i ^ distance) for i in range(count)])  8.28 us
    pallas_call x1, Pallas kernels, body(): gate_local(sc, entering, gate, ld, be, gate_x, ld_x, be_x, *bg, a, b, io,...  7.96 us
    pallas_call x2, Pallas kernels, chain(): pl.pallas_call(kernel, grid=(1,), in_specs=streams + [whole] * len(args),...  7.85 us
    ppermute x4, starting transfers between devices, feature_round(): return lax.ppermute(x, ('fsdp', 'ctx'), pairs)  7.82 us
    ppermute x2, waiting for transfers between devices, weight_round(): return lax.ppermute(x, ('fsdp', 'ctx'), pairs)  6.28 us
  transfers between devices with their start and end apart: 27, of which 8 were waited for; matrix products, arithmetic and copies ran while one was open for 0% of the time, Pallas kernels for 42%

profile of v4, /device:TPU:0, one launch (start us, length us, event | category | flops | bytes accessed | tf_op | source)
XLA Modules:
  0.0 139.5 jit_solution(13628075945795934937)
XLA Ops:
  0.6 0.1 collective-permute-start.3
  0.7 0.5 collective-permute-start
  1.2 0.1 collective-permute-start.1
  1.3 0.4 collective-permute-start.2
  1.7 4.1 %collective-permute-start.8 = (bf16[512,2048]{1,0:T(8,128)(2,1)}, bf16[512,2048]{1,0:T(8,128)(2,1)}, u32[]{:S(2)}, u32[]{:S(2)}) collective-permute-start(bf16[512,2048]{1,0:T(8,128)(2,1)} %param.17), channel_id=1, source_target_pairs={{33,0},{97,1},{35,2},{99,3},{37,4},{101,5},{39,6},{103,7},{41,8},{... | collective-permute-start | bytes 6291464 | tf_op jit(solution)/shard_map/out_weight/ppermute | solution.py:766
  5.9 0.6 pad_add_fusion.sc_ref
  6.5 0.0 collective-permute-done.1.lx_ref
  6.5 1.2 collective-permute-start.7
  7.6 0.0 collective-permute-done.2.rx_ref
  7.6 0.0 collective-permute-done.kx_ref
  7.6 0.0 collective-permute-done.3.vx_ref
  7.6 8.5 %write_local.1 = (bf16[16,208,128]{2,1,0:T(8,128)(2,1)}, bf16[16,128,128]{2,1,0:T(8,128)(2,1)}, bf16[16,128,128]{2,1,0:T(8,128)(2,1)}, bf16[16,128,128]{2,1,0:T(...) custom-call(s32[3]{0:T(128)} %pad_add_fusion.sc_ref, bf16[128,1024]{1,0:T(8,128)(2,1)} %bitcast.30, ...), custom_call_target="tpu_custom_call" | custom-call | flops 17999998976 | bytes 65536 | tf_op jit(solution)/shard_map/write_local/pallas_call | solution.py:783
  16.2 7.1 %all-to-all-start = ((bf16[16,208,128]{2,1,0:T(8,128)(2,1)}), bf16[16,208,128]{2,1,0:T(8,128)(2,1)}, u32[]{:S(2)}, u32[]{:S(2)}) async-start(bf16[16,208,128]{2,1,0:T(8,128)(2,1)} %get-tuple-element.67), calls=%async_computation | async-start | bytes 1703936 | tf_op jit(solution)/shard_map/all_to_all | solution.py:732
  23.3 2.6 %scale_local.1.own_ref.refs_4_ = bf16[128,2048]{1,0:T(8,128)(2,1)} custom-call(s32[3]{0:T(128)} %pad_add_fusion.sc_ref, s32[4]{0:T(128)} %lengths_ref.1, s32[4]{0:T(128)} %pairing_ref.1, f32[4]{0:T(128)} %ratio_ref.1, bf16[128,2048]{1,0:T(8,128)(2,1)} %bitcast.24), custom_call_target="tpu_custom_call" | custom-call | flops 10000000 | bytes 65536 | tf_op jit(solution)/shard_map/every_scaled/scale_local/pallas_call | solution.py:508
  25.8 0.0 collective-permute-start.6
  25.8 0.5 collective-permute-start.5
  26.3 0.0 collective-permute-start.4
  26.3 2.9 %collective-permute-done.4.qx_ref = bf16[128,1024]{1,0:T(8,128)(2,1)} collective-permute-done((bf16[128,1024]{1,0:T(8,128)(2,1)}, bf16[128,1024]{1,0:T(8,128)(2,1)}, u32[]{:S(2)}, u32[]{:S(2)}) %collective-permute-start.4) | collective-permute-done | bytes 262176 | tf_op jit(solution)/shard_map/swap_heads/ppermute | solution.py:738
  29.2 4.1 %read_local.1 = (bf16[16,128,128]{2,1,0:T(8,128)(2,1)}, bf16[16,128,128]{2,1,0:T(8,128)(2,1)}, bf16[16,128,128]{2,1,0:T(8,128)(2,1)}) custom-call(s32[3]{0:T(128)} %pad_add_fusion.sc_ref, bf16[128,1024]{1,0:T(8,128)(2,1)} %bitcast.27, bf16[128,1024]{1,0:T(8,128)(2,1)} %bitcast.31, f32[16,128]{1,0:T(8,128)} %bitcast.39, f32[16,128]{1,0:T(8,128)} %bitcast.44, ...), custom_call_target="tpu_custom_call" | custom-call | flops 10000000 | bytes 65536 | tf_op jit(solution)/shard_map/read_local/pallas_call | solution.py:790
  33.3 4.6 %all-to-all-done.refs_0_.refs_1_.refs_2_.refs_3_ = bf16[16,208,128]{2,1,0:T(8,128)(2,1)} async-done(((bf16[16,208,128]{2,1,0:T(8,128)(2,1)}), bf16[16,208,128]{2,1,0:T(8,128)(2,1)}, u32[]{:S(2)}, u32[]{:S(2)}) %all-to-all-start) | async-done | bytes 852000 | tf_op jit(solution)/shard_map/all_to_all | solution.py:732
  37.8 3.9 %chain.2 = bf16[16,64,128]{2,1,0:T(8,128)(2,1)} custom-call(bf16[16,208,128]{2,1,0:T(8,128)(2,1)} %all-to-all-done.refs_0_.refs_1_.refs_2_.refs_3_, bf16[16,208,128]{2,1,0:T(8,128)(2,1)} %all-to-all-done.refs_0_.refs_1_.refs_2_.refs_3_, bf16[16,208,128]{2,1,0:T(8,128)(2,1)} %all-to-all-done.refs_0_.refs_1_.refs_2_.refs_3_, ...), custom_call_target="tpu_custom_call" | custom-call | flops 10000000 | bytes 65536 | tf_op jit(solution)/shard_map/chain/pallas_call | solution.py:473
  41.7 4.2 %all-to-all-start.1 = ((bf16[16,64,128]{2,1,0:T(8,128)(2,1)}), bf16[16,64,128]{2,1,0:T(8,128)(2,1)}, u32[]{:S(2)}, u32[]{:S(2)}) async-start(bf16[16,64,128]{2,1,0:T(8,128)(2,1)} %chain.2), calls=%async_computation.1 | async-start | bytes 524288 | tf_op jit(solution)/shard_map/all_to_all | solution.py:732
  45.9 6.3 %collective-permute-done.8.refs_4_.refs_5_.refs_6_.refs_7_ = bf16[512,2048]{1,0:T(8,128)(2,1)} collective-permute-done((bf16[512,2048]{1,0:T(8,128)(2,1)}, bf16[512,2048]{1,0:T(8,128)(2,1)}, u32[]{:S(2)}, u32[]{:S(2)}) %collective-permute-start.8) | collective-permute-done | bytes 2097184 | tf_op jit(solution)/shard_map/out_weight/ppermute | solution.py:766
  52.2 0.0 collective-permute-done.7.refs_0_.refs_1_.refs_2_.refs_3_
  52.2 3.7 %collective-permute-start.11 = (bf16[128,2048]{1,0:T(8,128)(2,1)}, bf16[128,2048]{1,0:T(8,128)(2,1)}, u32[]{:S(2)}, u32[]{:S(2)}) collective-permute-start(bf16[128,2048]{1,0:T(8,128)(2,1)} %scale_local.1.own_ref.refs_4_), channel_id=1, source_target_pairs={{0,96},{32,64},{64,32},{96,0},{1,97},{33,65},{65,33},{97,1},{2,98}... | collective-permute-start | bytes 1572872 | tf_op jit(solution)/shard_map/every_scaled/ppermute | solution.py:738
  55.9 0.0 collective-permute-start.10
  55.9 0.9 collective-permute-start.9
  56.8 0.0 collective-permute-done.6.other_ref
  56.8 6.3 %back_local.1 = (bf16[128,1024]{1,0:T(8,128)(2,1)}, bf16[128,1024]{1,0:T(8,128)(2,1)}) custom-call(s32[3]{0:T(128)} %pad_add_fusion.sc_ref, bf16[128,2048]{1,0:T(8,128)(2,1)} %scale_local.1.own_ref.refs_4_, bf16[128,2048]{1,0:T(8,128)(2,1)} %collective-permute-done.6.other_ref, bf16[512,2048]{1,0:T(8,128)(2,1)} %collective-permute-done.7.refs_0_.refs_1_.refs_2_.refs_3_, ...), custom_call_target="tpu_custom_call" | custom-call | flops 10000000 | bytes 65536 | tf_op jit(solution)/shard_map/back_grad/back_local/pallas_call | solution.py:546
  63.0 0.0 collective-permute-done.5.gx_ref
  63.0 0.0 all-to-all-done.1
  63.0 8.0 %gate_local.1 = (bf16[128,512]{1,0:T(8,128)(2,1)}, bf16[128,512]{1,0:T(8,128)(2,1)}, bf16[128,512]{1,0:T(8,128)(2,1)}, bf16[128,512]{1,0:T(8,128)(2,1)}, bf16[12...) custom-call(s32[3]{0:T(128)} %pad_add_fusion.sc_ref, ...), custom_call_target="tpu_custom_call" | custom-call | flops 12000000000 | bytes 65536 | tf_op jit(solution)/shard_map/gate_local/pallas_call | solution.py:799
  71.0 7.1 %all-to-all-start.2 = ((bf16[16,64,128]{2,1,0:T(8,128)(2,1)}), bf16[16,64,128]{2,1,0:T(8,128)(2,1)}, u32[]{:S(2)}, u32[]{:S(2)}) async-start(bf16[16,64,128]{2,1,0:T(8,128)(2,1)} %bitcast.36), calls=%async_computation.2 | async-start | bytes 524288 | tf_op jit(solution)/shard_map/all_to_all | solution.py:732
  78.1 2.2 %collective-permute-start.12 = (bf16[128,512]{1,0:T(8,128)(2,1)}, bf16[128,512]{1,0:T(8,128)(2,1)}, u32[]{:S(2)}, u32[]{:S(2)}) collective-permute-start(bf16[128,512]{1,0:T(8,128)(2,1)} %get-tuple-element.92), channel_id=1, source_target_pairs={{0,0},{1,64},{2,2},{3,66},{4,4},{5,68},{6,6},{7,70},{8,8},{9,72},{... | collective-permute-start | bytes 393224 | tf_op jit(solution)/shard_map/every_normed/ppermute | solution.py:758
  80.3 2.6 %collective-permute-start.13 = (bf16[128,512]{1,0:T(8,128)(2,1)}, bf16[128,512]{1,0:T(8,128)(2,1)}, u32[]{:S(2)}, u32[]{:S(2)}) collective-permute-start(bf16[128,512]{1,0:T(8,128)(2,1)} %get-tuple-element.93), channel_id=1, source_target_pairs={{0,1},{1,65},{2,3},{3,67},{4,5},{5,69},{6,7},{7,71},{8,9},{9,73},{... | collective-permute-start | bytes 393224 | tf_op jit(solution)/shard_map/every_normed/ppermute | solution.py:758
  82.9 0.0 collective-permute-done.11.refs_7_
  82.9 0.0 collective-permute-start.14
  82.9 0.0 collective-permute-done.10.refs_6_
  82.9 3.0 %collective-permute-start.15 = (bf16[128,512]{1,0:T(8,128)(2,1)}, bf16[128,512]{1,0:T(8,128)(2,1)}, u32[]{:S(2)}, u32[]{:S(2)}) collective-permute-start(bf16[128,512]{1,0:T(8,128)(2,1)} %get-tuple-element.95), channel_id=1, source_target_pairs={{0,33},{1,97},{2,35},{3,99},{4,37},{5,101},{6,39},{7,103},{8,41},{... | collective-permute-start | bytes 393224 | tf_op jit(solution)/shard_map/every_normed/ppermute | solution.py:758
  85.9 1.0 all-to-all-done.2.refs_4_
  87.0 4.0 %chain.3 = bf16[16,64,128]{2,1,0:T(8,128)(2,1)} custom-call(bf16[16,208,128]{2,1,0:T(8,128)(2,1)} %all-to-all-done.refs_0_.refs_1_.refs_2_.refs_3_, bf16[16,208,128]{2,1,0:T(8,128)(2,1)} %all-to-all-done.refs_0_.refs_1_.refs_2_.refs_3_, bf16[16,208,128]{2,1,0:T(8,128)(2,1)} %all-to-all-done.refs_0_.refs_1_.refs_2_.refs_3_, ...), custom_call_target="tpu_custom_call" | custom-call | flops 10000000 | bytes 65536 | tf_op jit(solution)/shard_map/chain/pallas_call | solution.py:473
  90.9 6.2 %all-to-all-start.3 = ((bf16[16,64,128]{2,1,0:T(8,128)(2,1)}), bf16[16,64,128]{2,1,0:T(8,128)(2,1)}, u32[]{:S(2)}, u32[]{:S(2)}) async-start(bf16[16,64,128]{2,1,0:T(8,128)(2,1)} %chain.3), calls=%async_computation.3 | async-start | bytes 524288 | tf_op jit(solution)/shard_map/all_to_all | solution.py:732
  97.2 0.0 collective-permute-done.13.refs_1_
  97.2 0.0 collective-permute-done.14.refs_2_
  97.2 5.2 %weight_local.1 = (bf16[16,16,2048]{2,1,0:T(8,128)(2,1)}, bf16[16,16,2048]{2,1,0:T(8,128)(2,1)}) custom-call(s32[3]{0:T(128)} %pad_add_fusion.sc_ref, bf16[128,512]{1,0:T(8,128)(2,1)} %collective-permute-done.12.refs_0_, bf16[128,512]{1,0:T(8,128)(2,1)} %collective-permute-done.13.refs_1_, bf16[128,512]{1,0:T(8,128)(2,1)} %collective-permute-done.14.refs_2_, ...), custom_call_target="tpu_custom_call" | custom-call | flops 4000000000 | bytes 65536 | tf_op jit(solution)/shard_map/weight_grad/weight_local/pallas_call | solution.py:623
  102.4 0.9 collective-permute-start.21
  103.4 3.8 %all-to-all-done.3 = bf16[16,64,128]{2,1,0:T(8,128)(2,1)} async-done(((bf16[16,64,128]{2,1,0:T(8,128)(2,1)}), bf16[16,64,128]{2,1,0:T(8,128)(2,1)}, u32[]{:S(2)}, u32[]{:S(2)}) %all-to-all-start.3) | async-done | bytes 262176 | tf_op jit(solution)/shard_map/all_to_all | solution.py:732
  107.1 6.0 %late_local.1 = (bf16[128,1024]{1,0:T(8,128)(2,1)}, bf16[128,2048]{1,0:T(8,128)(2,1)}, bf16[128,512]{1,0:T(8,128)(2,1)}, bf16[128,1024]{1,0:T(8,128)(2,1)}) custom-call(s32[3]{0:T(128)} %pad_add_fusion.sc_ref, bf16[128,1024]{1,0:T(8,128)(2,1)} %bitcast.33, f32[16,128]{1,0:T(8,128)} %bitcast.41, f32[16,128]{1,0:T(8,128)} %bitcast.46, ...), custom_call_target="tpu_custom_call" | custom-call | flops 49999998976 | bytes 65536 | tf_op jit(solution)/shard_map/late_local/pallas_call | solution.py:813
  113.2 2.5 %join.1 = bf16[16,16,2048]{2,1,0:T(8,128)(2,1)} custom-call(bf16[16,16,2048]{2,1,0:T(8,128)(2,1)} %get-tuple-element.124.refs_0_.refs_1_, bf16[16,16,2048]{2,1,0:T(8,128)(2,1)} %get-tuple-element.124.refs_0_.refs_1_, bf16[16,16,2048]{2,1,0:T(8,128)(2,1)} %collective-permute-done.21.refs_2_.refs_3_, bf16[16,16,2048]{2,1,0:T(8,128)(2,1)} %collective-permute-done.21.refs_2_.refs_3_), custom_call_target="tpu_custom_call" | custom-call | flops 10000000 | bytes 65536 | tf_op jit(solution)/shard_map/weight_grad/join/pallas_call | solution.py:649
  115.6 4.3 %all-to-all-start.4 = ((bf16[16,16,2048]{2,1,0:T(8,128)(2,1)}), bf16[16,16,2048]{2,1,0:T(8,128)(2,1)}, u32[]{:S(2)}, u32[]{:S(2)}) async-start(bf16[16,16,2048]{2,1,0:T(8,128)(2,1)} %join.1), calls=%async_computation.4 | async-start | bytes 2097152 | tf_op jit(solution)/shard_map/weight_grad/all_to_all | solution.py:732
  120.0 5.9 %mixed_local.1 = (f32[128,2048]{1,0:T(8,128)}, bf16[128,2048]{1,0:T(8,128)(2,1)}) custom-call(s32[3]{0:T(128)} %pad_add_fusion.sc_ref, bf16[128,1024]{1,0:T(8,128)(2,1)} %get-tuple-element.108.no_ref, bf16[128,1024]{1,0:T(8,128)(2,1)} %get-tuple-element.109.nx_ref, bf16[512,2048]{1,0:T(8,128)(2,1)} %collective-permute-done.7.refs_0_.refs_1_.refs_2_.refs_3_, ...), custom_call_target="tpu_custom_call" | custom-call | flops 10000000 | bytes 65536 | tf_op jit(solution)/shard_map/mixed_out/mixed_local/pallas_call | solution.py:580
  125.9 0.1 collective-permute-start.16
  126.0 0.5 collective-permute-start.17
  126.5 0.1 collective-permute-start.20
  126.6 0.4 collective-permute-start.18
  127.0 0.1 collective-permute-start.19
  127.1 2.1 %collective-permute-done.18.refs_5_ = bf16[128,512]{1,0:T(8,128)(2,1)} collective-permute-done((bf16[128,512]{1,0:T(8,128)(2,1)}, bf16[128,512]{1,0:T(8,128)(2,1)}, u32[]{:S(2)}, u32[]{:S(2)}) %collective-permute-start.18) | collective-permute-done | bytes 131104 | tf_op jit(solution)/shard_map/swap_back/ppermute | solution.py:738
  129.2 0.2 collective-permute-done.19.refs_6_
  129.4 0.0 collective-permute-done.20.refs_7_
  129.4 2.7 %fill.1 = (bf16[128,2048]{1,0:T(8,128)(2,1)}, bf16[128,1024]{1,0:T(8,128)(2,1)}, bf16[128,1024]{1,0:T(8,128)(2,1)}, bf16[128,2048]{1,0:T(8,128)(2,1)}) custom-call(s32[3]{0:T(128)} %pad_add_fusion.sc_ref, bf16[128,2048]{1,0:T(8,128)(2,1)} %get-tuple-element.112.refs_0_, ...), custom_call_target="tpu_custom_call", output_to_operand_aliasing={{0}: (1, {}), {1}: (2, {}), {2}: (3, {}), {3}: (4, {})} | custom-call | flops 10000000 | bytes 65536 | tf_op jit(solution)/shard_map/swap_back/fill/pallas_call | solution.py:689
  132.1 0.0 collective-permute-done.16.c_ref
  132.1 2.1 %sum_shares.1 = bf16[128,2048]{1,0:T(8,128)(2,1)} custom-call(f32[128,2048]{1,0:T(8,128)} %get-tuple-element.110.a_ref.b_ref, f32[128,2048]{1,0:T(8,128)} %get-tuple-element.110.a_ref.b_ref, bf16[128,2048]{1,0:T(8,128)(2,1)} %collective-permute-done.16.c_ref), custom_call_target="tpu_custom_call" | custom-call | flops 10000000 | bytes 65536 | tf_op jit(solution)/shard_map/mixed_out/sum_shares/pallas_call | solution.py:717
  134.2 3.2 %all-to-all-done.4.refs_0_.refs_1_.refs_2_.refs_3_.refs_4_.refs_5_.refs_6_.refs_7_ = bf16[16,16,2048]{2,1,0:T(8,128)(2,1)} async-done(((bf16[16,16,2048]{2,1,0:T(8,128)(2,1)}), bf16[16,16,2048]{2,1,0:T(8,128)(2,1)}, u32[]{:S(2)}, u32[]{:S(2)}) %all-to-all-start.4) | async-done | bytes 1048608 | tf_op jit(solution)/shard_map/weight_grad/all_to_all | solution.py:732
  137.4 2.1 %total.1 = f32[16,2048]{1,0:T(8,128)} custom-call(bf16[16,16,2048]{2,1,0:T(8,128)(2,1)} %all-to-all-done.4.refs_0_.refs_1_.refs_2_.refs_3_.refs_4_.refs_5_.refs_6_.refs_7_, bf16[16,16,2048]{2,1,0:T(8,128)(2,1)} %all-to-all-done.4.refs_0_.refs_1_.refs_2_.refs_3_.refs_4_.refs_5_.refs_6_.refs_7_, ...), custom_call_target="tpu_custom_call" | custom-call | flops 10000000 | bytes 65536 | tf_op jit(solution)/shard_map/weight_grad/total/pallas_call | solution.py:668
  (5 shorter events, 0.0 us)
Async XLA Ops:
  0.6 7.0 %collective-permute-start.3 = (bf16[128,2048]{1,0:T(8,128)(2,1)}, bf16[128,2048]{1,0:T(8,128)(2,1)}, u32[]{:S(2)}, u32[]{:S(2)}) collective-permute-start(bf16[128,2048]{1,0:T(8,128)(2,1)} %bitcast.47), channel_id=1, source_target_pairs={{0,1},{1,0},{2,3},{3,2},{4,5},{5,4},{6,7},{7,6},{8,9},{9,8},{10,11... | collective-permute-start | bytes 1572872 | tf_op jit(solution)/shard_map/swap_heads/ppermute | solution.py:738
  0.7 6.9 %collective-permute-start = (bf16[128,1024]{1,0:T(8,128)(2,1)}, bf16[128,1024]{1,0:T(8,128)(2,1)}, u32[]{:S(2)}, u32[]{:S(2)}) collective-permute-start(bf16[128,1024]{1,0:T(8,128)(2,1)} %bitcast.29), channel_id=1, source_target_pairs={{0,1},{1,0},{2,3},{3,2},{4,5},{5,4},{6,7},{7,6},{8,9},{9,8},{10,11... | collective-permute-start | bytes 786440 | tf_op jit(solution)/shard_map/swap_heads/ppermute | solution.py:738
  1.2 5.2 %collective-permute-start.1 = (f32[16,128]{1,0:T(8,128)}, f32[16,128]{1,0:T(8,128)}, u32[]{:S(2)}, u32[]{:S(2)}) collective-permute-start(f32[16,128]{1,0:T(8,128)} %bitcast.37), channel_id=1, source_target_pairs={{0,1},{1,0},{2,3},{3,2},{4,5},{5,4},{6,7},{7,6},{8,9},{9,8},{10,11... | collective-permute-start | bytes 24584 | tf_op jit(solution)/shard_map/swap_heads/ppermute | solution.py:738
  1.3 6.3 %collective-permute-start.2 = (f32[16,128]{1,0:T(8,128)}, f32[16,128]{1,0:T(8,128)}, u32[]{:S(2)}, u32[]{:S(2)}) collective-permute-start(f32[16,128]{1,0:T(8,128)} %bitcast.42), channel_id=1, source_target_pairs={{0,1},{1,0},{2,3},{3,2},{4,5},{5,4},{6,7},{7,6},{8,9},{9,8},{10,11... | collective-permute-start | bytes 24584 | tf_op jit(solution)/shard_map/swap_heads/ppermute | solution.py:738
  1.7 50.5 %collective-permute-start.8 = (bf16[512,2048]{1,0:T(8,128)(2,1)}, bf16[512,2048]{1,0:T(8,128)(2,1)}, u32[]{:S(2)}, u32[]{:S(2)}) collective-permute-start(bf16[512,2048]{1,0:T(8,128)(2,1)} %param.17), channel_id=1, source_target_pairs={{33,0},{97,1},{35,2},{99,3},{37,4},{101,5},{39,6},{103,7},{41,8},{... | collective-permute-start | bytes 6291464 | tf_op jit(solution)/shard_map/out_weight/ppermute | solution.py:766
  6.5 45.7 %collective-permute-start.7 = (bf16[512,2048]{1,0:T(8,128)(2,1)}, bf16[512,2048]{1,0:T(8,128)(2,1)}, u32[]{:S(2)}, u32[]{:S(2)}) collective-permute-start(bf16[512,2048]{1,0:T(8,128)(2,1)} %param.17), channel_id=1, source_target_pairs={{1,0},{65,1},{3,2},{67,3},{5,4},{69,5},{7,6},{71,7},{9,8},{73,9},{... | collective-permute-start | bytes 6291464 | tf_op jit(solution)/shard_map/out_weight/ppermute | solution.py:766
  16.2 21.7 %all-to-all-start = ((bf16[16,208,128]{2,1,0:T(8,128)(2,1)}), bf16[16,208,128]{2,1,0:T(8,128)(2,1)}, u32[]{:S(2)}, u32[]{:S(2)}) async-start(bf16[16,208,128]{2,1,0:T(8,128)(2,1)} %get-tuple-element.67), calls=%async_computation | async-start | bytes 1703936 | tf_op jit(solution)/shard_map/all_to_all | solution.py:732
  25.8 30.9 %collective-permute-start.6 = (bf16[128,2048]{1,0:T(8,128)(2,1)}, bf16[128,2048]{1,0:T(8,128)(2,1)}, u32[]{:S(2)}, u32[]{:S(2)}) collective-permute-start(bf16[128,2048]{1,0:T(8,128)(2,1)} %scale_local.1.own_ref.refs_4_), channel_id=1, source_target_pairs={{0,1},{1,0},{2,3},{3,2},{4,5},{5,4},{6,7},{7,6},{8,9},{9,8},{10,11... | collective-permute-start | bytes 1572872 | tf_op jit(solution)/shard_map/swap_heads/ppermute | solution.py:738
  25.8 37.2 %collective-permute-start.5 = (bf16[128,2048]{1,0:T(8,128)(2,1)}, bf16[128,2048]{1,0:T(8,128)(2,1)}, u32[]{:S(2)}, u32[]{:S(2)}) collective-permute-start(bf16[128,2048]{1,0:T(8,128)(2,1)} %bitcast.49), channel_id=1, source_target_pairs={{0,1},{1,0},{2,3},{3,2},{4,5},{5,4},{6,7},{7,6},{8,9},{9,8},{10,11... | collective-permute-start | bytes 1572872 | tf_op jit(solution)/shard_map/swap_heads/ppermute | solution.py:738
  26.3 2.9 %collective-permute-start.4 = (bf16[128,1024]{1,0:T(8,128)(2,1)}, bf16[128,1024]{1,0:T(8,128)(2,1)}, u32[]{:S(2)}, u32[]{:S(2)}) collective-permute-start(bf16[128,1024]{1,0:T(8,128)(2,1)} %bitcast.26), channel_id=1, source_target_pairs={{0,1},{1,0},{2,3},{3,2},{4,5},{5,4},{6,7},{7,6},{8,9},{9,8},{10,11... | collective-permute-start | bytes 786440 | tf_op jit(solution)/shard_map/swap_heads/ppermute | solution.py:738
  41.7 21.3 %all-to-all-start.1 = ((bf16[16,64,128]{2,1,0:T(8,128)(2,1)}), bf16[16,64,128]{2,1,0:T(8,128)(2,1)}, u32[]{:S(2)}, u32[]{:S(2)}) async-start(bf16[16,64,128]{2,1,0:T(8,128)(2,1)} %chain.2), calls=%async_computation.1 | async-start | bytes 524288 | tf_op jit(solution)/shard_map/all_to_all | solution.py:732
  52.2 30.7 %collective-permute-start.11 = (bf16[128,2048]{1,0:T(8,128)(2,1)}, bf16[128,2048]{1,0:T(8,128)(2,1)}, u32[]{:S(2)}, u32[]{:S(2)}) collective-permute-start(bf16[128,2048]{1,0:T(8,128)(2,1)} %scale_local.1.own_ref.refs_4_), channel_id=1, source_target_pairs={{0,96},{32,64},{64,32},{96,0},{1,97},{33,65},{65,33},{97,1},{2,98}... | collective-permute-start | bytes 1572872 | tf_op jit(solution)/shard_map/every_scaled/ppermute | solution.py:738
  55.9 27.0 %collective-permute-start.10 = (bf16[128,2048]{1,0:T(8,128)(2,1)}, bf16[128,2048]{1,0:T(8,128)(2,1)}, u32[]{:S(2)}, u32[]{:S(2)}) collective-permute-start(bf16[128,2048]{1,0:T(8,128)(2,1)} %scale_local.1.own_ref.refs_4_), channel_id=1, source_target_pairs={{0,64},{32,96},{64,0},{96,32},{1,65},{33,97},{65,1},{97,33},{2,66}... | collective-permute-start | bytes 1572872 | tf_op jit(solution)/shard_map/every_scaled/ppermute | solution.py:738
  55.9 31.1 %collective-permute-start.9 = (bf16[128,2048]{1,0:T(8,128)(2,1)}, bf16[128,2048]{1,0:T(8,128)(2,1)}, u32[]{:S(2)}, u32[]{:S(2)}) collective-permute-start(bf16[128,2048]{1,0:T(8,128)(2,1)} %scale_local.1.own_ref.refs_4_), channel_id=1, source_target_pairs={{0,32},{32,0},{64,96},{96,64},{1,33},{33,1},{65,97},{97,65},{2,34}... | collective-permute-start | bytes 1572872 | tf_op jit(solution)/shard_map/every_scaled/ppermute | solution.py:738
  71.0 16.0 %all-to-all-start.2 = ((bf16[16,64,128]{2,1,0:T(8,128)(2,1)}), bf16[16,64,128]{2,1,0:T(8,128)(2,1)}, u32[]{:S(2)}, u32[]{:S(2)}) async-start(bf16[16,64,128]{2,1,0:T(8,128)(2,1)} %bitcast.36), calls=%async_computation.2 | async-start | bytes 524288 | tf_op jit(solution)/shard_map/all_to_all | solution.py:732
  78.1 19.1 %collective-permute-start.12 = (bf16[128,512]{1,0:T(8,128)(2,1)}, bf16[128,512]{1,0:T(8,128)(2,1)}, u32[]{:S(2)}, u32[]{:S(2)}) collective-permute-start(bf16[128,512]{1,0:T(8,128)(2,1)} %get-tuple-element.92), channel_id=1, source_target_pairs={{0,0},{1,64},{2,2},{3,66},{4,4},{5,68},{6,6},{7,70},{8,8},{9,72},{... | collective-permute-start | bytes 393224 | tf_op jit(solution)/shard_map/every_normed/ppermute | solution.py:758
  80.3 16.9 %collective-permute-start.13 = (bf16[128,512]{1,0:T(8,128)(2,1)}, bf16[128,512]{1,0:T(8,128)(2,1)}, u32[]{:S(2)}, u32[]{:S(2)}) collective-permute-start(bf16[128,512]{1,0:T(8,128)(2,1)} %get-tuple-element.93), channel_id=1, source_target_pairs={{0,1},{1,65},{2,3},{3,67},{4,5},{5,69},{6,7},{7,71},{8,9},{9,73},{... | collective-permute-start | bytes 393224 | tf_op jit(solution)/shard_map/every_normed/ppermute | solution.py:758
  82.9 14.3 %collective-permute-start.14 = (bf16[128,512]{1,0:T(8,128)(2,1)}, bf16[128,512]{1,0:T(8,128)(2,1)}, u32[]{:S(2)}, u32[]{:S(2)}) collective-permute-start(bf16[128,512]{1,0:T(8,128)(2,1)} %get-tuple-element.94), channel_id=1, source_target_pairs={{0,32},{1,96},{2,34},{3,98},{4,36},{5,100},{6,38},{7,102},{8,40},{... | collective-permute-start | bytes 393224 | tf_op jit(solution)/shard_map/every_normed/ppermute | solution.py:758
  82.9 14.3 %collective-permute-start.15 = (bf16[128,512]{1,0:T(8,128)(2,1)}, bf16[128,512]{1,0:T(8,128)(2,1)}, u32[]{:S(2)}, u32[]{:S(2)}) collective-permute-start(bf16[128,512]{1,0:T(8,128)(2,1)} %get-tuple-element.95), channel_id=1, source_target_pairs={{0,33},{1,97},{2,35},{3,99},{4,37},{5,101},{6,39},{7,103},{8,41},{... | collective-permute-start | bytes 393224 | tf_op jit(solution)/shard_map/every_normed/ppermute | solution.py:758
  90.9 16.2 %all-to-all-start.3 = ((bf16[16,64,128]{2,1,0:T(8,128)(2,1)}), bf16[16,64,128]{2,1,0:T(8,128)(2,1)}, u32[]{:S(2)}, u32[]{:S(2)}) async-start(bf16[16,64,128]{2,1,0:T(8,128)(2,1)} %chain.3), calls=%async_computation.3 | async-start | bytes 524288 | tf_op jit(solution)/shard_map/all_to_all | solution.py:732
  102.4 10.7 %collective-permute-start.21 = (bf16[16,16,2048]{2,1,0:T(8,128)(2,1)}, bf16[16,16,2048]{2,1,0:T(8,128)(2,1)}, u32[]{:S(2)}, u32[]{:S(2)}) collective-permute-start(bf16[16,16,2048]{2,1,0:T(8,128)(2,1)} %get-tuple-element.125), channel_id=1, source_target_pairs={{0,1},{1,0},{2,3},{3,2},{4,5},{5,4},{6,7},{7,6},{8,9},{9,8},{10,11... | collective-permute-start | bytes 3145736 | tf_op jit(solution)/shard_map/weight_grad/ppermute | solution.py:738
  115.6 21.8 %all-to-all-start.4 = ((bf16[16,16,2048]{2,1,0:T(8,128)(2,1)}), bf16[16,16,2048]{2,1,0:T(8,128)(2,1)}, u32[]{:S(2)}, u32[]{:S(2)}) async-start(bf16[16,16,2048]{2,1,0:T(8,128)(2,1)} %join.1), calls=%async_computation.4 | async-start | bytes 2097152 | tf_op jit(solution)/shard_map/weight_grad/all_to_all | solution.py:732
  125.9 6.2 %collective-permute-start.16 = (bf16[128,2048]{1,0:T(8,128)(2,1)}, bf16[128,2048]{1,0:T(8,128)(2,1)}, u32[]{:S(2)}, u32[]{:S(2)}) collective-permute-start(bf16[128,2048]{1,0:T(8,128)(2,1)} %get-tuple-element.111), channel_id=1, source_target_pairs={{0,1},{1,0},{2,3},{3,2},{4,5},{5,4},{6,7},{7,6},{8,9},{9,8},{10,11... | collective-permute-start | bytes 1572872 | tf_op jit(solution)/shard_map/mixed_out/ppermute | solution.py:738
  126.0 3.2 %collective-permute-start.17 = (bf16[128,1024]{1,0:T(8,128)(2,1)}, bf16[128,1024]{1,0:T(8,128)(2,1)}, u32[]{:S(2)}, u32[]{:S(2)}) collective-permute-start(bf16[128,1024]{1,0:T(8,128)(2,1)} %get-tuple-element.116), channel_id=1, source_target_pairs={{0,1},{1,0},{2,3},{3,2},{4,5},{5,4},{6,7},{7,6},{8,9},{9,8},{10,11... | collective-permute-start | bytes 786440 | tf_op jit(solution)/shard_map/swap_back/ppermute | solution.py:738
  126.5 2.9 %collective-permute-start.20 = (bf16[128,1024]{1,0:T(8,128)(2,1)}, bf16[128,1024]{1,0:T(8,128)(2,1)}, u32[]{:S(2)}, u32[]{:S(2)}) collective-permute-start(bf16[128,1024]{1,0:T(8,128)(2,1)} %get-tuple-element.119), channel_id=1, source_target_pairs={{0,1},{1,0},{2,3},{3,2},{4,5},{5,4},{6,7},{7,6},{8,9},{9,8},{10,11... | collective-permute-start | bytes 786440 | tf_op jit(solution)/shard_map/swap_back/ppermute | solution.py:738
  126.6 2.6 %collective-permute-start.18 = (bf16[128,512]{1,0:T(8,128)(2,1)}, bf16[128,512]{1,0:T(8,128)(2,1)}, u32[]{:S(2)}, u32[]{:S(2)}) collective-permute-start(bf16[128,512]{1,0:T(8,128)(2,1)} %get-tuple-element.117), channel_id=1, source_target_pairs={{0,1},{1,0},{2,3},{3,2},{4,5},{5,4},{6,7},{7,6},{8,9},{9,8},{10,11... | collective-permute-start | bytes 393224 | tf_op jit(solution)/shard_map/swap_back/ppermute | solution.py:738
  127.0 2.4 %collective-permute-start.19 = (bf16[128,512]{1,0:T(8,128)(2,1)}, bf16[128,512]{1,0:T(8,128)(2,1)}, u32[]{:S(2)}, u32[]{:S(2)}) collective-permute-start(bf16[128,512]{1,0:T(8,128)(2,1)} %get-tuple-element.118), channel_id=1, source_target_pairs={{0,1},{1,0},{2,3},{3,2},{4,5},{5,4},{6,7},{7,6},{8,9},{9,8},{10,11... | collective-permute-start | bytes 393224 | tf_op jit(solution)/shard_map/swap_back/ppermute | solution.py:738

commit v5 on v4

--- a/solution.py
+++ b/solution.py
@@ -684,7 +684,7 @@
         out_ref[...] = part_ref[...]
 
 
-def fill(sc, wholes, parts):
+def fill(sc, wholes, parts, gflops):
     count = len(wholes)
     return pl.pallas_call(
         fill_kernel,
@@ -698,32 +698,45 @@
         out_shape=[shape(whole.shape) for whole in wholes],
         input_output_aliases={1 + n: n for n in range(count)},
         compiler_params=PARAMS,
-        cost_estimate=cost(0.01),
+        cost_estimate=cost(gflops),
         name="fill",
     )(sc, *wholes, *parts)
 
 
-def sum_kernel(a_ref, b_ref, c_ref, out_ref):
-    width = a_ref.shape[1]
-    out_ref[:, :width] = (a_ref[...] + c_ref[:, :width].astype(F32)).astype(BF16)
-    out_ref[:, width:] = (b_ref[...] + c_ref[:, width:].astype(F32)).astype(BF16)
-
-
-def sum_shares(own, other, steps=2):
-    rows, columns = own.shape
-    part = columns // (2 * steps)
-    halves = [block((rows, part), lambda i, n=n: (0, 2 * i + n)) for n in range(2)]
-    whole = block((rows, 2 * part), lambda i: (0, i))
-    return pl.pallas_call(
-        sum_kernel,
-        grid=(steps,),
-        in_specs=halves + [whole],
-        out_specs=whole,
-        out_shape=shape(own.shape),
+def finish_kernel(sc_ref, *refs):
+    count = (len(refs) - 4) // 3
+    owns, other_ref, mixed_ref = refs[:2], refs[2], refs[3 + 2 * count]
+    for part_ref, out_ref in zip(refs[3 + count:3 + 2 * count], refs[4 + 2 * count:]):
+        out_ref[...] = part_ref[...]
+    width = owns[0].shape[1]
+    for n in range(2):
+        lanes = slice(n * width, (n + 1) * width)
+        mixed_ref[:, lanes] = (owns[n][...] + other_ref[:, lanes].astype(F32)).astype(BF16)
+
+
+def finish(sc, mixed, wholes, parts):
+    count, steps = len(wholes), 2
+    columns = mixed[1].shape[1]
+    some = lambda part: block((T, part.shape[1] // steps), lambda i, sc: (0, i))
+    return pl.pallas_call(
+        finish_kernel,
+        grid_spec=pltpu.PrefetchScalarGridSpec(
+            num_scalar_prefetch=1,
+            grid=(steps,),
+            in_specs=[block((T, columns // 4), lambda i, sc, n=n: (0, 2 * i + n))
+                      for n in range(2)]
+            + [some(mixed[1])] + [pl.BlockSpec(memory_space=pl.ANY)] * count
+            + [some(part) for part in parts],
+            out_specs=[some(mixed[1])]
+            + [block((T, part.shape[1] // steps), lambda i, sc: (0, steps * (1 - sc[0]) + i))
+               for part in parts],
+        ),
+        out_shape=[shape(mixed[1].shape)] + [shape(whole.shape) for whole in wholes],
+        input_output_aliases={4 + n: 1 + n for n in range(count)},
         compiler_params=PARAMS,
         cost_estimate=cost(0.01),
-        name="sum_shares",
-    )(own, own, other)
+        name="finish",
+    )(sc, mixed[0], *mixed, *wholes, *parts)
 
 
 def exchange(x):
@@ -808,21 +821,19 @@
         rows = list(tie(states, *rows)[1:])
         keep, send = weight_local(sc, rows, every_scaled)
         send = sibling(send)
-    with jax.named_scope("swap_back"):
-        others = [sibling(gate_grad_x), sibling(dq_x)]
+        gate_grad, dq = fill(sc, [gate_grad, dq], [sibling(gate_grad_x), sibling(dq_x)], 25)
+        keep, gate_grad = tie(keep, gate_grad)
+        terms = join(keep, send)
+        weight_grad = total(exchange(terms))
+        leaving, terms = tie(leaving, terms)
     dk, dv, dk_x, dv_x = late_local(sc, k, ld, be, k_x, ld_x, be_x, t, u, a, entering, second,
                                     leaving, gs, dkn, du)
-    with jax.named_scope("weight_grad"):
-        dk, keep = tie(dk, keep)
-        weight_grad = total(exchange(join(keep, send)))
     with jax.named_scope("mixed_out"):
         dk, normed, normed_x = tie(dk, normed, normed_x)
         mixed, mixed_x = mixed_local(sc, normed, normed_x, heads_weight)
     with jax.named_scope("swap_back"):
-        gate_grad, dq, dk, dv = fill(
-            sc, [gate_grad, dq, dk, dv], others + [sibling(dk_x), sibling(dv_x)])
-    with jax.named_scope("mixed_out"):
-        mixed = sum_shares(mixed, sibling(mixed_x))
+        mixed, dk, dv = finish(
+            sc, [mixed, sibling(mixed_x)], [dk, dv], [sibling(dk_x), sibling(dv_x)])
     return mixed[None], dq[None], dk[None], dv[None], gate_grad[None], weight_grad
 
 

time: 141 us -> 140 us (level); the launches traced: 140 us -> 137 us
  waiting for transfers between devices: 24 us -> 16.6 us
  starting transfers between devices: 50.3 us -> 54.6 us
    all_to_all x5, waiting for transfers between devices: 12.6 us -> 5.06 us  [exchange(): lax.all_to_all(x, 'ctx', split_axis=0, concat_axis=0, tiled=True, axis_in...]
    all_to_all x5, starting transfers between devices: 28.9 us -> 32.8 us  [exchange(): lax.all_to_all(x, 'ctx', split_axis=0, concat_axis=0, tiled=True, axis_in...]
  transfers between devices with their start and end apart: 27 -> 27, of which waited for: 8 -> 6; matrix products, arithmetic and copies ran while one was open for 0% -> 0% of each run, Pallas kernels for 42% -> 45%
where the time goes in v5:
time: 140 us; the launch traced here: 137 us
  Pallas kernels  64.3 us (46%)
  starting transfers between devices  54.6 us (39%)
  waiting for transfers between devices  16.6 us (12%)
    all_to_all x5, starting transfers between devices, exchange(): lax.all_to_all(x, 'ctx', split_axis=0, concat_axis=0, tiled=True, axis_in...  32.8 us
    ppermute x16, starting transfers between devices, cross(): return lax.ppermute(x, axis, [(i, i ^ distance) for i in range(count)])  8.71 us
    pallas_call x1, Pallas kernels, body(): ab, t, u0, kg, a, b = write_local(sc, k, v, ld, be, k_x, v_x, ld_x, be_x)  8.54 us
    pallas_call x1, Pallas kernels, body(): gate_local(sc, entering, gate, ld, be, gate_x, ld_x, be_x, *bg, a, b, io,...  7.92 us
    pallas_call x2, Pallas kernels, chain(): pl.pallas_call(kernel, grid=(1,), in_specs=streams + [whole] * len(args),...  7.84 us
    ppermute x4, starting transfers between devices, feature_round(): return lax.ppermute(x, ('fsdp', 'ctx'), pairs)  7.81 us
    pallas_call x1, Pallas kernels, back_local(): pl.pallas_call(back_kernel, grid_spec=pltpu.PrefetchScalarGridSpec(num_sc...  6.26 us
    ppermute x2, waiting for transfers between devices, weight_round(): return lax.ppermute(x, ('fsdp', 'ctx'), pairs)  6.24 us
  transfers between devices with their start and end apart: 27, of which 6 were waited for; matrix products, arithmetic and copies ran while one was open for 0% of the time, Pallas kernels for 45%

profile of v5, /device:TPU:0, one launch (start us, length us, event | category | flops | bytes accessed | tf_op | source)
XLA Modules:
  0.0 137.0 jit_solution(10502704514186069258)
XLA Ops:
  0.6 0.1 collective-permute-start.3
  0.7 0.5 collective-permute-start
  1.2 0.1 collective-permute-start.1
  1.3 0.4 collective-permute-start.2
  1.7 4.1 %collective-permute-start.8 = (bf16[512,2048]{1,0:T(8,128)(2,1)}, bf16[512,2048]{1,0:T(8,128)(2,1)}, u32[]{:S(2)}, u32[]{:S(2)}) collective-permute-start(bf16[512,2048]{1,0:T(8,128)(2,1)} %param.17), channel_id=1, source_target_pairs={{33,0},{97,1},{35,2},{99,3},{37,4},{101,5},{39,6},{103,7},{41,8},{... | collective-permute-start | bytes 6291464 | tf_op jit(solution)/shard_map/out_weight/ppermute | solution.py:779
  5.9 0.6 pad_add_fusion.sc_ref
  6.5 0.0 collective-permute-done.1.lx_ref
  6.5 1.2 collective-permute-start.7
  7.7 0.0 collective-permute-done.2.rx_ref
  7.7 0.0 collective-permute-done.kx_ref
  7.7 0.0 collective-permute-done.3.vx_ref
  7.7 8.5 %write_local.1 = (bf16[16,208,128]{2,1,0:T(8,128)(2,1)}, bf16[16,128,128]{2,1,0:T(8,128)(2,1)}, bf16[16,128,128]{2,1,0:T(8,128)(2,1)}, bf16[16,128,128]{2,1,0:T(...) custom-call(s32[3]{0:T(128)} %pad_add_fusion.sc_ref, bf16[128,1024]{1,0:T(8,128)(2,1)} %bitcast.28, ...), custom_call_target="tpu_custom_call" | custom-call | flops 17999998976 | bytes 65536 | tf_op jit(solution)/shard_map/write_local/pallas_call | solution.py:796
  16.2 7.1 %all-to-all-start = ((bf16[16,208,128]{2,1,0:T(8,128)(2,1)}), bf16[16,208,128]{2,1,0:T(8,128)(2,1)}, u32[]{:S(2)}, u32[]{:S(2)}) async-start(bf16[16,208,128]{2,1,0:T(8,128)(2,1)} %get-tuple-element.69), calls=%async_computation | async-start | bytes 1703936 | tf_op jit(solution)/shard_map/all_to_all | solution.py:745
  23.3 2.6 %scale_local.1.own_ref.refs_4_ = bf16[128,2048]{1,0:T(8,128)(2,1)} custom-call(s32[3]{0:T(128)} %pad_add_fusion.sc_ref, s32[4]{0:T(128)} %lengths_ref.1, s32[4]{0:T(128)} %pairing_ref.1, f32[4]{0:T(128)} %ratio_ref.1, bf16[128,2048]{1,0:T(8,128)(2,1)} %bitcast.22), custom_call_target="tpu_custom_call" | custom-call | flops 10000000 | bytes 65536 | tf_op jit(solution)/shard_map/every_scaled/scale_local/pallas_call | solution.py:508
  25.9 0.0 collective-permute-start.6
  25.9 0.5 collective-permute-start.5
  26.4 0.0 collective-permute-start.4
  26.4 2.9 %collective-permute-done.4.qx_ref = bf16[128,1024]{1,0:T(8,128)(2,1)} collective-permute-done((bf16[128,1024]{1,0:T(8,128)(2,1)}, bf16[128,1024]{1,0:T(8,128)(2,1)}, u32[]{:S(2)}, u32[]{:S(2)}) %collective-permute-start.4) | collective-permute-done | bytes 262176 | tf_op jit(solution)/shard_map/swap_heads/ppermute | solution.py:751
  29.2 4.1 %read_local.1 = (bf16[16,128,128]{2,1,0:T(8,128)(2,1)}, bf16[16,128,128]{2,1,0:T(8,128)(2,1)}, bf16[16,128,128]{2,1,0:T(8,128)(2,1)}) custom-call(s32[3]{0:T(128)} %pad_add_fusion.sc_ref, bf16[128,1024]{1,0:T(8,128)(2,1)} %bitcast.25, bf16[128,1024]{1,0:T(8,128)(2,1)} %bitcast.29, f32[16,128]{1,0:T(8,128)} %bitcast.36, f32[16,128]{1,0:T(8,128)} %bitcast.41, ...), custom_call_target="tpu_custom_call" | custom-call | flops 10000000 | bytes 65536 | tf_op jit(solution)/shard_map/read_local/pallas_call | solution.py:803
  33.3 4.5 %all-to-all-done.refs_0_.refs_1_.refs_2_.refs_3_ = bf16[16,208,128]{2,1,0:T(8,128)(2,1)} async-done(((bf16[16,208,128]{2,1,0:T(8,128)(2,1)}), bf16[16,208,128]{2,1,0:T(8,128)(2,1)}, u32[]{:S(2)}, u32[]{:S(2)}) %all-to-all-start) | async-done | bytes 852000 | tf_op jit(solution)/shard_map/all_to_all | solution.py:745
  37.9 3.9 %chain.2 = bf16[16,64,128]{2,1,0:T(8,128)(2,1)} custom-call(bf16[16,208,128]{2,1,0:T(8,128)(2,1)} %all-to-all-done.refs_0_.refs_1_.refs_2_.refs_3_, bf16[16,208,128]{2,1,0:T(8,128)(2,1)} %all-to-all-done.refs_0_.refs_1_.refs_2_.refs_3_, bf16[16,208,128]{2,1,0:T(8,128)(2,1)} %all-to-all-done.refs_0_.refs_1_.refs_2_.refs_3_, ...), custom_call_target="tpu_custom_call" | custom-call | flops 10000000 | bytes 65536 | tf_op jit(solution)/shard_map/chain/pallas_call | solution.py:473
  41.8 4.2 %all-to-all-start.1 = ((bf16[16,64,128]{2,1,0:T(8,128)(2,1)}), bf16[16,64,128]{2,1,0:T(8,128)(2,1)}, u32[]{:S(2)}, u32[]{:S(2)}) async-start(bf16[16,64,128]{2,1,0:T(8,128)(2,1)} %chain.2), calls=%async_computation.1 | async-start | bytes 524288 | tf_op jit(solution)/shard_map/all_to_all | solution.py:745
  46.0 6.2 %collective-permute-done.8.refs_4_.refs_5_.refs_6_.refs_7_ = bf16[512,2048]{1,0:T(8,128)(2,1)} collective-permute-done((bf16[512,2048]{1,0:T(8,128)(2,1)}, bf16[512,2048]{1,0:T(8,128)(2,1)}, u32[]{:S(2)}, u32[]{:S(2)}) %collective-permute-start.8) | collective-permute-done | bytes 2097184 | tf_op jit(solution)/shard_map/out_weight/ppermute | solution.py:779
  52.2 0.0 collective-permute-done.7.refs_0_.refs_1_.refs_2_.refs_3_
  52.2 3.7 %collective-permute-start.11 = (bf16[128,2048]{1,0:T(8,128)(2,1)}, bf16[128,2048]{1,0:T(8,128)(2,1)}, u32[]{:S(2)}, u32[]{:S(2)}) collective-permute-start(bf16[128,2048]{1,0:T(8,128)(2,1)} %scale_local.1.own_ref.refs_4_), channel_id=1, source_target_pairs={{0,96},{32,64},{64,32},{96,0},{1,97},{33,65},{65,33},{97,1},{2,98}... | collective-permute-start | bytes 1572872 | tf_op jit(solution)/shard_map/every_scaled/ppermute | solution.py:751
  55.9 0.0 collective-permute-start.10
  55.9 0.9 collective-permute-start.9
  56.8 0.0 collective-permute-done.6.other_ref
  56.8 6.3 %back_local.1 = (bf16[128,1024]{1,0:T(8,128)(2,1)}, bf16[128,1024]{1,0:T(8,128)(2,1)}) custom-call(s32[3]{0:T(128)} %pad_add_fusion.sc_ref, bf16[128,2048]{1,0:T(8,128)(2,1)} %scale_local.1.own_ref.refs_4_, bf16[128,2048]{1,0:T(8,128)(2,1)} %collective-permute-done.6.other_ref, bf16[512,2048]{1,0:T(8,128)(2,1)} %collective-permute-done.7.refs_0_.refs_1_.refs_2_.refs_3_, ...), custom_call_target="tpu_custom_call" | custom-call | flops 10000000 | bytes 65536 | tf_op jit(solution)/shard_map/back_grad/back_local/pallas_call | solution.py:546
  63.0 0.0 all-to-all-done.1
  63.0 7.9 %gate_local.1 = (bf16[128,512]{1,0:T(8,128)(2,1)}, bf16[128,512]{1,0:T(8,128)(2,1)}, bf16[128,512]{1,0:T(8,128)(2,1)}, bf16[128,512]{1,0:T(8,128)(2,1)}, bf16[12...) custom-call(s32[3]{0:T(128)} %pad_add_fusion.sc_ref, ...), custom_call_target="tpu_custom_call" | custom-call | flops 12000000000 | bytes 65536 | tf_op jit(solution)/shard_map/gate_local/pallas_call | solution.py:812
  71.0 7.1 %all-to-all-start.2 = ((bf16[16,64,128]{2,1,0:T(8,128)(2,1)}), bf16[16,64,128]{2,1,0:T(8,128)(2,1)}, u32[]{:S(2)}, u32[]{:S(2)}) async-start(bf16[16,64,128]{2,1,0:T(8,128)(2,1)} %bitcast.33), calls=%async_computation.2 | async-start | bytes 524288 | tf_op jit(solution)/shard_map/all_to_all | solution.py:745
  78.1 2.2 %collective-permute-start.12 = (bf16[128,512]{1,0:T(8,128)(2,1)}, bf16[128,512]{1,0:T(8,128)(2,1)}, u32[]{:S(2)}, u32[]{:S(2)}) collective-permute-start(bf16[128,512]{1,0:T(8,128)(2,1)} %get-tuple-element.90), channel_id=1, source_target_pairs={{0,0},{1,64},{2,2},{3,66},{4,4},{5,68},{6,6},{7,70},{8,8},{9,72},{... | collective-permute-start | bytes 393224 | tf_op jit(solution)/shard_map/every_normed/ppermute | solution.py:771
  80.2 2.6 %collective-permute-start.13 = (bf16[128,512]{1,0:T(8,128)(2,1)}, bf16[128,512]{1,0:T(8,128)(2,1)}, u32[]{:S(2)}, u32[]{:S(2)}) collective-permute-start(bf16[128,512]{1,0:T(8,128)(2,1)} %get-tuple-element.91), channel_id=1, source_target_pairs={{0,1},{1,65},{2,3},{3,67},{4,5},{5,69},{6,7},{7,71},{8,9},{9,73},{... | collective-permute-start | bytes 393224 | tf_op jit(solution)/shard_map/every_normed/ppermute | solution.py:771
  82.8 0.0 collective-permute-done.11.refs_7_
  82.8 0.0 collective-permute-start.14
  82.8 0.0 collective-permute-done.10.refs_6_
  82.9 3.0 %collective-permute-start.15 = (bf16[128,512]{1,0:T(8,128)(2,1)}, bf16[128,512]{1,0:T(8,128)(2,1)}, u32[]{:S(2)}, u32[]{:S(2)}) collective-permute-start(bf16[128,512]{1,0:T(8,128)(2,1)} %get-tuple-element.93), channel_id=1, source_target_pairs={{0,33},{1,97},{2,35},{3,99},{4,37},{5,101},{6,39},{7,103},{8,41},{... | collective-permute-start | bytes 393224 | tf_op jit(solution)/shard_map/every_normed/ppermute | solution.py:771
  85.9 0.0 collective-permute-done.9.refs_5_
  85.9 1.2 collective-permute-start.17
  87.1 4.0 %chain.3 = bf16[16,64,128]{2,1,0:T(8,128)(2,1)} custom-call(bf16[16,208,128]{2,1,0:T(8,128)(2,1)} %all-to-all-done.refs_0_.refs_1_.refs_2_.refs_3_, bf16[16,208,128]{2,1,0:T(8,128)(2,1)} %all-to-all-done.refs_0_.refs_1_.refs_2_.refs_3_, bf16[16,208,128]{2,1,0:T(8,128)(2,1)} %all-to-all-done.refs_0_.refs_1_.refs_2_.refs_3_, ...), custom_call_target="tpu_custom_call" | custom-call | flops 10000000 | bytes 65536 | tf_op jit(solution)/shard_map/chain/pallas_call | solution.py:473
  91.1 7.2 %all-to-all-start.3 = ((bf16[16,64,128]{2,1,0:T(8,128)(2,1)}), bf16[16,64,128]{2,1,0:T(8,128)(2,1)}, u32[]{:S(2)}, u32[]{:S(2)}) async-start(bf16[16,64,128]{2,1,0:T(8,128)(2,1)} %chain.3), calls=%async_computation.3 | async-start | bytes 524288 | tf_op jit(solution)/shard_map/all_to_all | solution.py:745
  98.3 0.0 collective-permute-done.12.refs_0_
  98.3 0.1 collective-permute-start.16
  98.4 0.0 collective-permute-done.13.refs_1_
  98.4 0.0 collective-permute-done.14.refs_2_
  98.5 5.3 %weight_local.1 = (bf16[16,16,2048]{2,1,0:T(8,128)(2,1)}, bf16[16,16,2048]{2,1,0:T(8,128)(2,1)}) custom-call(s32[3]{0:T(128)} %pad_add_fusion.sc_ref, bf16[128,512]{1,0:T(8,128)(2,1)} %collective-permute-done.12.refs_0_, bf16[128,512]{1,0:T(8,128)(2,1)} %collective-permute-done.13.refs_1_, bf16[128,512]{1,0:T(8,128)(2,1)} %collective-permute-done.14.refs_2_, ...), custom_call_target="tpu_custom_call" | custom-call | flops 4000000000 | bytes 65536 | tf_op jit(solution)/shard_map/weight_grad/weight_local/pallas_call | solution.py:623
  103.7 0.6 collective-permute-start.18
  104.3 0.0 collective-permute-done.17.refs_3_
  104.3 0.0 collective-permute-done.16.refs_2_
  104.3 2.4 %fill.1 = (bf16[128,2048]{1,0:T(8,128)(2,1)}, bf16[128,1024]{1,0:T(8,128)(2,1)}) custom-call(s32[3]{0:T(128)} %pad_add_fusion.sc_ref, bf16[128,2048]{1,0:T(8,128)(2,1)} %get-tuple-element.103.refs_0_, bf16[128,1024]{1,0:T(8,128)(2,1)} %get-tuple-element.104.refs_1_, ...), custom_call_target="tpu_custom_call", output_to_operand_aliasing={{0}: (1, {}), {1}: (2, {})} | custom-call | flops 24999999488 | bytes 65536 | tf_op jit(solution)/shard_map/weight_grad/fill/pallas_call | solution.py:689
  106.7 0.2 collective-permute-done.18.refs_2_.refs_3_
  106.9 2.4 %join.1 = bf16[16,16,2048]{2,1,0:T(8,128)(2,1)} custom-call(bf16[16,16,2048]{2,1,0:T(8,128)(2,1)} %get-tuple-element.108.refs_0_.refs_1_, bf16[16,16,2048]{2,1,0:T(8,128)(2,1)} %get-tuple-element.108.refs_0_.refs_1_, bf16[16,16,2048]{2,1,0:T(8,128)(2,1)} %collective-permute-done.18.refs_2_.refs_3_, bf16[16,16,2048]{2,1,0:T(8,128)(2,1)} %collective-permute-done.18.refs_2_.refs_3_), custom_call_target="tpu_custom_call" | custom-call | flops 10000000 | bytes 65536 | tf_op jit(solution)/shard_map/weight_grad/join/pallas_call | solution.py:649
  109.3 7.2 %all-to-all-start.4 = ((bf16[16,16,2048]{2,1,0:T(8,128)(2,1)}), bf16[16,16,2048]{2,1,0:T(8,128)(2,1)}, u32[]{:S(2)}, u32[]{:S(2)}) async-start(bf16[16,16,2048]{2,1,0:T(8,128)(2,1)} %join.1), calls=%async_computation.4 | async-start | bytes 2097152 | tf_op jit(solution)/shard_map/weight_grad/all_to_all | solution.py:745
  116.6 6.0 %late_local.1 = (bf16[128,1024]{1,0:T(8,128)(2,1)}, bf16[128,2048]{1,0:T(8,128)(2,1)}, bf16[128,512]{1,0:T(8,128)(2,1)}, bf16[128,1024]{1,0:T(8,128)(2,1)}) custom-call(s32[3]{0:T(128)} %pad_add_fusion.sc_ref, bf16[128,1024]{1,0:T(8,128)(2,1)} %bitcast.31, f32[16,128]{1,0:T(8,128)} %bitcast.38, f32[16,128]{1,0:T(8,128)} %bitcast.43, ...), custom_call_target="tpu_custom_call" | custom-call | flops 49999998976 | bytes 65536 | tf_op jit(solution)/shard_map/late_local/pallas_call | solution.py:829
  122.6 5.9 %mixed_local.1 = (f32[128,2048]{1,0:T(8,128)}, bf16[128,2048]{1,0:T(8,128)(2,1)}) custom-call(s32[3]{0:T(128)} %pad_add_fusion.sc_ref, bf16[128,1024]{1,0:T(8,128)(2,1)} %get-tuple-element.117.no_ref, bf16[128,1024]{1,0:T(8,128)(2,1)} %get-tuple-element.118.nx_ref, bf16[512,2048]{1,0:T(8,128)(2,1)} %collective-permute-done.7.refs_0_.refs_1_.refs_2_.refs_3_, ...), custom_call_target="tpu_custom_call" | custom-call | flops 10000000 | bytes 65536 | tf_op jit(solution)/shard_map/mixed_out/mixed_local/pallas_call | solution.py:580
  128.5 0.2 collective-permute-start.19
  128.7 0.4 collective-permute-start.21
  129.1 0.1 collective-permute-start.20
  129.2 2.2 %collective-permute-done.20.refs_5_ = bf16[128,512]{1,0:T(8,128)(2,1)} collective-permute-done((bf16[128,512]{1,0:T(8,128)(2,1)}, bf16[128,512]{1,0:T(8,128)(2,1)}, u32[]{:S(2)}, u32[]{:S(2)}) %collective-permute-start.20) | collective-permute-done | bytes 131104 | tf_op jit(solution)/shard_map/swap_back/ppermute | solution.py:751
  131.4 0.0 collective-permute-done.19.refs_2_
  131.4 3.0 %finish.1 = (bf16[128,2048]{1,0:T(8,128)(2,1)}, bf16[128,1024]{1,0:T(8,128)(2,1)}, bf16[128,2048]{1,0:T(8,128)(2,1)}) custom-call(s32[3]{0:T(128)} %pad_add_fusion.sc_ref, f32[128,2048]{1,0:T(8,128)} %get-tuple-element.119.refs_0_.refs_1_, f32[128,2048]{1,0:T(8,128)} %get-tuple-element.119.refs_0_.refs_1_, ...), custom_call_target="tpu_custom_call", output_to_operand_aliasing={{1}: (4, {}), {2}: (5, {})} | custom-call | flops 10000000 | bytes 65536 | tf_op jit(solution)/shard_map/swap_back/finish/pallas_call | solution.py:721
  134.4 0.5 all-to-all-done.4.refs_0_.refs_1_.refs_2_.refs_3_.refs_4_.refs_5_.refs_6_.refs_7_
  134.9 2.1 %total.1 = f32[16,2048]{1,0:T(8,128)} custom-call(bf16[16,16,2048]{2,1,0:T(8,128)(2,1)} %all-to-all-done.4.refs_0_.refs_1_.refs_2_.refs_3_.refs_4_.refs_5_.refs_6_.refs_7_, bf16[16,16,2048]{2,1,0:T(8,128)(2,1)} %all-to-all-done.4.refs_0_.refs_1_.refs_2_.refs_3_.refs_4_.refs_5_.refs_6_.refs_7_, ...), custom_call_target="tpu_custom_call" | custom-call | flops 10000000 | bytes 65536 | tf_op jit(solution)/shard_map/weight_grad/total/pallas_call | solution.py:668
  (5 shorter events, 0.0 us)
Async XLA Ops:
  0.6 7.0 %collective-permute-start.3 = (bf16[128,2048]{1,0:T(8,128)(2,1)}, bf16[128,2048]{1,0:T(8,128)(2,1)}, u32[]{:S(2)}, u32[]{:S(2)}) collective-permute-start(bf16[128,2048]{1,0:T(8,128)(2,1)} %bitcast.44), channel_id=1, source_target_pairs={{0,1},{1,0},{2,3},{3,2},{4,5},{5,4},{6,7},{7,6},{8,9},{9,8},{10,11... | collective-permute-start | bytes 1572872 | tf_op jit(solution)/shard_map/swap_heads/ppermute | solution.py:751
  0.7 6.9 %collective-permute-start = (bf16[128,1024]{1,0:T(8,128)(2,1)}, bf16[128,1024]{1,0:T(8,128)(2,1)}, u32[]{:S(2)}, u32[]{:S(2)}) collective-permute-start(bf16[128,1024]{1,0:T(8,128)(2,1)} %bitcast.27), channel_id=1, source_target_pairs={{0,1},{1,0},{2,3},{3,2},{4,5},{5,4},{6,7},{7,6},{8,9},{9,8},{10,11... | collective-permute-start | bytes 786440 | tf_op jit(solution)/shard_map/swap_heads/ppermute | solution.py:751
  1.2 5.3 %collective-permute-start.1 = (f32[16,128]{1,0:T(8,128)}, f32[16,128]{1,0:T(8,128)}, u32[]{:S(2)}, u32[]{:S(2)}) collective-permute-start(f32[16,128]{1,0:T(8,128)} %bitcast.34), channel_id=1, source_target_pairs={{0,1},{1,0},{2,3},{3,2},{4,5},{5,4},{6,7},{7,6},{8,9},{9,8},{10,11... | collective-permute-start | bytes 24584 | tf_op jit(solution)/shard_map/swap_heads/ppermute | solution.py:751
  1.3 6.3 %collective-permute-start.2 = (f32[16,128]{1,0:T(8,128)}, f32[16,128]{1,0:T(8,128)}, u32[]{:S(2)}, u32[]{:S(2)}) collective-permute-start(f32[16,128]{1,0:T(8,128)} %bitcast.39), channel_id=1, source_target_pairs={{0,1},{1,0},{2,3},{3,2},{4,5},{5,4},{6,7},{7,6},{8,9},{9,8},{10,11... | collective-permute-start | bytes 24584 | tf_op jit(solution)/shard_map/swap_heads/ppermute | solution.py:751
  1.7 50.5 %collective-permute-start.8 = (bf16[512,2048]{1,0:T(8,128)(2,1)}, bf16[512,2048]{1,0:T(8,128)(2,1)}, u32[]{:S(2)}, u32[]{:S(2)}) collective-permute-start(bf16[512,2048]{1,0:T(8,128)(2,1)} %param.17), channel_id=1, source_target_pairs={{33,0},{97,1},{35,2},{99,3},{37,4},{101,5},{39,6},{103,7},{41,8},{... | collective-permute-start | bytes 6291464 | tf_op jit(solution)/shard_map/out_weight/ppermute | solution.py:779
  6.5 45.7 %collective-permute-start.7 = (bf16[512,2048]{1,0:T(8,128)(2,1)}, bf16[512,2048]{1,0:T(8,128)(2,1)}, u32[]{:S(2)}, u32[]{:S(2)}) collective-permute-start(bf16[512,2048]{1,0:T(8,128)(2,1)} %param.17), channel_id=1, source_target_pairs={{1,0},{65,1},{3,2},{67,3},{5,4},{69,5},{7,6},{71,7},{9,8},{73,9},{... | collective-permute-start | bytes 6291464 | tf_op jit(solution)/shard_map/out_weight/ppermute | solution.py:779
  16.2 21.7 %all-to-all-start = ((bf16[16,208,128]{2,1,0:T(8,128)(2,1)}), bf16[16,208,128]{2,1,0:T(8,128)(2,1)}, u32[]{:S(2)}, u32[]{:S(2)}) async-start(bf16[16,208,128]{2,1,0:T(8,128)(2,1)} %get-tuple-element.69), calls=%async_computation | async-start | bytes 1703936 | tf_op jit(solution)/shard_map/all_to_all | solution.py:745
  25.9 30.9 %collective-permute-start.6 = (bf16[128,2048]{1,0:T(8,128)(2,1)}, bf16[128,2048]{1,0:T(8,128)(2,1)}, u32[]{:S(2)}, u32[]{:S(2)}) collective-permute-start(bf16[128,2048]{1,0:T(8,128)(2,1)} %scale_local.1.own_ref.refs_4_), channel_id=1, source_target_pairs={{0,1},{1,0},{2,3},{3,2},{4,5},{5,4},{6,7},{7,6},{8,9},{9,8},{10,11... | collective-permute-start | bytes 1572872 | tf_op jit(solution)/shard_map/swap_heads/ppermute | solution.py:751
  25.9 37.1 %collective-permute-start.5 = (bf16[128,2048]{1,0:T(8,128)(2,1)}, bf16[128,2048]{1,0:T(8,128)(2,1)}, u32[]{:S(2)}, u32[]{:S(2)}) collective-permute-start(bf16[128,2048]{1,0:T(8,128)(2,1)} %bitcast.46), channel_id=1, source_target_pairs={{0,1},{1,0},{2,3},{3,2},{4,5},{5,4},{6,7},{7,6},{8,9},{9,8},{10,11... | collective-permute-start | bytes 1572872 | tf_op jit(solution)/shard_map/swap_heads/ppermute | solution.py:751
  26.4 2.9 %collective-permute-start.4 = (bf16[128,1024]{1,0:T(8,128)(2,1)}, bf16[128,1024]{1,0:T(8,128)(2,1)}, u32[]{:S(2)}, u32[]{:S(2)}) collective-permute-start(bf16[128,1024]{1,0:T(8,128)(2,1)} %bitcast.24), channel_id=1, source_target_pairs={{0,1},{1,0},{2,3},{3,2},{4,5},{5,4},{6,7},{7,6},{8,9},{9,8},{10,11... | collective-permute-start | bytes 786440 | tf_op jit(solution)/shard_map/swap_heads/ppermute | solution.py:751
  41.8 21.3 %all-to-all-start.1 = ((bf16[16,64,128]{2,1,0:T(8,128)(2,1)}), bf16[16,64,128]{2,1,0:T(8,128)(2,1)}, u32[]{:S(2)}, u32[]{:S(2)}) async-start(bf16[16,64,128]{2,1,0:T(8,128)(2,1)} %chain.2), calls=%async_computation.1 | async-start | bytes 524288 | tf_op jit(solution)/shard_map/all_to_all | solution.py:745
  52.2 30.6 %collective-permute-start.11 = (bf16[128,2048]{1,0:T(8,128)(2,1)}, bf16[128,2048]{1,0:T(8,128)(2,1)}, u32[]{:S(2)}, u32[]{:S(2)}) collective-permute-start(bf16[128,2048]{1,0:T(8,128)(2,1)} %scale_local.1.own_ref.refs_4_), channel_id=1, source_target_pairs={{0,96},{32,64},{64,32},{96,0},{1,97},{33,65},{65,33},{97,1},{2,98}... | collective-permute-start | bytes 1572872 | tf_op jit(solution)/shard_map/every_scaled/ppermute | solution.py:751
  55.9 27.0 %collective-permute-start.10 = (bf16[128,2048]{1,0:T(8,128)(2,1)}, bf16[128,2048]{1,0:T(8,128)(2,1)}, u32[]{:S(2)}, u32[]{:S(2)}) collective-permute-start(bf16[128,2048]{1,0:T(8,128)(2,1)} %scale_local.1.own_ref.refs_4_), channel_id=1, source_target_pairs={{0,64},{32,96},{64,0},{96,32},{1,65},{33,97},{65,1},{97,33},{2,66}... | collective-permute-start | bytes 1572872 | tf_op jit(solution)/shard_map/every_scaled/ppermute | solution.py:751
  55.9 30.0 %collective-permute-start.9 = (bf16[128,2048]{1,0:T(8,128)(2,1)}, bf16[128,2048]{1,0:T(8,128)(2,1)}, u32[]{:S(2)}, u32[]{:S(2)}) collective-permute-start(bf16[128,2048]{1,0:T(8,128)(2,1)} %scale_local.1.own_ref.refs_4_), channel_id=1, source_target_pairs={{0,32},{32,0},{64,96},{96,64},{1,33},{33,1},{65,97},{97,65},{2,34}... | collective-permute-start | bytes 1572872 | tf_op jit(solution)/shard_map/every_scaled/ppermute | solution.py:751
  71.0 16.2 %all-to-all-start.2 = ((bf16[16,64,128]{2,1,0:T(8,128)(2,1)}), bf16[16,64,128]{2,1,0:T(8,128)(2,1)}, u32[]{:S(2)}, u32[]{:S(2)}) async-start(bf16[16,64,128]{2,1,0:T(8,128)(2,1)} %bitcast.33), calls=%async_computation.2 | async-start | bytes 524288 | tf_op jit(solution)/shard_map/all_to_all | solution.py:745
  78.1 20.3 %collective-permute-start.12 = (bf16[128,512]{1,0:T(8,128)(2,1)}, bf16[128,512]{1,0:T(8,128)(2,1)}, u32[]{:S(2)}, u32[]{:S(2)}) collective-permute-start(bf16[128,512]{1,0:T(8,128)(2,1)} %get-tuple-element.90), channel_id=1, source_target_pairs={{0,0},{1,64},{2,2},{3,66},{4,4},{5,68},{6,6},{7,70},{8,8},{9,72},{... | collective-permute-start | bytes 393224 | tf_op jit(solution)/shard_map/every_normed/ppermute | solution.py:771
  80.2 18.2 %collective-permute-start.13 = (bf16[128,512]{1,0:T(8,128)(2,1)}, bf16[128,512]{1,0:T(8,128)(2,1)}, u32[]{:S(2)}, u32[]{:S(2)}) collective-permute-start(bf16[128,512]{1,0:T(8,128)(2,1)} %get-tuple-element.91), channel_id=1, source_target_pairs={{0,1},{1,65},{2,3},{3,67},{4,5},{5,69},{6,7},{7,71},{8,9},{9,73},{... | collective-permute-start | bytes 393224 | tf_op jit(solution)/shard_map/every_normed/ppermute | solution.py:771
  82.8 15.6 %collective-permute-start.14 = (bf16[128,512]{1,0:T(8,128)(2,1)}, bf16[128,512]{1,0:T(8,128)(2,1)}, u32[]{:S(2)}, u32[]{:S(2)}) collective-permute-start(bf16[128,512]{1,0:T(8,128)(2,1)} %get-tuple-element.92), channel_id=1, source_target_pairs={{0,32},{1,96},{2,34},{3,98},{4,36},{5,100},{6,38},{7,102},{8,40},{... | collective-permute-start | bytes 393224 | tf_op jit(solution)/shard_map/every_normed/ppermute | solution.py:771
  82.9 15.6 %collective-permute-start.15 = (bf16[128,512]{1,0:T(8,128)(2,1)}, bf16[128,512]{1,0:T(8,128)(2,1)}, u32[]{:S(2)}, u32[]{:S(2)}) collective-permute-start(bf16[128,512]{1,0:T(8,128)(2,1)} %get-tuple-element.93), channel_id=1, source_target_pairs={{0,33},{1,97},{2,35},{3,99},{4,37},{5,101},{6,39},{7,103},{8,41},{... | collective-permute-start | bytes 393224 | tf_op jit(solution)/shard_map/every_normed/ppermute | solution.py:771
  85.9 18.4 %collective-permute-start.17 = (bf16[128,512]{1,0:T(8,128)(2,1)}, bf16[128,512]{1,0:T(8,128)(2,1)}, u32[]{:S(2)}, u32[]{:S(2)}) collective-permute-start(bf16[128,512]{1,0:T(8,128)(2,1)} %get-tuple-element.106), channel_id=1, source_target_pairs={{0,1},{1,0},{2,3},{3,2},{4,5},{5,4},{6,7},{7,6},{8,9},{9,8},{10,11... | collective-permute-start | bytes 393224 | tf_op jit(solution)/shard_map/weight_grad/ppermute | solution.py:751
  91.1 18.2 %all-to-all-start.3 = ((bf16[16,64,128]{2,1,0:T(8,128)(2,1)}), bf16[16,64,128]{2,1,0:T(8,128)(2,1)}, u32[]{:S(2)}, u32[]{:S(2)}) async-start(bf16[16,64,128]{2,1,0:T(8,128)(2,1)} %chain.3), calls=%async_computation.3 | async-start | bytes 524288 | tf_op jit(solution)/shard_map/all_to_all | solution.py:745
  98.3 6.0 %collective-permute-start.16 = (bf16[128,1024]{1,0:T(8,128)(2,1)}, bf16[128,1024]{1,0:T(8,128)(2,1)}, u32[]{:S(2)}, u32[]{:S(2)}) collective-permute-start(bf16[128,1024]{1,0:T(8,128)(2,1)} %get-tuple-element.105), channel_id=1, source_target_pairs={{0,1},{1,0},{2,3},{3,2},{4,5},{5,4},{6,7},{7,6},{8,9},{9,8},{10,11... | collective-permute-start | bytes 786440 | tf_op jit(solution)/shard_map/weight_grad/ppermute | solution.py:751
  103.7 3.2 %collective-permute-start.18 = (bf16[16,16,2048]{2,1,0:T(8,128)(2,1)}, bf16[16,16,2048]{2,1,0:T(8,128)(2,1)}, u32[]{:S(2)}, u32[]{:S(2)}) collective-permute-start(bf16[16,16,2048]{2,1,0:T(8,128)(2,1)} %get-tuple-element.109), channel_id=1, source_target_pairs={{0,1},{1,0},{2,3},{3,2},{4,5},{5,4},{6,7},{7,6},{8,9},{9,8},{10,11... | collective-permute-start | bytes 3145736 | tf_op jit(solution)/shard_map/weight_grad/ppermute | solution.py:751
  109.3 25.6 %all-to-all-start.4 = ((bf16[16,16,2048]{2,1,0:T(8,128)(2,1)}), bf16[16,16,2048]{2,1,0:T(8,128)(2,1)}, u32[]{:S(2)}, u32[]{:S(2)}) async-start(bf16[16,16,2048]{2,1,0:T(8,128)(2,1)} %join.1), calls=%async_computation.4 | async-start | bytes 2097152 | tf_op jit(solution)/shard_map/weight_grad/all_to_all | solution.py:745
  128.5 2.9 %collective-permute-start.19 = (bf16[128,2048]{1,0:T(8,128)(2,1)}, bf16[128,2048]{1,0:T(8,128)(2,1)}, u32[]{:S(2)}, u32[]{:S(2)}) collective-permute-start(bf16[128,2048]{1,0:T(8,128)(2,1)} %get-tuple-element.120), channel_id=1, source_target_pairs={{0,1},{1,0},{2,3},{3,2},{4,5},{5,4},{6,7},{7,6},{8,9},{9,8},{10,11... | collective-permute-start | bytes 1572872 | tf_op jit(solution)/shard_map/swap_back/ppermute | solution.py:751
  128.7 2.7 %collective-permute-start.21 = (bf16[128,1024]{1,0:T(8,128)(2,1)}, bf16[128,1024]{1,0:T(8,128)(2,1)}, u32[]{:S(2)}, u32[]{:S(2)}) collective-permute-start(bf16[128,1024]{1,0:T(8,128)(2,1)} %get-tuple-element.124), channel_id=1, source_target_pairs={{0,1},{1,0},{2,3},{3,2},{4,5},{5,4},{6,7},{7,6},{8,9},{9,8},{10,11... | collective-permute-start | bytes 786440 | tf_op jit(solution)/shard_map/swap_back/ppermute | solution.py:751
  129.1 2.3 %collective-permute-start.20 = (bf16[128,512]{1,0:T(8,128)(2,1)}, bf16[128,512]{1,0:T(8,128)(2,1)}, u32[]{:S(2)}, u32[]{:S(2)}) collective-permute-start(bf16[128,512]{1,0:T(8,128)(2,1)} %get-tuple-element.123), channel_id=1, source_target_pairs={{0,1},{1,0},{2,3},{3,2},{4,5},{5,4},{6,7},{7,6},{8,9},{9,8},{10,11... | collective-permute-start | bytes 393224 | tf_op jit(solution)/shard_map/swap_back/ppermute | solution.py:751

commit v6 on v5

--- a/solution.py
+++ b/solution.py
@@ -525,12 +525,13 @@
     return (2 * (me % 2) + core) ^ me
 
 
-def back_kernel(sc_ref, own_ref, other_ref, *refs):
-    bo_ref, bx_ref = refs[8:]
-    scaled = jnp.concatenate([own_ref[...], other_ref[...]], axis=0)
+def back_kernel(sc_ref, *refs):
+    bo_ref, bx_ref = refs[16:]
+    scaled = jnp.concatenate(
+        [jnp.concatenate([refs[n][...], refs[4 + n][...]], axis=0) for n in range(4)], axis=1)
     first = pl.program_id(0) < 2
     weight = jnp.concatenate(
-        [jnp.where(first, refs[n][...], refs[4 + n][...]) for n in range(4)], axis=1)
+        [jnp.where(first, refs[8 + n][...], refs[12 + n][...]) for n in range(4)], axis=1)
     product = dot1(scaled, weight, NT).astype(BF16)
     bo_ref[...] = product[:T]
     bx_ref[...] = product[T:]
@@ -539,7 +540,7 @@
 def back_local(sc, own, other, weights):
     features, columns = weights[0].shape
     width, part = features // 2, columns // 4
-    tokens = block((T, columns), lambda i, sc: (0, 0))
+    tokens = [block((T, part), lambda i, sc, n=n: (0, n)) for n in range(4)]
     out = block((T, width), lambda i, sc: (0, 2 * ((i // 2) ^ (sc[1] % 2)) + i % 2))
     early = [block((width, part), lambda i, sc, n=n: (jnp.minimum(i, 1), n)) for n in range(4)]
     late = [block((width, part), lambda i, sc, n=n: (jnp.maximum(i - 2, 0), n)) for n in range(4)]
@@ -548,14 +549,14 @@
         grid_spec=pltpu.PrefetchScalarGridSpec(
             num_scalar_prefetch=1,
             grid=(4,),
-            in_specs=[tokens, tokens] + early + late,
+            in_specs=tokens + tokens + early + late,
             out_specs=[out, out],
         ),
         out_shape=[shape((T, 2 * features))] * 2,
         compiler_params=PARAMS,
         cost_estimate=cost(0.01),
         name="back_local",
-    )(sc, own, other, *[weights[0]] * 4, *[weights[1]] * 4)
+    )(sc, *[own] * 4, *[other] * 4, *[weights[0]] * 4, *[weights[1]] * 4)
 
 
 def mixed_kernel(sc_ref, no_ref, nx_ref, *refs):
@@ -593,7 +594,7 @@
 
 
 def weight_kernel(sc_ref, *refs):
-    keep_ref, send_ref, rows_ref, part_ref, sems = refs[8:]
+    keep_ref, send_ref, rows_ref, part_ref, sems = refs[20:]
     for n in range(4):
         rows_ref[n ^ turn(sc_ref)] = refs[n][...]
     rows = rows_ref[...].reshape(4 * T, rows_ref.shape[2])
@@ -603,7 +604,7 @@
     copies = []
     for n in range(4):
         lanes = slice(n * width, (n + 1) * width)
-        scaled = jnp.concatenate([ref[:, lanes] for ref in refs[4:8]], axis=0)
+        scaled = jnp.concatenate([ref[...] for ref in refs[4 + n:20:4]], axis=0)
         part_ref[:, :, :, lanes] = dot1(rows, scaled, TN).astype(BF16).reshape(
             chips, cores, height, width)
         for m in range(2):
@@ -625,7 +626,8 @@
         grid_spec=pltpu.PrefetchScalarGridSpec(
             num_scalar_prefetch=1,
             grid=(1,),
-            in_specs=[same(part) for part in rows + scaled],
+            in_specs=[same(part) for part in rows]
+            + [block((T, columns // 4), lambda i, sc, n=n: (0, n)) for n in range(4)] * 4,
             out_specs=[pl.BlockSpec(memory_space=pl.ANY)] * 2,
             scratch_shapes=[pltpu.VMEM((4, T, features), BF16),
                             pltpu.VMEM((features // 32, 2, 16, columns), BF16),
@@ -635,7 +637,7 @@
         compiler_params=PARAMS,
         cost_estimate=cost(4),
         name="weight_local",
-    )(sc, *rows, *scaled)
+    )(sc, *rows, *[part for part in scaled for _ in range(4)])
 
 
 def join_kernel(*refs):

time: 140 us -> 140 us (level)
  no operation moved by 1% of the time
where the time goes in v6:
time: 140 us; the launch traced here: 137 us
  Pallas kernels  64.3 us (46%)
  starting transfers between devices  54.6 us (39%)
  waiting for transfers between devices  16.6 us (12%)
    all_to_all x5, starting transfers between devices, exchange(): lax.all_to_all(x, 'ctx', split_axis=0, concat_axis=0, tiled=True, axis_in...  32.8 us
    ppermute x16, starting transfers between devices, cross(): return lax.ppermute(x, axis, [(i, i ^ distance) for i in range(count)])  8.71 us
    pallas_call x1, Pallas kernels, body(): ab, t, u0, kg, a, b = write_local(sc, k, v, ld, be, k_x, v_x, ld_x, be_x)  8.54 us
    pallas_call x1, Pallas kernels, body(): gate_local(sc, entering, gate, ld, be, gate_x, ld_x, be_x, *bg, a, b, io,...  7.92 us
    pallas_call x2, Pallas kernels, chain(): pl.pallas_call(kernel, grid=(1,), in_specs=streams + [whole] * len(args),...  7.84 us
    ppermute x4, starting transfers between devices, feature_round(): return lax.ppermute(x, ('fsdp', 'ctx'), pairs)  7.81 us
    ppermute x2, waiting for transfers between devices, weight_round(): return lax.ppermute(x, ('fsdp', 'ctx'), pairs)  6.24 us
    pallas_call x1, Pallas kernels, back_local(): pl.pallas_call(back_kernel, grid_spec=pltpu.PrefetchScalarGridSpec(num_sc...  6.17 us
  transfers between devices with their start and end apart: 27, of which 6 were waited for; matrix products, arithmetic and copies ran while one was open for 0% of the time, Pallas kernels for 45%

profile of v6, /device:TPU:0, one launch (start us, length us, event | category | flops | bytes accessed | tf_op | source)
XLA Modules:
  0.0 137.0 jit_solution(8473633784939603877)
XLA Ops:
  0.6 0.1 collective-permute-start.3
  0.7 0.5 collective-permute-start
  1.2 0.1 collective-permute-start.1
  1.3 0.4 collective-permute-start.2
  1.7 4.1 %collective-permute-start.8 = (bf16[512,2048]{1,0:T(8,128)(2,1)}, bf16[512,2048]{1,0:T(8,128)(2,1)}, u32[]{:S(2)}, u32[]{:S(2)}) collective-permute-start(bf16[512,2048]{1,0:T(8,128)(2,1)} %param.17), channel_id=1, source_target_pairs={{33,0},{97,1},{35,2},{99,3},{37,4},{101,5},{39,6},{103,7},{41,8},{... | collective-permute-start | bytes 6291464 | tf_op jit(solution)/shard_map/out_weight/ppermute | solution.py:781
  5.9 0.6 pad_add_fusion.sc_ref
  6.5 0.0 collective-permute-done.1.lx_ref
  6.5 1.2 collective-permute-start.7
  7.7 0.0 collective-permute-done.2.rx_ref
  7.7 0.0 collective-permute-done.kx_ref
  7.7 0.0 collective-permute-done.3.vx_ref
  7.7 8.5 %write_local.1 = (bf16[16,208,128]{2,1,0:T(8,128)(2,1)}, bf16[16,128,128]{2,1,0:T(8,128)(2,1)}, bf16[16,128,128]{2,1,0:T(8,128)(2,1)}, bf16[16,128,128]{2,1,0:T(...) custom-call(s32[3]{0:T(128)} %pad_add_fusion.sc_ref, bf16[128,1024]{1,0:T(8,128)(2,1)} %bitcast.28, ...), custom_call_target="tpu_custom_call" | custom-call | flops 17999998976 | bytes 65536 | tf_op jit(solution)/shard_map/write_local/pallas_call | solution.py:798
  16.2 7.1 %all-to-all-start = ((bf16[16,208,128]{2,1,0:T(8,128)(2,1)}), bf16[16,208,128]{2,1,0:T(8,128)(2,1)}, u32[]{:S(2)}, u32[]{:S(2)}) async-start(bf16[16,208,128]{2,1,0:T(8,128)(2,1)} %get-tuple-element.69), calls=%async_computation | async-start | bytes 1703936 | tf_op jit(solution)/shard_map/all_to_all | solution.py:747
  23.3 2.6 %scale_local.1.refs_0_.refs_1_.refs_2_.refs_3_.refs_4_.refs_5_.refs_6_.refs_7_ = bf16[128,2048]{1,0:T(8,128)(2,1)} custom-call(s32[3]{0:T(128)} %pad_add_fusion.sc_ref, s32[4]{0:T(128)} %lengths_ref.1, s32[4]{0:T(128)} %pairing_ref.1, f32[4]{0:T(128)} %ratio_ref.1, bf16[128,2048]{1,0:T(8,128)(2,1)} %bitcast.22), custom_call_target="tpu_custom_call" | custom-call | flops 10000000 | bytes 65536 | tf_op jit(solution)/shard_map/every_scaled/scale_local/pallas_call | solution.py:508
  25.9 0.0 collective-permute-start.6
  25.9 0.5 collective-permute-start.5
  26.4 0.0 collective-permute-start.4
  26.4 2.9 %collective-permute-done.4.qx_ref = bf16[128,1024]{1,0:T(8,128)(2,1)} collective-permute-done((bf16[128,1024]{1,0:T(8,128)(2,1)}, bf16[128,1024]{1,0:T(8,128)(2,1)}, u32[]{:S(2)}, u32[]{:S(2)}) %collective-permute-start.4) | collective-permute-done | bytes 262176 | tf_op jit(solution)/shard_map/swap_heads/ppermute | solution.py:753
  29.2 4.1 %read_local.1 = (bf16[16,128,128]{2,1,0:T(8,128)(2,1)}, bf16[16,128,128]{2,1,0:T(8,128)(2,1)}, bf16[16,128,128]{2,1,0:T(8,128)(2,1)}) custom-call(s32[3]{0:T(128)} %pad_add_fusion.sc_ref, bf16[128,1024]{1,0:T(8,128)(2,1)} %bitcast.25, bf16[128,1024]{1,0:T(8,128)(2,1)} %bitcast.29, f32[16,128]{1,0:T(8,128)} %bitcast.36, f32[16,128]{1,0:T(8,128)} %bitcast.41, ...), custom_call_target="tpu_custom_call" | custom-call | flops 10000000 | bytes 65536 | tf_op jit(solution)/shard_map/read_local/pallas_call | solution.py:805
  33.3 4.5 %all-to-all-done.refs_0_.refs_1_.refs_2_.refs_3_ = bf16[16,208,128]{2,1,0:T(8,128)(2,1)} async-done(((bf16[16,208,128]{2,1,0:T(8,128)(2,1)}), bf16[16,208,128]{2,1,0:T(8,128)(2,1)}, u32[]{:S(2)}, u32[]{:S(2)}) %all-to-all-start) | async-done | bytes 852000 | tf_op jit(solution)/shard_map/all_to_all | solution.py:747
  37.9 3.9 %chain.2 = bf16[16,64,128]{2,1,0:T(8,128)(2,1)} custom-call(bf16[16,208,128]{2,1,0:T(8,128)(2,1)} %all-to-all-done.refs_0_.refs_1_.refs_2_.refs_3_, bf16[16,208,128]{2,1,0:T(8,128)(2,1)} %all-to-all-done.refs_0_.refs_1_.refs_2_.refs_3_, bf16[16,208,128]{2,1,0:T(8,128)(2,1)} %all-to-all-done.refs_0_.refs_1_.refs_2_.refs_3_, ...), custom_call_target="tpu_custom_call" | custom-call | flops 10000000 | bytes 65536 | tf_op jit(solution)/shard_map/chain/pallas_call | solution.py:473
  41.8 4.2 %all-to-all-start.1 = ((bf16[16,64,128]{2,1,0:T(8,128)(2,1)}), bf16[16,64,128]{2,1,0:T(8,128)(2,1)}, u32[]{:S(2)}, u32[]{:S(2)}) async-start(bf16[16,64,128]{2,1,0:T(8,128)(2,1)} %chain.2), calls=%async_computation.1 | async-start | bytes 524288 | tf_op jit(solution)/shard_map/all_to_all | solution.py:747
  46.0 6.2 %collective-permute-done.8.refs_12_.refs_13_.refs_14_.refs_15_.refs_4_.refs_5_.refs_6_.refs_7_ = bf16[512,2048]{1,0:T(8,128)(2,1)} collective-permute-done((bf16[512,2048]{1,0:T(8,128)(2,1)}, bf16[512,2048]{1,0:T(8,128)(2,1)}, u32[]{:S(2)}, u32[]{:S(2)}) %collective-permute-start.8) | collective-permute-done | bytes 2097184 | tf_op jit(solution)/shard_map/out_weight/ppermute | solution.py:781
  52.2 0.0 collective-permute-done.7.refs_8_.refs_9_.refs_10_.refs_11_.refs_0_.refs_1_.refs_2_.refs_3_
  52.2 3.7 %collective-permute-start.11 = (bf16[128,2048]{1,0:T(8,128)(2,1)}, bf16[128,2048]{1,0:T(8,128)(2,1)}, u32[]{:S(2)}, u32[]{:S(2)}) collective-permute-start(bf16[128,2048]{1,0:T(8,128)(2,1)} %scale_local.1.refs_0_.refs_1_.refs_2_.refs_3_.refs_4_.refs_5_.refs_6_.refs_7_), channel_id=1, source_target_pairs={{0,96},{32,64},{64,32},{96,0},{1,97},{33,65},{65,33},{97,1},{2,98}... | collective-permute-start | bytes 1572872 | tf_op jit(solution)/shard_map/every_scaled/ppermute | solution.py:753
  55.9 0.0 collective-permute-start.10
  55.9 0.9 collective-permute-start.9
  56.8 0.0 collective-permute-done.6.refs_4_.refs_5_.refs_6_.refs_7_
  56.8 6.2 %back_local.1 = (bf16[128,1024]{1,0:T(8,128)(2,1)}, bf16[128,1024]{1,0:T(8,128)(2,1)}) custom-call(s32[3]{0:T(128)} %pad_add_fusion.sc_ref, bf16[128,2048]{1,0:T(8,128)(2,1)} %scale_local.1.refs_0_.refs_1_.refs_2_.refs_3_.refs_4_.refs_5_.refs_6_.refs_7_, bf16[128,2048]{1,0:T(8,128)(2,1)} %scale_local.1.refs_0_.refs_1_.refs_2_.refs_3_.refs_4_.refs_5_.refs_6_.refs_7_, ...), custom_call_target="tpu_custom_call" | custom-call | flops 10000000 | bytes 65536 | tf_op jit(solution)/shard_map/back_grad/back_local/pallas_call | solution.py:547
  62.9 0.0 collective-permute-done.5.gx_ref
  62.9 0.0 all-to-all-done.1
  63.0 7.9 %gate_local.1 = (bf16[128,512]{1,0:T(8,128)(2,1)}, bf16[128,512]{1,0:T(8,128)(2,1)}, bf16[128,512]{1,0:T(8,128)(2,1)}, bf16[128,512]{1,0:T(8,128)(2,1)}, bf16[12...) custom-call(s32[3]{0:T(128)} %pad_add_fusion.sc_ref, ...), custom_call_target="tpu_custom_call" | custom-call | flops 12000000000 | bytes 65536 | tf_op jit(solution)/shard_map/gate_local/pallas_call | solution.py:814
  70.9 7.1 %all-to-all-start.2 = ((bf16[16,64,128]{2,1,0:T(8,128)(2,1)}), bf16[16,64,128]{2,1,0:T(8,128)(2,1)}, u32[]{:S(2)}, u32[]{:S(2)}) async-start(bf16[16,64,128]{2,1,0:T(8,128)(2,1)} %bitcast.33), calls=%async_computation.2 | async-start | bytes 524288 | tf_op jit(solution)/shard_map/all_to_all | solution.py:747
  78.0 2.2 %collective-permute-start.12 = (bf16[128,512]{1,0:T(8,128)(2,1)}, bf16[128,512]{1,0:T(8,128)(2,1)}, u32[]{:S(2)}, u32[]{:S(2)}) collective-permute-start(bf16[128,512]{1,0:T(8,128)(2,1)} %get-tuple-element.90), channel_id=1, source_target_pairs={{0,0},{1,64},{2,2},{3,66},{4,4},{5,68},{6,6},{7,70},{8,8},{9,72},{... | collective-permute-start | bytes 393224 | tf_op jit(solution)/shard_map/every_normed/ppermute | solution.py:773
  80.2 2.6 %collective-permute-start.13 = (bf16[128,512]{1,0:T(8,128)(2,1)}, bf16[128,512]{1,0:T(8,128)(2,1)}, u32[]{:S(2)}, u32[]{:S(2)}) collective-permute-start(bf16[128,512]{1,0:T(8,128)(2,1)} %get-tuple-element.91), channel_id=1, source_target_pairs={{0,1},{1,65},{2,3},{3,67},{4,5},{5,69},{6,7},{7,71},{8,9},{9,73},{... | collective-permute-start | bytes 393224 | tf_op jit(solution)/shard_map/every_normed/ppermute | solution.py:773
  82.8 0.0 collective-permute-done.11.refs_16_.refs_17_.refs_18_.refs_19_
  82.8 0.0 collective-permute-start.14
  82.8 0.0 collective-permute-done.10.refs_12_.refs_13_.refs_14_.refs_15_
  82.8 3.0 %collective-permute-start.15 = (bf16[128,512]{1,0:T(8,128)(2,1)}, bf16[128,512]{1,0:T(8,128)(2,1)}, u32[]{:S(2)}, u32[]{:S(2)}) collective-permute-start(bf16[128,512]{1,0:T(8,128)(2,1)} %get-tuple-element.93), channel_id=1, source_target_pairs={{0,33},{1,97},{2,35},{3,99},{4,37},{5,101},{6,39},{7,103},{8,41},{... | collective-permute-start | bytes 393224 | tf_op jit(solution)/shard_map/every_normed/ppermute | solution.py:773
  85.8 0.0 collective-permute-done.9.refs_8_.refs_9_.refs_10_.refs_11_
  85.8 1.2 collective-permute-start.17
  87.1 0.0 all-to-all-done.2.refs_4_
  87.1 4.0 %chain.3 = bf16[16,64,128]{2,1,0:T(8,128)(2,1)} custom-call(bf16[16,208,128]{2,1,0:T(8,128)(2,1)} %all-to-all-done.refs_0_.refs_1_.refs_2_.refs_3_, bf16[16,208,128]{2,1,0:T(8,128)(2,1)} %all-to-all-done.refs_0_.refs_1_.refs_2_.refs_3_, bf16[16,208,128]{2,1,0:T(8,128)(2,1)} %all-to-all-done.refs_0_.refs_1_.refs_2_.refs_3_, ...), custom_call_target="tpu_custom_call" | custom-call | flops 10000000 | bytes 65536 | tf_op jit(solution)/shard_map/chain/pallas_call | solution.py:473
  91.1 7.2 %all-to-all-start.3 = ((bf16[16,64,128]{2,1,0:T(8,128)(2,1)}), bf16[16,64,128]{2,1,0:T(8,128)(2,1)}, u32[]{:S(2)}, u32[]{:S(2)}) async-start(bf16[16,64,128]{2,1,0:T(8,128)(2,1)} %chain.3), calls=%async_computation.3 | async-start | bytes 524288 | tf_op jit(solution)/shard_map/all_to_all | solution.py:747
  98.3 0.0 collective-permute-done.12.refs_0_
  98.3 0.1 collective-permute-start.16
  98.4 0.0 collective-permute-done.13.refs_1_
  98.4 0.0 collective-permute-done.15.refs_3_
  98.4 5.3 %weight_local.1 = (bf16[16,16,2048]{2,1,0:T(8,128)(2,1)}, bf16[16,16,2048]{2,1,0:T(8,128)(2,1)}) custom-call(s32[3]{0:T(128)} %pad_add_fusion.sc_ref, bf16[128,512]{1,0:T(8,128)(2,1)} %collective-permute-done.12.refs_0_, bf16[128,512]{1,0:T(8,128)(2,1)} %collective-permute-done.13.refs_1_, bf16[128,512]{1,0:T(8,128)(2,1)} %collective-permute-done.14.refs_2_, ...), custom_call_target="tpu_custom_call" | custom-call | flops 4000000000 | bytes 65536 | tf_op jit(solution)/shard_map/weight_grad/weight_local/pallas_call | solution.py:624
  103.7 0.6 collective-permute-start.18
  104.3 2.4 %fill.1 = (bf16[128,2048]{1,0:T(8,128)(2,1)}, bf16[128,1024]{1,0:T(8,128)(2,1)}) custom-call(s32[3]{0:T(128)} %pad_add_fusion.sc_ref, bf16[128,2048]{1,0:T(8,128)(2,1)} %get-tuple-element.103.refs_0_, bf16[128,1024]{1,0:T(8,128)(2,1)} %get-tuple-element.104.refs_1_, ...), custom_call_target="tpu_custom_call", output_to_operand_aliasing={{0}: (1, {}), {1}: (2, {})} | custom-call | flops 24999999488 | bytes 65536 | tf_op jit(solution)/shard_map/weight_grad/fill/pallas_call | solution.py:691
  106.7 0.2 collective-permute-done.18.refs_2_.refs_3_
  106.9 2.4 %join.1 = bf16[16,16,2048]{2,1,0:T(8,128)(2,1)} custom-call(bf16[16,16,2048]{2,1,0:T(8,128)(2,1)} %get-tuple-element.108.refs_0_.refs_1_, bf16[16,16,2048]{2,1,0:T(8,128)(2,1)} %get-tuple-element.108.refs_0_.refs_1_, bf16[16,16,2048]{2,1,0:T(8,128)(2,1)} %collective-permute-done.18.refs_2_.refs_3_, bf16[16,16,2048]{2,1,0:T(8,128)(2,1)} %collective-permute-done.18.refs_2_.refs_3_), custom_call_target="tpu_custom_call" | custom-call | flops 10000000 | bytes 65536 | tf_op jit(solution)/shard_map/weight_grad/join/pallas_call | solution.py:651
  109.3 0.0 all-to-all-done.3
  109.3 7.2 %all-to-all-start.4 = ((bf16[16,16,2048]{2,1,0:T(8,128)(2,1)}), bf16[16,16,2048]{2,1,0:T(8,128)(2,1)}, u32[]{:S(2)}, u32[]{:S(2)}) async-start(bf16[16,16,2048]{2,1,0:T(8,128)(2,1)} %join.1), calls=%async_computation.4 | async-start | bytes 2097152 | tf_op jit(solution)/shard_map/weight_grad/all_to_all | solution.py:747
  116.6 6.0 %late_local.1 = (bf16[128,1024]{1,0:T(8,128)(2,1)}, bf16[128,2048]{1,0:T(8,128)(2,1)}, bf16[128,512]{1,0:T(8,128)(2,1)}, bf16[128,1024]{1,0:T(8,128)(2,1)}) custom-call(s32[3]{0:T(128)} %pad_add_fusion.sc_ref, bf16[128,1024]{1,0:T(8,128)(2,1)} %bitcast.31, f32[16,128]{1,0:T(8,128)} %bitcast.38, f32[16,128]{1,0:T(8,128)} %bitcast.43, ...), custom_call_target="tpu_custom_call" | custom-call | flops 49999998976 | bytes 65536 | tf_op jit(solution)/shard_map/late_local/pallas_call | solution.py:831
  122.6 5.9 %mixed_local.1 = (f32[128,2048]{1,0:T(8,128)}, bf16[128,2048]{1,0:T(8,128)(2,1)}) custom-call(s32[3]{0:T(128)} %pad_add_fusion.sc_ref, bf16[128,1024]{1,0:T(8,128)(2,1)} %get-tuple-element.117.no_ref, bf16[128,1024]{1,0:T(8,128)(2,1)} %get-tuple-element.118.nx_ref, ...), custom_call_target="tpu_custom_call" | custom-call | flops 10000000 | bytes 65536 | tf_op jit(solution)/shard_map/mixed_out/mixed_local/pallas_call | solution.py:581
  128.5 0.2 collective-permute-start.19
  128.7 0.4 collective-permute-start.21
  129.1 0.1 collective-permute-start.20
  129.2 2.2 %collective-permute-done.20.refs_5_ = bf16[128,512]{1,0:T(8,128)(2,1)} collective-permute-done((bf16[128,512]{1,0:T(8,128)(2,1)}, bf16[128,512]{1,0:T(8,128)(2,1)}, u32[]{:S(2)}, u32[]{:S(2)}) %collective-permute-start.20) | collective-permute-done | bytes 131104 | tf_op jit(solution)/shard_map/swap_back/ppermute | solution.py:753
  131.4 3.0 %finish.1 = (bf16[128,2048]{1,0:T(8,128)(2,1)}, bf16[128,1024]{1,0:T(8,128)(2,1)}, bf16[128,2048]{1,0:T(8,128)(2,1)}) custom-call(s32[3]{0:T(128)} %pad_add_fusion.sc_ref, f32[128,2048]{1,0:T(8,128)} %get-tuple-element.119.refs_0_.refs_1_, f32[128,2048]{1,0:T(8,128)} %get-tuple-element.119.refs_0_.refs_1_, ...), custom_call_target="tpu_custom_call", output_to_operand_aliasing={{1}: (4, {}), {2}: (5, {})} | custom-call | flops 10000000 | bytes 65536 | tf_op jit(solution)/shard_map/swap_back/finish/pallas_call | solution.py:723
  134.4 0.5 all-to-all-done.4.refs_0_.refs_1_.refs_2_.refs_3_.refs_4_.refs_5_.refs_6_.refs_7_
  134.9 2.1 %total.1 = f32[16,2048]{1,0:T(8,128)} custom-call(bf16[16,16,2048]{2,1,0:T(8,128)(2,1)} %all-to-all-done.4.refs_0_.refs_1_.refs_2_.refs_3_.refs_4_.refs_5_.refs_6_.refs_7_, bf16[16,16,2048]{2,1,0:T(8,128)(2,1)} %all-to-all-done.4.refs_0_.refs_1_.refs_2_.refs_3_.refs_4_.refs_5_.refs_6_.refs_7_, ...), custom_call_target="tpu_custom_call" | custom-call | flops 10000000 | bytes 65536 | tf_op jit(solution)/shard_map/weight_grad/total/pallas_call | solution.py:670
  (5 shorter events, 0.0 us)
Async XLA Ops:
  0.6 7.0 %collective-permute-start.3 = (bf16[128,2048]{1,0:T(8,128)(2,1)}, bf16[128,2048]{1,0:T(8,128)(2,1)}, u32[]{:S(2)}, u32[]{:S(2)}) collective-permute-start(bf16[128,2048]{1,0:T(8,128)(2,1)} %bitcast.44), channel_id=1, source_target_pairs={{0,1},{1,0},{2,3},{3,2},{4,5},{5,4},{6,7},{7,6},{8,9},{9,8},{10,11... | collective-permute-start | bytes 1572872 | tf_op jit(solution)/shard_map/swap_heads/ppermute | solution.py:753
  0.7 6.9 %collective-permute-start = (bf16[128,1024]{1,0:T(8,128)(2,1)}, bf16[128,1024]{1,0:T(8,128)(2,1)}, u32[]{:S(2)}, u32[]{:S(2)}) collective-permute-start(bf16[128,1024]{1,0:T(8,128)(2,1)} %bitcast.27), channel_id=1, source_target_pairs={{0,1},{1,0},{2,3},{3,2},{4,5},{5,4},{6,7},{7,6},{8,9},{9,8},{10,11... | collective-permute-start | bytes 786440 | tf_op jit(solution)/shard_map/swap_heads/ppermute | solution.py:753
  1.2 5.3 %collective-permute-start.1 = (f32[16,128]{1,0:T(8,128)}, f32[16,128]{1,0:T(8,128)}, u32[]{:S(2)}, u32[]{:S(2)}) collective-permute-start(f32[16,128]{1,0:T(8,128)} %bitcast.34), channel_id=1, source_target_pairs={{0,1},{1,0},{2,3},{3,2},{4,5},{5,4},{6,7},{7,6},{8,9},{9,8},{10,11... | collective-permute-start | bytes 24584 | tf_op jit(solution)/shard_map/swap_heads/ppermute | solution.py:753
  1.3 6.3 %collective-permute-start.2 = (f32[16,128]{1,0:T(8,128)}, f32[16,128]{1,0:T(8,128)}, u32[]{:S(2)}, u32[]{:S(2)}) collective-permute-start(f32[16,128]{1,0:T(8,128)} %bitcast.39), channel_id=1, source_target_pairs={{0,1},{1,0},{2,3},{3,2},{4,5},{5,4},{6,7},{7,6},{8,9},{9,8},{10,11... | collective-permute-start | bytes 24584 | tf_op jit(solution)/shard_map/swap_heads/ppermute | solution.py:753
  1.7 50.5 %collective-permute-start.8 = (bf16[512,2048]{1,0:T(8,128)(2,1)}, bf16[512,2048]{1,0:T(8,128)(2,1)}, u32[]{:S(2)}, u32[]{:S(2)}) collective-permute-start(bf16[512,2048]{1,0:T(8,128)(2,1)} %param.17), channel_id=1, source_target_pairs={{33,0},{97,1},{35,2},{99,3},{37,4},{101,5},{39,6},{103,7},{41,8},{... | collective-permute-start | bytes 6291464 | tf_op jit(solution)/shard_map/out_weight/ppermute | solution.py:781
  6.5 45.7 %collective-permute-start.7 = (bf16[512,2048]{1,0:T(8,128)(2,1)}, bf16[512,2048]{1,0:T(8,128)(2,1)}, u32[]{:S(2)}, u32[]{:S(2)}) collective-permute-start(bf16[512,2048]{1,0:T(8,128)(2,1)} %param.17), channel_id=1, source_target_pairs={{1,0},{65,1},{3,2},{67,3},{5,4},{69,5},{7,6},{71,7},{9,8},{73,9},{... | collective-permute-start | bytes 6291464 | tf_op jit(solution)/shard_map/out_weight/ppermute | solution.py:781
  16.2 21.7 %all-to-all-start = ((bf16[16,208,128]{2,1,0:T(8,128)(2,1)}), bf16[16,208,128]{2,1,0:T(8,128)(2,1)}, u32[]{:S(2)}, u32[]{:S(2)}) async-start(bf16[16,208,128]{2,1,0:T(8,128)(2,1)} %get-tuple-element.69), calls=%async_computation | async-start | bytes 1703936 | tf_op jit(solution)/shard_map/all_to_all | solution.py:747
  25.9 30.9 %collective-permute-start.6 = (bf16[128,2048]{1,0:T(8,128)(2,1)}, bf16[128,2048]{1,0:T(8,128)(2,1)}, u32[]{:S(2)}, u32[]{:S(2)}) collective-permute-start(bf16[128,2048]{1,0:T(8,128)(2,1)} %scale_local.1.refs_0_.refs_1_.refs_2_.refs_3_.refs_4_.refs_5_.refs_6_.refs_7_), channel_id=1, source_target_pairs={{0,1},{1,0},{2,3},{3,2},{4,5},{5,4},{6,7},{7,6},{8,9},{9,8},{10,11... | collective-permute-start | bytes 1572872 | tf_op jit(solution)/shard_map/swap_heads/ppermute | solution.py:753
  25.9 37.1 %collective-permute-start.5 = (bf16[128,2048]{1,0:T(8,128)(2,1)}, bf16[128,2048]{1,0:T(8,128)(2,1)}, u32[]{:S(2)}, u32[]{:S(2)}) collective-permute-start(bf16[128,2048]{1,0:T(8,128)(2,1)} %bitcast.46), channel_id=1, source_target_pairs={{0,1},{1,0},{2,3},{3,2},{4,5},{5,4},{6,7},{7,6},{8,9},{9,8},{10,11... | collective-permute-start | bytes 1572872 | tf_op jit(solution)/shard_map/swap_heads/ppermute | solution.py:753
  26.4 2.9 %collective-permute-start.4 = (bf16[128,1024]{1,0:T(8,128)(2,1)}, bf16[128,1024]{1,0:T(8,128)(2,1)}, u32[]{:S(2)}, u32[]{:S(2)}) collective-permute-start(bf16[128,1024]{1,0:T(8,128)(2,1)} %bitcast.24), channel_id=1, source_target_pairs={{0,1},{1,0},{2,3},{3,2},{4,5},{5,4},{6,7},{7,6},{8,9},{9,8},{10,11... | collective-permute-start | bytes 786440 | tf_op jit(solution)/shard_map/swap_heads/ppermute | solution.py:753
  41.8 21.2 %all-to-all-start.1 = ((bf16[16,64,128]{2,1,0:T(8,128)(2,1)}), bf16[16,64,128]{2,1,0:T(8,128)(2,1)}, u32[]{:S(2)}, u32[]{:S(2)}) async-start(bf16[16,64,128]{2,1,0:T(8,128)(2,1)} %chain.2), calls=%async_computation.1 | async-start | bytes 524288 | tf_op jit(solution)/shard_map/all_to_all | solution.py:747
  52.2 30.6 %collective-permute-start.11 = (bf16[128,2048]{1,0:T(8,128)(2,1)}, bf16[128,2048]{1,0:T(8,128)(2,1)}, u32[]{:S(2)}, u32[]{:S(2)}) collective-permute-start(bf16[128,2048]{1,0:T(8,128)(2,1)} %scale_local.1.refs_0_.refs_1_.refs_2_.refs_3_.refs_4_.refs_5_.refs_6_.refs_7_), channel_id=1, source_target_pairs={{0,96},{32,64},{64,32},{96,0},{1,97},{33,65},{65,33},{97,1},{2,98}... | collective-permute-start | bytes 1572872 | tf_op jit(solution)/shard_map/every_scaled/ppermute | solution.py:753
  55.9 26.9 %collective-permute-start.10 = (bf16[128,2048]{1,0:T(8,128)(2,1)}, bf16[128,2048]{1,0:T(8,128)(2,1)}, u32[]{:S(2)}, u32[]{:S(2)}) collective-permute-start(bf16[128,2048]{1,0:T(8,128)(2,1)} %scale_local.1.refs_0_.refs_1_.refs_2_.refs_3_.refs_4_.refs_5_.refs_6_.refs_7_), channel_id=1, source_target_pairs={{0,64},{32,96},{64,0},{96,32},{1,65},{33,97},{65,1},{97,33},{2,66}... | collective-permute-start | bytes 1572872 | tf_op jit(solution)/shard_map/every_scaled/ppermute | solution.py:753
  55.9 29.9 %collective-permute-start.9 = (bf16[128,2048]{1,0:T(8,128)(2,1)}, bf16[128,2048]{1,0:T(8,128)(2,1)}, u32[]{:S(2)}, u32[]{:S(2)}) collective-permute-start(bf16[128,2048]{1,0:T(8,128)(2,1)} %scale_local.1.refs_0_.refs_1_.refs_2_.refs_3_.refs_4_.refs_5_.refs_6_.refs_7_), channel_id=1, source_target_pairs={{0,32},{32,0},{64,96},{96,64},{1,33},{33,1},{65,97},{97,65},{2,34}... | collective-permute-start | bytes 1572872 | tf_op jit(solution)/shard_map/every_scaled/ppermute | solution.py:753
  70.9 16.2 %all-to-all-start.2 = ((bf16[16,64,128]{2,1,0:T(8,128)(2,1)}), bf16[16,64,128]{2,1,0:T(8,128)(2,1)}, u32[]{:S(2)}, u32[]{:S(2)}) async-start(bf16[16,64,128]{2,1,0:T(8,128)(2,1)} %bitcast.33), calls=%async_computation.2 | async-start | bytes 524288 | tf_op jit(solution)/shard_map/all_to_all | solution.py:747
  78.0 20.3 %collective-permute-start.12 = (bf16[128,512]{1,0:T(8,128)(2,1)}, bf16[128,512]{1,0:T(8,128)(2,1)}, u32[]{:S(2)}, u32[]{:S(2)}) collective-permute-start(bf16[128,512]{1,0:T(8,128)(2,1)} %get-tuple-element.90), channel_id=1, source_target_pairs={{0,0},{1,64},{2,2},{3,66},{4,4},{5,68},{6,6},{7,70},{8,8},{9,72},{... | collective-permute-start | bytes 393224 | tf_op jit(solution)/shard_map/every_normed/ppermute | solution.py:773
  80.2 18.2 %collective-permute-start.13 = (bf16[128,512]{1,0:T(8,128)(2,1)}, bf16[128,512]{1,0:T(8,128)(2,1)}, u32[]{:S(2)}, u32[]{:S(2)}) collective-permute-start(bf16[128,512]{1,0:T(8,128)(2,1)} %get-tuple-element.91), channel_id=1, source_target_pairs={{0,1},{1,65},{2,3},{3,67},{4,5},{5,69},{6,7},{7,71},{8,9},{9,73},{... | collective-permute-start | bytes 393224 | tf_op jit(solution)/shard_map/every_normed/ppermute | solution.py:773
  82.8 15.6 %collective-permute-start.14 = (bf16[128,512]{1,0:T(8,128)(2,1)}, bf16[128,512]{1,0:T(8,128)(2,1)}, u32[]{:S(2)}, u32[]{:S(2)}) collective-permute-start(bf16[128,512]{1,0:T(8,128)(2,1)} %get-tuple-element.92), channel_id=1, source_target_pairs={{0,32},{1,96},{2,34},{3,98},{4,36},{5,100},{6,38},{7,102},{8,40},{... | collective-permute-start | bytes 393224 | tf_op jit(solution)/shard_map/every_normed/ppermute | solution.py:773
  82.8 15.6 %collective-permute-start.15 = (bf16[128,512]{1,0:T(8,128)(2,1)}, bf16[128,512]{1,0:T(8,128)(2,1)}, u32[]{:S(2)}, u32[]{:S(2)}) collective-permute-start(bf16[128,512]{1,0:T(8,128)(2,1)} %get-tuple-element.93), channel_id=1, source_target_pairs={{0,33},{1,97},{2,35},{3,99},{4,37},{5,101},{6,39},{7,103},{8,41},{... | collective-permute-start | bytes 393224 | tf_op jit(solution)/shard_map/every_normed/ppermute | solution.py:773
  85.8 18.4 %collective-permute-start.17 = (bf16[128,512]{1,0:T(8,128)(2,1)}, bf16[128,512]{1,0:T(8,128)(2,1)}, u32[]{:S(2)}, u32[]{:S(2)}) collective-permute-start(bf16[128,512]{1,0:T(8,128)(2,1)} %get-tuple-element.106), channel_id=1, source_target_pairs={{0,1},{1,0},{2,3},{3,2},{4,5},{5,4},{6,7},{7,6},{8,9},{9,8},{10,11... | collective-permute-start | bytes 393224 | tf_op jit(solution)/shard_map/weight_grad/ppermute | solution.py:753
  91.1 18.3 %all-to-all-start.3 = ((bf16[16,64,128]{2,1,0:T(8,128)(2,1)}), bf16[16,64,128]{2,1,0:T(8,128)(2,1)}, u32[]{:S(2)}, u32[]{:S(2)}) async-start(bf16[16,64,128]{2,1,0:T(8,128)(2,1)} %chain.3), calls=%async_computation.3 | async-start | bytes 524288 | tf_op jit(solution)/shard_map/all_to_all | solution.py:747
  98.3 6.0 %collective-permute-start.16 = (bf16[128,1024]{1,0:T(8,128)(2,1)}, bf16[128,1024]{1,0:T(8,128)(2,1)}, u32[]{:S(2)}, u32[]{:S(2)}) collective-permute-start(bf16[128,1024]{1,0:T(8,128)(2,1)} %get-tuple-element.105), channel_id=1, source_target_pairs={{0,1},{1,0},{2,3},{3,2},{4,5},{5,4},{6,7},{7,6},{8,9},{9,8},{10,11... | collective-permute-start | bytes 786440 | tf_op jit(solution)/shard_map/weight_grad/ppermute | solution.py:753
  103.7 3.2 %collective-permute-start.18 = (bf16[16,16,2048]{2,1,0:T(8,128)(2,1)}, bf16[16,16,2048]{2,1,0:T(8,128)(2,1)}, u32[]{:S(2)}, u32[]{:S(2)}) collective-permute-start(bf16[16,16,2048]{2,1,0:T(8,128)(2,1)} %get-tuple-element.109), channel_id=1, source_target_pairs={{0,1},{1,0},{2,3},{3,2},{4,5},{5,4},{6,7},{7,6},{8,9},{9,8},{10,11... | collective-permute-start | bytes 3145736 | tf_op jit(solution)/shard_map/weight_grad/ppermute | solution.py:753
  109.3 25.6 %all-to-all-start.4 = ((bf16[16,16,2048]{2,1,0:T(8,128)(2,1)}), bf16[16,16,2048]{2,1,0:T(8,128)(2,1)}, u32[]{:S(2)}, u32[]{:S(2)}) async-start(bf16[16,16,2048]{2,1,0:T(8,128)(2,1)} %join.1), calls=%async_computation.4 | async-start | bytes 2097152 | tf_op jit(solution)/shard_map/weight_grad/all_to_all | solution.py:747
  128.5 2.9 %collective-permute-start.19 = (bf16[128,2048]{1,0:T(8,128)(2,1)}, bf16[128,2048]{1,0:T(8,128)(2,1)}, u32[]{:S(2)}, u32[]{:S(2)}) collective-permute-start(bf16[128,2048]{1,0:T(8,128)(2,1)} %get-tuple-element.120), channel_id=1, source_target_pairs={{0,1},{1,0},{2,3},{3,2},{4,5},{5,4},{6,7},{7,6},{8,9},{9,8},{10,11... | collective-permute-start | bytes 1572872 | tf_op jit(solution)/shard_map/swap_back/ppermute | solution.py:753
  128.7 2.7 %collective-permute-start.21 = (bf16[128,1024]{1,0:T(8,128)(2,1)}, bf16[128,1024]{1,0:T(8,128)(2,1)}, u32[]{:S(2)}, u32[]{:S(2)}) collective-permute-start(bf16[128,1024]{1,0:T(8,128)(2,1)} %get-tuple-element.124), channel_id=1, source_target_pairs={{0,1},{1,0},{2,3},{3,2},{4,5},{5,4},{6,7},{7,6},{8,9},{9,8},{10,11... | collective-permute-start | bytes 786440 | tf_op jit(solution)/shard_map/swap_back/ppermute | solution.py:753
  129.1 2.3 %collective-permute-start.20 = (bf16[128,512]{1,0:T(8,128)(2,1)}, bf16[128,512]{1,0:T(8,128)(2,1)}, u32[]{:S(2)}, u32[]{:S(2)}) collective-permute-start(bf16[128,512]{1,0:T(8,128)(2,1)} %get-tuple-element.123), channel_id=1, source_target_pairs={{0,1},{1,0},{2,3},{3,2},{4,5},{5,4},{6,7},{7,6},{8,9},{9,8},{10,11... | collective-permute-start | bytes 393224 | tf_op jit(solution)/shard_map/swap_back/ppermute | solution.py:753
